TPU v7x, 32 devices: a whole 2x2x4 slice. The times are simulated.
32 devices in a mesh: dp: 16 (over z, x, core), group: 2 (over y).
Axes of the slice: x: 2, y: 2, z: 4, core: 2. Of those that a mesh axis runs over, the one named last changes fastest.
Arguments:
- tokens: bfloat16 [16384, 7168], P('dp', 'group'), may hold values from -6 to 6
- proj_in: bfloat16 [32, 1024, 2, 7168], P(None, 'dp', None, 'group'), may hold values from -0.0625 to 0.0625
- proj_out: bfloat16 [32, 1024, 7168], P(None, 'dp', 'group'), may hold values from -0.1875 to 0.1875
- expert_list: int32 [16, 2], replicated, may hold values from 0 to 31, as said below
- block_pattern: int32 [16, 2, 8], replicated, may hold values from 0 to 1, as said below
- route_weight: float32 [16384, 2], P('dp'), may hold values from 0.1 to 1
Outputs:
- mixed: bfloat16 [16384, 7168], P('dp', 'group')
Inputs may be any that keep to these rules, and one draw needn't show every extreme that they name: `expert_list`: each row names 2 different experts of the window. `block_pattern`: 1 where the list slot's expert acts on that block of 128 tokens, else 0; the share of ones differs from token group to token group, and in every draw some token group has every block of every slot set.
All inputs are finite; a program needn't handle non-finite values.
Results may differ from a plain program's by a relative error of at most 0.025.
Values may be sent and summed in bfloat16 or wider, within the bound.
No kernel may reach another device: no remote copies, remote signals or barrier semaphores. Data moves between devices by JAX's collectives and lax.ppermute only.
A program may use at most 256 MiB of HBM per device.

v0:
```python
import jax
import jax.numpy as jnp
from jax import lax
from jax.sharding import PartitionSpec as P


def on_device(tokens, proj_in, proj_out, expert_list, block_pattern, route_weight):
    group_size = lax.axis_size("group")
    dp_index = lax.axis_index("dp")
    group_index = lax.axis_index("group")
    row_count = tokens.shape[0]
    slots = expert_list.shape[1]
    block_rows = row_count // block_pattern.shape[2]
    share_rows = row_count // group_size
    width_here = tokens.shape[1]
    requested = expert_list.T.reshape(-1)
    send_in = jnp.take(proj_in, requested, axis=0).reshape(slots, -1, 2, width_here)
    send_out = jnp.take(proj_out, requested, axis=0).reshape(slots, -1, width_here)
    own_pattern = lax.dynamic_index_in_dim(block_pattern, dp_index, 0, keepdims=False)
    block_mask = jnp.repeat(own_pattern, block_rows, axis=1).astype(jnp.float32)
    token_scale = route_weight.T * block_mask
    weight_in = lax.all_to_all(send_in, "dp", split_axis=1, concat_axis=1, tiled=True)
    weight_out = lax.all_to_all(send_out, "dp", split_axis=1, concat_axis=1, tiled=True)
    partial_here = jnp.einsum(
        "td,kfcd->ktcf", tokens, weight_in, preferred_element_type=jnp.float32
    )
    shares = lax.psum_scatter(
        partial_here.astype(jnp.bfloat16), "group", scatter_dimension=1, tiled=True
    ).astype(jnp.float32)
    own_scale = lax.dynamic_slice_in_dim(token_scale, group_index * share_rows, share_rows, 1)
    hidden = (own_scale[:, :, None] * jax.nn.silu(shares[:, :, 0]) * shares[:, :, 1]).astype(
        jnp.bfloat16
    )
    combined = jnp.einsum(
        "ktf,kfd->td",
        lax.all_gather(hidden, "group", axis=1, tiled=True),
        weight_out,
        preferred_element_type=jnp.float32,
    )
    return combined.astype(jnp.bfloat16)


def solution(mesh):
    return jax.shard_map(
        on_device,
        mesh=mesh,
        in_specs=(
            P("dp", "group"),
            P(None, "dp", None, "group"),
            P(None, "dp", "group"),
            P(),
            P(),
            P("dp", None),
        ),
        out_specs=P("dp", "group"),
        check_vma=False,
    )
```

profile of v0, /device:TPU:8, one launch (start us, length us, event | category | flops | bytes accessed | tf_op | source)
XLA Modules:
  0.0 1149.1 jit_solution(15741557608836812871)
XLA Ops:
  6.5 0.7 compare_and_fusion
  7.2 0.1 broadcast_in_dim.29
  7.3 0.1 broadcast_in_dim.30
  7.4 0.8 reshape.51
  8.2 59.3 %gather_fusion = bf16[32,64,2,3584]{3,2,1,0:T(2,128)(2,1)} fusion(bf16[32,64,2,3584]{3,2,1,0:T(2,128)(2,1)} %param.7, s32[1024]{0:T(1024)S(1)} %pad_clamp_fusion), kind=kCustom, calls=%fused_computation | custom fusion | bytes 58720384 | tf_op jit(solution)/shard_map/jit(_take)/gather | solution.py:17
  67.5 20.3 %copy.23 = bf16[32,64,2,3584]{3,1,0,2:T(8,128)(2,1)} copy(bf16[32,64,2,3584]{3,2,1,0:T(2,128)(2,1)} %gather_fusion) | data formatting | bytes 58720256 | tf_op jit(solution)/shard_map/jit(_take)/gather | solution.py:17
  87.8 20.5 %bitcast_select_fusion = bf16[2,1024,2,3584]{3,1,0,2:T(8,128)(2,1)} fusion(pred[2,1024]{1,0:T(4,128)(4,1)S(1)} %broadcast_in_dim.30, bf16[2,1024,2,3584]{3,1,0,2:T(8,128)(2,1)} %bitcast.40), kind=kLoop, calls=%fused_computation.2 | loop fusion | flops 14680064 | bytes 58722304 | tf_op jit(solution)/shard_map/jit(_take)/select_n | solution.py:17
  108.3 53.1 %copy.24 = bf16[2,1024,2,3584]{3,2,0,1:T(2,128)(2,1)} copy(bf16[2,1024,2,3584]{3,1,0,2:T(8,128)(2,1)} %bitcast_select_fusion) | data formatting | bytes 58720256 | tf_op jit(solution)/shard_map/jit(_take)/select_n | solution.py:17
  161.4 6.3 all-to-all-start
  167.7 12.8 %gather_fusion.1 = bf16[32,64,3584]{2,1,0:T(8,128)(2,1)} fusion(bf16[32,64,3584]{2,1,0:T(8,128)(2,1)} %param.8, s32[1024]{0:T(1024)S(1)} %pad_clamp_fusion), kind=kCustom, calls=%fused_computation.1 | custom fusion | bytes 29360256 | tf_op jit(solution)/shard_map/jit(_take)/gather | solution.py:18
  180.5 6.2 bitcast_select_fusion.1
  186.6 80.7 %copy.27 = bf16[2,1024,3584]{2,0,1:T(2,128)(2,1)} copy(bf16[2,1024,3584]{2,1,0:T(8,128)(2,1)S(1)} %bitcast_select_fusion.1) | data formatting | bytes 29360128 | tf_op jit(solution)/shard_map/jit(_take)/select_n | solution.py:18
  267.3 530.5 %all-to-all-done = bf16[2,1024,2,3584]{3,2,0,1:T(2,128)(2,1)} async-done(((bf16[2,1024,2,3584]{3,2,0,1:T(2,128)(2,1)}), bf16[2,1024,2,3584]{3,2,0,1:T(2,128)(2,1)}, u32[]{:S(2)}, u32[]{:S(2)}) %all-to-all-start) | async-done | bytes 29360160 | tf_op jit(solution)/shard_map/all_to_all | solution.py:22
  797.8 6.6 all-to-all-start.1
  804.3 0.0 copy-start
  804.3 0.0 copy-start.1
  804.4 0.2 reduce-scatter.2.cloned.1.call-start
  804.6 39.3 %convert_bitcast_fusion = bf16[2,1024,2,1024]{1,3,2,0:T(8,128)(2,1)} fusion(bf16[1024,3584]{1,0:T(8,128)(2,1)} %param.6, bf16[2,1024,2,3584]{3,2,0,1:T(2,128)(2,1)} %all-to-all-done), kind=kOutput, calls=%fused_computation.9 | convolution fusion | flops 30068965376 | bytes 45088768 | tf_op jit(solution)/shard_map/td,kfcd->ktcf/dot_general | solution.py:24
  843.9 0.0 reduce-scatter.2.cloned.1.call-update
  844.0 0.0 all-gather.2.cloned.1.call-start
  844.0 0.0 copy-done
  844.0 0.2 convert_reduce_fusion
  844.2 0.1 broadcast_bitcast_fusion
  844.3 0.0 copy-done.1
  844.3 100.0 %reduce-scatter.2.cloned.1.call-done = bf16[2,512,2,1024]{1,3,2,0:T(8,128)(2,1)} async-done(((bf16[2,1024,2,1024]{1,3,2,0:T(8,128)(2,1)}), bf16[2,512,2,1024]{1,3,2,0:T(8,128)(2,1)}) %reduce-scatter.2.cloned.1.call-update) | async-done | bytes 4194320 | tf_op jit(solution)/shard_map/reduce_scatter | solution.py:27
  944.3 3.4 convert_element_type.30
  947.6 2.8 fusion.12
  950.4 0.0 all-gather.2.cloned.1.call-update
  950.4 169.4 %all-to-all-done.1 = bf16[2,1024,3584]{2,0,1:T(2,128)(2,1)} async-done(((bf16[2,1024,3584]{2,0,1:T(2,128)(2,1)}), bf16[2,1024,3584]{2,0,1:T(2,128)(2,1)}, u32[]{:S(2)}, u32[]{:S(2)}) %all-to-all-start.1) | async-done | bytes 14680096 | tf_op jit(solution)/shard_map/all_to_all | solution.py:23
  1119.9 0.0 all-gather.2.cloned.1.call-done
  1119.9 22.4 %bitcast_convert_fusion = bf16[1024,3584]{1,0:T(8,128)(2,1)} fusion(bf16[2,1024,1024]{1,2,0:T(8,128)(2,1)} %all-gather.2.cloned.1.call-done, bf16[2,1024,3584]{2,0,1:T(2,128)(2,1)} %all-to-all-done.1), kind=kOutput, calls=%fused_computation.5 | convolution fusion | flops 15036055552 | bytes 26214400 | tf_op jit(solution)/shard_map/ktf,kfd->td/dot_general | solution.py:34
  (4 shorter events, 0.0 us)
Async XLA Ops:
  161.4 636.4 %all-to-all-start = ((bf16[2,1024,2,3584]{3,2,0,1:T(2,128)(2,1)}), bf16[2,1024,2,3584]{3,2,0,1:T(2,128)(2,1)}, u32[]{:S(2)}, u32[]{:S(2)}) async-start(bf16[2,1024,2,3584]{3,2,0,1:T(2,128)(2,1)} %copy.24), calls=%async_computation | async-start | bytes 58720256 | tf_op jit(solution)/shard_map/all_to_all | solution.py:22
  797.8 322.1 %all-to-all-start.1 = ((bf16[2,1024,3584]{2,0,1:T(2,128)(2,1)}), bf16[2,1024,3584]{2,0,1:T(2,128)(2,1)}, u32[]{:S(2)}, u32[]{:S(2)}) async-start(bf16[2,1024,3584]{2,0,1:T(2,128)(2,1)} %copy.27), calls=%async_computation.2 | async-start | bytes 29360128 | tf_op jit(solution)/shard_map/all_to_all | solution.py:23
  804.3 39.7 %copy-start = (s32[16,2,8]{0,2,1:T(8,128)S(1)}, s32[16,2,8]{0,2,1:T(8,128)}, u32[]{:S(2)}) copy-start(s32[16,2,8]{0,2,1:T(8,128)} %param.10) | copy-start | bytes 3076
  804.3 39.9 %copy-start.1 = (f32[1024,2]{0,1:T(2,128)S(1)}, f32[1024,2]{0,1:T(2,128)}, u32[]{:S(2)}) copy-start(f32[1024,2]{0,1:T(2,128)} %param.11) | copy-start | bytes 24580
  804.4 139.9 %reduce-scatter.2.cloned.1.call-start = ((), (), s32[]{:S(2)}) async-start(), calls=%async_computation.3 | async-start | bytes 12582912 | tf_op jit(solution)/shard_map/reduce_scatter | solution.py:27
  844.0 275.9 %all-gather.2.cloned.1.call-start = ((), (), s32[]{:S(2)}) async-start(), calls=%async_computation.4 | async-start | bytes 6291456 | tf_op jit(solution)/shard_map/all_gather | solution.py:36
Sparse Core Ops, SparseCore 0:
  844.1 100.1 reduce-scatter.1
  950.5 56.7 all-gather.1
where the time goes:
time: 1150 us
  waiting for transfers between devices  800 us (70%)
  local copies, waits for them, and re-layouts  227 us (20%)
  matrix products  61.7 us (5%)
  other arithmetic  33.7 us (3%)
  between operations  13.5 us (1%)
  starting transfers between devices  13.1 us (1%)
    all_to_all x1, waiting for transfers between devices, on_device(): lax.all_to_all(send_in, 'dp', split_axis=1, concat_axis=1, tiled=True)  530 us
    all_to_all x1, waiting for transfers between devices, on_device(): lax.all_to_all(send_out, 'dp', split_axis=1, concat_axis=1, tiled=True)  169 us
    reduce_scatter x1, waiting for transfers between devices, on_device(): lax.psum_scatter(partial_here.astype(jnp.bfloat16), 'group', scatter_dime...  100 us
    select_n x1, local copies, waits for them, and re-layouts, on_device(): jnp.take(proj_out, requested, axis=0).reshape(slots, -1, width_here)  80.7 us
    gather x2, local copies, waits for them, and re-layouts, on_device(): jnp.take(proj_in, requested, axis=0).reshape(slots, -1, 2, width_here)  79.6 us
    select_n x1, local copies, waits for them, and re-layouts, on_device(): jnp.take(proj_in, requested, axis=0).reshape(slots, -1, 2, width_here)  53.1 us
    dot_general x1, matrix products, on_device(): jnp.einsum('td,kfcd->ktcf', tokens, weight_in, preferred_element_type=jnp...  39.3 us
  transfers between devices with their start and end apart: 4, of which 3 were waited for; matrix products, arithmetic and copies ran while one was open for 13% of the time, Pallas kernels for 0%

commit v1 on v0

v1 whole, which is shorter than its diff:
```python
import jax
import jax.numpy as jnp
from jax import lax
from jax.sharding import PartitionSpec as P

SLABS = 4
CHUNKS = 4


def on_device(tokens, proj_in, proj_out, expert_list, block_pattern, route_weight):
    dp_size = lax.axis_size("dp")
    group_size = lax.axis_size("group")
    peers = dp_size // SLABS
    dp_index = lax.axis_index("dp")
    slab = dp_index // peers
    column = dp_index % peers
    rows, width = tokens.shape
    slots = expert_list.shape[1]
    blocks = block_pattern.shape[2]
    units = proj_in.shape[1]
    step = rows // CHUNKS

    def over_z(value, hops):
        pairs = [(a * peers + j, b * peers + j) for a, b in hops for j in range(peers)]
        return lax.ppermute(value, "dp", pairs)

    def over_peers(value, offset):
        pairs = [
            (a * peers + j, a * peers + (j + offset) % peers)
            for a in range(SLABS)
            for j in range(peers)
        ]
        return lax.ppermute(value, "dp", pairs)

    swap_half = [(0, 1), (1, 0), (2, 3), (3, 2)]
    middle = [(1, 2), (2, 1)]
    outward = [(1, 0), (2, 3)]
    inward = [(0, 1), (3, 2)]
    low_half = slab < 2
    outer = (slab == 0) | (slab == 3)
    slab_of = [
        jnp.where(low_half, 3, 0),
        jnp.where(low_half, 2, 1),
        slab ^ 1,
        slab,
    ]

    scale_all = lax.all_gather(route_weight.T, "dp", axis=0)
    mask_all = jnp.repeat(block_pattern, rows // blocks, axis=2).astype(jnp.float32)

    def scale_of(turn):
        group = slab_of[turn] * peers + column
        return lax.dynamic_index_in_dim(scale_all, group, 0, keepdims=False) * (
            lax.dynamic_index_in_dim(mask_all, group, 0, keepdims=False)
        )

    def weights_of(turn):
        got_in, got_out = [], []
        for offset in range(peers):
            group = slab_of[turn] * peers + (column + offset) % peers
            chosen = lax.dynamic_index_in_dim(expert_list, group, 0, keepdims=False)
            part_in = jnp.stack(
                [lax.dynamic_index_in_dim(proj_in, chosen[l], 0, keepdims=False) for l in range(slots)]
            )
            part_out = jnp.stack(
                [lax.dynamic_index_in_dim(proj_out, chosen[l], 0, keepdims=False) for l in range(slots)]
            )
            if offset:
                part_in = over_peers(part_in, offset)
                part_out = over_peers(part_out, offset)
            got_in.append(part_in)
            got_out.append(part_out)
        return jnp.concatenate(got_in, axis=1), jnp.concatenate(got_out, axis=1)

    def hidden_of(token_rows, weight_in, scale):
        part = jnp.einsum(
            "td,lfcd->lctf", token_rows, weight_in, preferred_element_type=jnp.float32
        ).astype(jnp.bfloat16)
        total = part.astype(jnp.float32)
        for offset in range(1, group_size):
            pairs = [(i, (i + offset) % group_size) for i in range(group_size)]
            total = total + lax.ppermute(part, "group", pairs).astype(jnp.float32)
        return (scale[:, :, None] * jax.nn.silu(total[:, 0]) * total[:, 1]).astype(jnp.bfloat16)

    def out_of(hidden, weight_out):
        return jnp.einsum("ltf,lfd->td", hidden, weight_out, preferred_element_type=jnp.float32)

    weights = [weights_of(turn) for turn in range(4)]
    scales = [scale_of(turn) for turn in range(4)]
    results = []
    for chunk in range(CHUNKS):
        low = chunk * step
        own = tokens[low : low + step]
        near = over_z(own, swap_half)
        inner = over_z(own, middle)
        far_mid = over_z(near, middle)
        far = jnp.where(outer, over_z(far_mid, outward), far_mid)
        inner = jnp.where(outer, over_z(inner, outward), inner)
        partial = []
        for turn, token_rows in enumerate((far, inner, near, own)):
            hidden = hidden_of(token_rows, weights[turn][0], scales[turn][:, low : low + step])
            partial.append(out_of(hidden, weights[turn][1]))

        def send(value, hops):
            return over_z(value.astype(jnp.bfloat16), hops).astype(jnp.float32)

        to_far = partial[0] + send(partial[0], inward)
        to_inner = partial[1] + send(partial[1], inward)
        to_near = partial[2] + send(to_far, middle)
        own_sum = partial[3] + send(to_inner, middle) + send(to_near, swap_half)
        results.append(own_sum.astype(jnp.bfloat16))
    return jnp.concatenate(results, axis=0)


def solution(mesh):
    return jax.shard_map(
        on_device,
        mesh=mesh,
        in_specs=(
            P("dp", "group"),
            P(None, "dp", None, "group"),
            P(None, "dp", "group"),
            P(),
            P(),
            P("dp", None),
        ),
        out_specs=P("dp", "group"),
        check_vma=False,
    )
```

time: 1150 us -> 1560 us (1.36)
  waiting for transfers between devices: 800 us -> 987 us
  local copies, waits for them, and re-layouts: 227 us -> 73.7 us
  starting transfers between devices: 13.1 us -> 136 us
  blocking collectives: 0 us -> 117 us
  matrix products: 61.7 us -> 111 us
  between operations: 13.5 us -> 61.6 us
  other arithmetic: 33.7 us -> 62.4 us
    ppermute x0 -> x80, waiting for transfers between devices: none -> 987 us  [the longest x40 767 us: over_z(): return lax.ppermute(value, 'dp', pairs)]
    all_to_all x2 -> x0, waiting for transfers between devices: 700 us -> none  [the longest x1 530 us: on_device(): lax.all_to_all(send_in, 'dp', split_axis=1, concat_axis=1, tiled=True)]
    ppermute x0 -> x80, starting transfers between devices: none -> 136 us  [the longest x40 91.8 us: over_z(): return lax.ppermute(value, 'dp', pairs)]
    select_n x2 -> x0, local copies, waits for them, and re-layouts: 134 us -> none  [the longest x1 80.7 us: on_device(): jnp.take(proj_out, requested, axis=0).reshape(slots, -1, width_here)]
    all_gather x0 -> x1, blocking collectives: none -> 117 us  [on_device(): scale_all = lax.all_gather(route_weight.T, 'dp', axis=0)]
    reduce_scatter x1 -> x0, waiting for transfers between devices: 100 us -> none  [on_device(): lax.psum_scatter(partial_here.astype(jnp.bfloat16), 'group', scatter_dime...]
    gather x3 -> x0, local copies, waits for them, and re-layouts: 92.4 us -> none  [the longest x2 79.6 us: on_device(): jnp.take(proj_in, requested, axis=0).reshape(slots, -1, 2, width_here)]
    dot_general x2 -> x32, matrix products: 61.7 us -> 111 us  [the longest x16 57.4 us: out_of(): jnp.einsum('ltf,lfd->td', hidden, weight_out, preferred_element_type=jnp....]
  transfers between devices with their start and end apart: 4 -> 80, of which waited for: 3 -> 45; matrix products, arithmetic and copies ran while one was open for 13% -> 14% of each run, Pallas kernels for 0% -> 0%
where the time goes in v1:
time: 1560 us; the launch traced here: 1550 us
  waiting for transfers between devices  987 us (63%)
  starting transfers between devices  136 us (9%)
  blocking collectives  117 us (8%)
  matrix products  111 us (7%)
  local copies, waits for them, and re-layouts  73.7 us (5%)
  other arithmetic  62.4 us (4%)
  between operations  61.6 us (4%)
    ppermute x40, waiting for transfers between devices, over_z(): return lax.ppermute(value, 'dp', pairs)  767 us
    ppermute x24, waiting for transfers between devices, over_peers(): return lax.ppermute(value, 'dp', pairs)  133 us
    all_gather x1, blocking collectives, on_device(): scale_all = lax.all_gather(route_weight.T, 'dp', axis=0)  117 us
    ppermute x40, starting transfers between devices, over_z(): return lax.ppermute(value, 'dp', pairs)  91.8 us
    ppermute x16, waiting for transfers between devices, hidden_of(): total = total + lax.ppermute(part, 'group', pairs).astype(jnp.float32)  87.3 us
    dot_general x16, matrix products, out_of(): jnp.einsum('ltf,lfd->td', hidden, weight_out, preferred_element_type=jnp....  57.4 us
    dot_general x16, matrix products, hidden_of(): jnp.einsum('td,lfcd->lctf', token_rows, weight_in, preferred_element_type...  53.6 us
    dynamic_slice x2, local copies, waits for them, and re-layouts, weights_of(): lax.dynamic_index_in_dim(proj_in, chosen[l], 0, keepdims=False)  31.2 us
  transfers between devices with their start and end apart: 80, of which 45 were waited for; matrix products, arithmetic and copies ran while one was open for 14% of the time, Pallas kernels for 0%

profile of v1, /device:TPU:8, one launch (start us, length us, event | category | flops | bytes accessed | tf_op | source)
XLA Modules:
  0.0 1548.9 jit_solution(7811511935592608479)
XLA Ops:
  39.1 17.9 %constant_dynamic-slice_fusion.84 = (bf16[1,64,2,3584]{3,2,1,0:T(2,128)(2,1)}, bf16[1,64,2,3584]{3,2,1,0:T(2,128)(2,1)}, bf16[1,64,2,3584]{3,2,1,0:T(2,128)(2,1)...) fusion(bf16[32,64,2,3584]{3,2,1,0:T(2,128)(2,1)} %param.7, ...), kind=kLoop, calls=%fused_computation.368 | loop fusion | bytes 33030216 | tf_op jit(solution)/shard_map/jit(dynamic_index_in_dim)/dynamic_slice | solution.py:63
  85.3 13.3 constant_dynamic-slice_fusion.83
  114.0 117.4 %all-gather.1 = f32[16,2,1024]{2,1,0:T(2,128)S(1)} all-gather(f32[1,2,1024]{2,1,0:T(2,128)S(1)} %bitcast.496), channel_id=2, replica_groups=mesh['dp'=16,'group'=2] {'dp'}, dimensions={0}, use_global_device_ids=true | all-gather | bytes 139264 | tf_op jit(solution)/shard_map/all_gather | solution.py:48
  292.6 22.4 %collective-permute-done.28 = bf16[2,64,2,3584]{3,1,2,0:T(8,128)(2,1)S(1)} collective-permute-done((bf16[2,64,2,3584]{3,1,2,0:T(8,128)(2,1)S(1)}, bf16[2,64,2,3584]{3,1,2,0:T(8,128)(2,1)S(1)}, u32[]{:S(2)}, u32[]{:S(2)}) %collective-permute-start.28) | collective-permute-done | bytes 1835040 | tf_op jit(solution)/shard_map/ppermute | solution.py:33
  326.9 31.2 %collective-permute-done.1 = bf16[2,64,2,3584]{3,1,2,0:T(8,128)(2,1)S(1)} collective-permute-done((bf16[2,64,2,3584]{3,1,2,0:T(8,128)(2,1)S(1)}, bf16[2,64,2,3584]{3,1,2,0:T(8,128)(2,1)S(1)}, u32[]{:S(2)}, u32[]{:S(2)}) %collective-permute-start.1) | collective-permute-done | bytes 1835040 | tf_op jit(solution)/shard_map/ppermute | solution.py:33
  358.1 7.6 collective-permute-start.20
  365.7 28.0 %collective-permute-done.2 = bf16[2,64,2,3584]{3,1,2,0:T(8,128)(2,1)S(1)} collective-permute-done((bf16[2,64,2,3584]{3,1,2,0:T(8,128)(2,1)}, bf16[2,64,2,3584]{3,1,2,0:T(8,128)(2,1)S(1)}, u32[]{:S(2)}, u32[]{:S(2)}) %collective-permute-start.2) | collective-permute-done | bytes 1835040 | tf_op jit(solution)/shard_map/ppermute | solution.py:33
  406.7 30.1 %collective-permute-done.19 = bf16[2,64,2,3584]{3,1,2,0:T(8,128)(2,1)} collective-permute-done((bf16[2,64,2,3584]{3,1,2,0:T(8,128)(2,1)}, bf16[2,64,2,3584]{3,1,2,0:T(8,128)(2,1)}, u32[]{:S(2)}, u32[]{:S(2)}) %collective-permute-start.19) | collective-permute-done | bytes 1835040 | tf_op jit(solution)/shard_map/ppermute | solution.py:33
  439.7 17.7 %collective-permute-done.20 = bf16[2,64,2,3584]{3,1,2,0:T(8,128)(2,1)} collective-permute-done((bf16[2,64,2,3584]{3,1,2,0:T(8,128)(2,1)}, bf16[2,64,2,3584]{3,1,2,0:T(8,128)(2,1)}, u32[]{:S(2)}, u32[]{:S(2)}) %collective-permute-start.20) | collective-permute-done | bytes 1835040 | tf_op jit(solution)/shard_map/ppermute | solution.py:33
  460.7 5.9 pad_maximum_fusion.2
  466.6 6.5 fusion.191
  474.6 6.5 fusion.186
  484.0 16.4 %collective-permute-done.58 = bf16[256,3584]{1,0:T(8,128)(2,1)} collective-permute-done((bf16[256,3584]{1,0:T(8,128)(2,1)}, bf16[256,3584]{1,0:T(8,128)(2,1)}, u32[]{:S(2)}, u32[]{:S(2)}) %collective-permute-start.58) | collective-permute-done | bytes 1835040 | tf_op jit(solution)/shard_map/ppermute | solution.py:25
  502.0 5.7 fusion.181
  507.7 32.1 %collective-permute-done.72 = bf16[256,3584]{1,0:T(8,128)(2,1)} collective-permute-done((bf16[256,3584]{1,0:T(8,128)(2,1)}, bf16[256,3584]{1,0:T(8,128)(2,1)}, u32[]{:S(2)}, u32[]{:S(2)}) %collective-permute-start.72) | collective-permute-done | bytes 1835040 | tf_op jit(solution)/shard_map/ppermute | solution.py:25
  567.2 9.6 collective-permute-done.52
  579.4 8.6 collective-permute-done.59
  593.7 5.5 collective-permute-done.66
  603.6 9.9 collective-permute-done.73
  620.0 9.2 collective-permute-done.67
  642.4 35.6 %collective-permute-done.54 = bf16[256,3584]{1,0:T(8,128)(2,1)} collective-permute-done((bf16[256,3584]{1,0:T(8,128)(2,1)S(1)}, bf16[256,3584]{1,0:T(8,128)(2,1)}, u32[]{:S(2)}, u32[]{:S(2)}) %collective-permute-start.54) | collective-permute-done | bytes 1835040 | tf_op jit(solution)/shard_map/ppermute | solution.py:25
  682.5 33.9 %collective-permute-done.68 = bf16[256,3584]{1,0:T(8,128)(2,1)} collective-permute-done((bf16[256,3584]{1,0:T(8,128)(2,1)S(1)}, bf16[256,3584]{1,0:T(8,128)(2,1)}, u32[]{:S(2)}, u32[]{:S(2)}) %collective-permute-start.68) | collective-permute-done | bytes 1835040 | tf_op jit(solution)/shard_map/ppermute | solution.py:25
  720.1 9.4 collective-permute-done.12
  741.8 8.6 collective-permute-done.41
  754.0 7.6 collective-permute-done.55
  774.5 39.3 %collective-permute-done.60 = bf16[256,3584]{1,0:T(8,128)(2,1)S(1)} collective-permute-done((bf16[256,3584]{1,0:T(8,128)(2,1)}, bf16[256,3584]{1,0:T(8,128)(2,1)S(1)}, u32[]{:S(2)}, u32[]{:S(2)}) %collective-permute-start.60) | collective-permute-done | bytes 1835040 | tf_op jit(solution)/shard_map/ppermute | solution.py:25
  823.2 27.3 %collective-permute-done.74 = bf16[256,3584]{1,0:T(8,128)(2,1)} collective-permute-done((bf16[256,3584]{1,0:T(8,128)(2,1)}, bf16[256,3584]{1,0:T(8,128)(2,1)}, u32[]{:S(2)}, u32[]{:S(2)}) %collective-permute-start.74) | collective-permute-done | bytes 1835040 | tf_op jit(solution)/shard_map/ppermute | solution.py:25
  857.9 37.0 %collective-permute-done.61 = bf16[256,3584]{1,0:T(8,128)(2,1)} collective-permute-done((bf16[256,3584]{1,0:T(8,128)(2,1)S(1)}, bf16[256,3584]{1,0:T(8,128)(2,1)}, u32[]{:S(2)}, u32[]{:S(2)}) %collective-permute-start.61) | collective-permute-done | bytes 1835040 | tf_op jit(solution)/shard_map/ppermute | solution.py:25
  898.5 29.6 %collective-permute-done.75 = bf16[256,3584]{1,0:T(8,128)(2,1)} collective-permute-done((bf16[256,3584]{1,0:T(8,128)(2,1)}, bf16[256,3584]{1,0:T(8,128)(2,1)}, u32[]{:S(2)}, u32[]{:S(2)}) %collective-permute-start.75) | collective-permute-done | bytes 1835040 | tf_op jit(solution)/shard_map/ppermute | solution.py:25
  934.0 9.0 collective-permute-done.48
  944.6 8.1 collective-permute-done.62
  952.9 5.5 collective-permute-done.76
  970.6 32.8 %collective-permute-done.16 = bf16[256,3584]{1,0:T(8,128)(2,1)S(1)} collective-permute-done((bf16[256,3584]{1,0:T(8,128)(2,1)}, bf16[256,3584]{1,0:T(8,128)(2,1)S(1)}, u32[]{:S(2)}, u32[]{:S(2)}) %collective-permute-start.16) | collective-permute-done | bytes 1835040 | tf_op jit(solution)/shard_map/ppermute | solution.py:25
  1005.2 37.5 %collective-permute-done.42 = bf16[256,3584]{1,0:T(8,128)(2,1)S(1)} collective-permute-done((bf16[256,3584]{1,0:T(8,128)(2,1)}, bf16[256,3584]{1,0:T(8,128)(2,1)S(1)}, u32[]{:S(2)}, u32[]{:S(2)}) %collective-permute-start.42) | collective-permute-done | bytes 1835040 | tf_op jit(solution)/shard_map/ppermute | solution.py:25
  1048.9 33.2 %collective-permute-done.56 = bf16[256,3584]{1,0:T(8,128)(2,1)S(1)} collective-permute-done((bf16[256,3584]{1,0:T(8,128)(2,1)}, bf16[256,3584]{1,0:T(8,128)(2,1)S(1)}, u32[]{:S(2)}, u32[]{:S(2)}) %collective-permute-start.56) | collective-permute-done | bytes 1835040 | tf_op jit(solution)/shard_map/ppermute | solution.py:25
  1083.9 37.5 %collective-permute-done.70 = bf16[256,3584]{1,0:T(8,128)(2,1)S(1)} collective-permute-done((bf16[256,3584]{1,0:T(8,128)(2,1)}, bf16[256,3584]{1,0:T(8,128)(2,1)S(1)}, u32[]{:S(2)}, u32[]{:S(2)}) %collective-permute-start.70) | collective-permute-done | bytes 1835040 | tf_op jit(solution)/shard_map/ppermute | solution.py:25
  1128.3 32.4 %collective-permute-done.35 = bf16[256,3584]{1,0:T(8,128)(2,1)S(1)} collective-permute-done((bf16[256,3584]{1,0:T(8,128)(2,1)}, bf16[256,3584]{1,0:T(8,128)(2,1)S(1)}, u32[]{:S(2)}, u32[]{:S(2)}) %collective-permute-start.35) | collective-permute-done | bytes 1835040 | tf_op jit(solution)/shard_map/ppermute | solution.py:25
  1162.7 37.3 %collective-permute-done.49 = bf16[256,3584]{1,0:T(8,128)(2,1)S(1)} collective-permute-done((bf16[256,3584]{1,0:T(8,128)(2,1)}, bf16[256,3584]{1,0:T(8,128)(2,1)S(1)}, u32[]{:S(2)}, u32[]{:S(2)}) %collective-permute-start.49) | collective-permute-done | bytes 1835040 | tf_op jit(solution)/shard_map/ppermute | solution.py:25
  1202.5 36.9 %collective-permute-done.63 = bf16[256,3584]{1,0:T(8,128)(2,1)S(1)} collective-permute-done((bf16[256,3584]{1,0:T(8,128)(2,1)}, bf16[256,3584]{1,0:T(8,128)(2,1)S(1)}, u32[]{:S(2)}, u32[]{:S(2)}) %collective-permute-start.63) | collective-permute-done | bytes 1835040 | tf_op jit(solution)/shard_map/ppermute | solution.py:25
  1246.7 24.1 %collective-permute-done.77 = bf16[256,3584]{1,0:T(8,128)(2,1)S(1)} collective-permute-done((bf16[256,3584]{1,0:T(8,128)(2,1)}, bf16[256,3584]{1,0:T(8,128)(2,1)S(1)}, u32[]{:S(2)}, u32[]{:S(2)}) %collective-permute-start.77) | collective-permute-done | bytes 1835040 | tf_op jit(solution)/shard_map/ppermute | solution.py:25
  1277.4 6.8 collective-permute-done.36
  1293.2 30.4 %collective-permute-done.50 = bf16[256,3584]{1,0:T(8,128)(2,1)} collective-permute-done((bf16[256,3584]{1,0:T(8,128)(2,1)S(1)}, bf16[256,3584]{1,0:T(8,128)(2,1)}, u32[]{:S(2)}, u32[]{:S(2)}) %collective-permute-start.50) | collective-permute-done | bytes 1835040 | tf_op jit(solution)/shard_map/ppermute | solution.py:25
  1327.3 35.7 %collective-permute-done.64 = bf16[256,3584]{1,0:T(8,128)(2,1)} collective-permute-done((bf16[256,3584]{1,0:T(8,128)(2,1)S(1)}, bf16[256,3584]{1,0:T(8,128)(2,1)}, u32[]{:S(2)}, u32[]{:S(2)}) %collective-permute-start.64) | collective-permute-done | bytes 1835040 | tf_op jit(solution)/shard_map/ppermute | solution.py:25
  1366.6 35.6 %collective-permute-done.17 = bf16[256,3584]{1,0:T(8,128)(2,1)S(1)} collective-permute-done((bf16[256,3584]{1,0:T(8,128)(2,1)S(1)}, bf16[256,3584]{1,0:T(8,128)(2,1)S(1)}, u32[]{:S(2)}, u32[]{:S(2)}) %collective-permute-start.17) | collective-permute-done | bytes 1835040 | tf_op jit(solution)/shard_map/ppermute | solution.py:25
  1405.2 36.4 %collective-permute-done.78 = bf16[256,3584]{1,0:T(8,128)(2,1)} collective-permute-done((bf16[256,3584]{1,0:T(8,128)(2,1)S(1)}, bf16[256,3584]{1,0:T(8,128)(2,1)}, u32[]{:S(2)}, u32[]{:S(2)}) %collective-permute-start.78) | collective-permute-done | bytes 1835040 | tf_op jit(solution)/shard_map/ppermute | solution.py:25
  1445.3 35.5 %collective-permute-done.43 = bf16[256,3584]{1,0:T(8,128)(2,1)S(1)} collective-permute-done((bf16[256,3584]{1,0:T(8,128)(2,1)S(1)}, bf16[256,3584]{1,0:T(8,128)(2,1)S(1)}, u32[]{:S(2)}, u32[]{:S(2)}) %collective-permute-start.43) | collective-permute-done | bytes 1835040 | tf_op jit(solution)/shard_map/ppermute | solution.py:25
  1490.8 29.4 %collective-permute-done.57 = bf16[256,3584]{1,0:T(8,128)(2,1)S(1)} collective-permute-done((bf16[256,3584]{1,0:T(8,128)(2,1)S(1)}, bf16[256,3584]{1,0:T(8,128)(2,1)S(1)}, u32[]{:S(2)}, u32[]{:S(2)}) %collective-permute-start.57) | collective-permute-done | bytes 1835040 | tf_op jit(solution)/shard_map/ppermute | solution.py:25
  1521.9 21.4 %collective-permute-done.71 = bf16[256,3584]{1,0:T(8,128)(2,1)S(1)} collective-permute-done((bf16[256,3584]{1,0:T(8,128)(2,1)S(1)}, bf16[256,3584]{1,0:T(8,128)(2,1)S(1)}, u32[]{:S(2)}, u32[]{:S(2)}) %collective-permute-start.71) | collective-permute-done | bytes 1835040 | tf_op jit(solution)/shard_map/ppermute | solution.py:25
  (476 shorter events, 332.1 us)
Async XLA Ops:
  58.6 220.7 %collective-permute-start.9 = (bf16[2,64,2,3584]{3,1,2,0:T(8,128)(2,1)}, bf16[2,64,2,3584]{3,1,2,0:T(8,128)(2,1)}, u32[]{:S(2)}, u32[]{:S(2)}) collective-permute-start(bf16[2,64,2,3584]{3,1,2,0:T(8,128)(2,1)} %pad_maximum_fusion.14), channel_id=1, source_target_pairs={{0,6},{2,0},{4,2},{6,4},{8,14},{10,8},{12,10},{14,12},{16,22},{18,... | collective-permute-start | bytes 5505032 | tf_op jit(solution)/shard_map/ppermute | solution.py:33
  100.3 182.2 %collective-permute-start.7 = (bf16[2,64,2,3584]{3,1,2,0:T(8,128)(2,1)}, bf16[2,64,2,3584]{3,1,2,0:T(8,128)(2,1)}, u32[]{:S(2)}, u32[]{:S(2)}) collective-permute-start(bf16[2,64,2,3584]{3,1,2,0:T(8,128)(2,1)} %pad_maximum_fusion.12), channel_id=1, source_target_pairs={{0,2},{2,4},{4,6},{6,0},{8,10},{10,12},{12,14},{14,8},{16,18},{18,... | collective-permute-start | bytes 5505032 | tf_op jit(solution)/shard_map/ppermute | solution.py:33
  102.1 181.0 %collective-permute-start.8 = (bf16[2,64,2,3584]{3,1,2,0:T(8,128)(2,1)}, bf16[2,64,2,3584]{3,1,2,0:T(8,128)(2,1)}, u32[]{:S(2)}, u32[]{:S(2)}) collective-permute-start(bf16[2,64,2,3584]{3,1,2,0:T(8,128)(2,1)} %pad_maximum_fusion.13), channel_id=1, source_target_pairs={{0,4},{2,6},{4,0},{6,2},{8,12},{10,14},{12,8},{14,10},{16,20},{18,... | collective-permute-start | bytes 5505032 | tf_op jit(solution)/shard_map/ppermute | solution.py:33
  104.7 179.7 %collective-permute-start.26 = (bf16[2,64,2,3584]{3,1,2,0:T(8,128)(2,1)}, bf16[2,64,2,3584]{3,1,2,0:T(8,128)(2,1)}, u32[]{:S(2)}, u32[]{:S(2)}) collective-permute-start(bf16[2,64,2,3584]{3,1,2,0:T(8,128)(2,1)} %pad_maximum_fusion.18), channel_id=1, source_target_pairs={{0,2},{2,4},{4,6},{6,0},{8,10},{10,12},{12,14},{14,8},{16,18},{18,... | collective-permute-start | bytes 5505032 | tf_op jit(solution)/shard_map/ppermute | solution.py:33
  107.0 182.3 %collective-permute-start.27 = (bf16[2,64,2,3584]{3,1,2,0:T(8,128)(2,1)}, bf16[2,64,2,3584]{3,1,2,0:T(8,128)(2,1)}, u32[]{:S(2)}, u32[]{:S(2)}) collective-permute-start(bf16[2,64,2,3584]{3,1,2,0:T(8,128)(2,1)} %pad_maximum_fusion.19), channel_id=1, source_target_pairs={{0,4},{2,6},{4,0},{6,2},{8,12},{10,14},{12,8},{14,10},{16,20},{18,... | collective-permute-start | bytes 5505032 | tf_op jit(solution)/shard_map/ppermute | solution.py:33
  283.0 75.1 %collective-permute-start.1 = (bf16[2,64,2,3584]{3,1,2,0:T(8,128)(2,1)S(1)}, bf16[2,64,2,3584]{3,1,2,0:T(8,128)(2,1)S(1)}, u32[]{:S(2)}, u32[]{:S(2)}) collective-permute-start(bf16[2,64,2,3584]{3,1,2,0:T(8,128)(2,1)S(1)} %pad_maximum_fusion.10), channel_id=1, source_target_pairs={{0,4},{2,6},{4,0},{6,2},{8,12},{10,14},{12,8},{14,10},{16,20},{18,... | collective-permute-start | bytes 5505032 | tf_op jit(solution)/shard_map/ppermute | solution.py:33
  284.4 109.3 %collective-permute-start.2 = (bf16[2,64,2,3584]{3,1,2,0:T(8,128)(2,1)}, bf16[2,64,2,3584]{3,1,2,0:T(8,128)(2,1)S(1)}, u32[]{:S(2)}, u32[]{:S(2)}) collective-permute-start(bf16[2,64,2,3584]{3,1,2,0:T(8,128)(2,1)} %pad_maximum_fusion.11), channel_id=1, source_target_pairs={{0,6},{2,0},{4,2},{6,4},{8,14},{10,8},{12,10},{14,12},{16,22},{18,... | collective-permute-start | bytes 5505032 | tf_op jit(solution)/shard_map/ppermute | solution.py:33
  289.3 177.3 %collective-permute-start.21 = (bf16[256,3584]{1,0:T(8,128)(2,1)}, bf16[256,3584]{1,0:T(8,128)(2,1)}, u32[]{:S(2)}, u32[]{:S(2)}) collective-permute-start(bf16[256,3584]{1,0:T(8,128)(2,1)} %get-tuple-element.69), channel_id=1, source_target_pairs={{0,8},{2,10},{4,12},{6,14},{8,0},{10,2},{12,4},{14,6},{16,24},{18,... | collective-permute-start | bytes 5505032 | tf_op jit(solution)/shard_map/ppermute | solution.py:25
  314.9 89.7 %collective-permute-start.18 = (bf16[2,64,2,3584]{3,1,2,0:T(8,128)(2,1)}, bf16[2,64,2,3584]{3,1,2,0:T(8,128)(2,1)}, u32[]{:S(2)}, u32[]{:S(2)}) collective-permute-start(bf16[2,64,2,3584]{3,1,2,0:T(8,128)(2,1)} %pad_maximum_fusion.15), channel_id=1, source_target_pairs={{0,2},{2,4},{4,6},{6,0},{8,10},{10,12},{12,14},{14,8},{16,18},{18,... | collective-permute-start | bytes 5505032 | tf_op jit(solution)/shard_map/ppermute | solution.py:33
  325.1 111.7 %collective-permute-start.19 = (bf16[2,64,2,3584]{3,1,2,0:T(8,128)(2,1)}, bf16[2,64,2,3584]{3,1,2,0:T(8,128)(2,1)}, u32[]{:S(2)}, u32[]{:S(2)}) collective-permute-start(bf16[2,64,2,3584]{3,1,2,0:T(8,128)(2,1)} %pad_maximum_fusion.16), channel_id=1, source_target_pairs={{0,4},{2,6},{4,0},{6,2},{8,12},{10,14},{12,8},{14,10},{16,20},{18,... | collective-permute-start | bytes 5505032 | tf_op jit(solution)/shard_map/ppermute | solution.py:33
  358.1 99.4 %collective-permute-start.20 = (bf16[2,64,2,3584]{3,1,2,0:T(8,128)(2,1)}, bf16[2,64,2,3584]{3,1,2,0:T(8,128)(2,1)}, u32[]{:S(2)}, u32[]{:S(2)}) collective-permute-start(bf16[2,64,2,3584]{3,1,2,0:T(8,128)(2,1)} %pad_maximum_fusion.17), channel_id=1, source_target_pairs={{0,6},{2,0},{4,2},{6,4},{8,14},{10,8},{12,10},{14,12},{16,22},{18,... | collective-permute-start | bytes 5505032 | tf_op jit(solution)/shard_map/ppermute | solution.py:33
  393.7 79.4 %collective-permute-start.44 = (bf16[256,3584]{1,0:T(8,128)(2,1)}, bf16[256,3584]{1,0:T(8,128)(2,1)}, u32[]{:S(2)}, u32[]{:S(2)}) collective-permute-start(bf16[256,3584]{1,0:T(8,128)(2,1)} %get-tuple-element.70), channel_id=1, source_target_pairs={{0,8},{2,10},{4,12},{6,14},{8,0},{10,2},{12,4},{14,6},{16,24},{18,... | collective-permute-start | bytes 5505032 | tf_op jit(solution)/shard_map/ppermute | solution.py:25
  404.6 140.3 %collective-permute-start.10 = (bf16[256,3584]{1,0:T(8,128)(2,1)}, bf16[256,3584]{1,0:T(8,128)(2,1)}, u32[]{:S(2)}, u32[]{:S(2)}) collective-permute-start(bf16[256,3584]{1,0:T(8,128)(2,1)} %get-tuple-element.69), channel_id=1, source_target_pairs={{8,16},{10,18},{12,20},{14,22},{16,8},{18,10},{20,12},{22,14},{9,1... | collective-permute-start | bytes 5505032 | tf_op jit(solution)/shard_map/ppermute | solution.py:25
  436.8 113.0 %collective-permute-start.39 = (bf16[256,3584]{1,0:T(8,128)(2,1)}, bf16[256,3584]{1,0:T(8,128)(2,1)}, u32[]{:S(2)}, u32[]{:S(2)}) collective-permute-start(bf16[256,3584]{1,0:T(8,128)(2,1)} %get-tuple-element.70), channel_id=1, source_target_pairs={{8,16},{10,18},{12,20},{14,22},{16,8},{18,10},{20,12},{22,14},{9,1... | collective-permute-start | bytes 5505032 | tf_op jit(solution)/shard_map/ppermute | solution.py:25
  473.1 73.8 %collective-permute-start.22 = (bf16[2,2,256,256]{2,3,0,1:T(8,128)(2,1)}, bf16[2,2,256,256]{2,3,0,1:T(8,128)(2,1)}, u32[]{:S(2)}, u32[]{:S(2)}) collective-permute-start(bf16[2,2,256,256]{2,3,0,1:T(8,128)(2,1)} %fusion.191), channel_id=1, source_target_pairs={{0,1},{1,0},{2,3},{3,2},{4,5},{5,4},{6,7},{7,6},{8,9},{9,8},{10,11... | collective-permute-start | bytes 1572872 | tf_op jit(solution)/shard_map/ppermute | solution.py:82
  549.8 79.4 %collective-permute-start.67 = (bf16[256,3584]{1,0:T(8,128)(2,1)}, bf16[256,3584]{1,0:T(8,128)(2,1)S(1)}, u32[]{:S(2)}, u32[]{:S(2)}) collective-permute-start(bf16[256,3584]{1,0:T(8,128)(2,1)} %get-tuple-element.71), channel_id=1, source_target_pairs={{8,16},{10,18},{12,20},{14,22},{16,8},{18,10},{20,12},{22,14},{9,1... | collective-permute-start | bytes 5505032 | tf_op jit(solution)/shard_map/ppermute | solution.py:25
  555.2 75.7 %collective-permute-start.11 = (bf16[256,3584]{1,0:T(8,128)(2,1)}, bf16[256,3584]{1,0:T(8,128)(2,1)S(1)}, u32[]{:S(2)}, u32[]{:S(2)}) collective-permute-start(bf16[256,3584]{1,0:T(8,128)(2,1)} %collective-permute-done.10), channel_id=1, source_target_pairs={{8,0},{10,2},{12,4},{14,6},{16,24},{18,26},{20,28},{22,30},{9,1},{... | collective-permute-start | bytes 5505032 | tf_op jit(solution)/shard_map/ppermute | solution.py:25
  602.9 128.6 %collective-permute-start.15 = (bf16[2,64,3584]{2,1,0:T(8,128)(2,1)S(1)}, bf16[2,64,3584]{2,1,0:T(8,128)(2,1)}, u32[]{:S(2)}, u32[]{:S(2)}) collective-permute-start(bf16[2,64,3584]{2,1,0:T(8,128)(2,1)S(1)} %copy-done.68), channel_id=1, source_target_pairs={{0,6},{2,0},{4,2},{6,4},{8,14},{10,8},{12,10},{14,12},{16,22},{18,... | collective-permute-start | bytes 2752520 | tf_op jit(solution)/shard_map/ppermute | solution.py:33
  629.2 106.2 %collective-permute-start.14 = (bf16[2,64,3584]{2,1,0:T(8,128)(2,1)S(1)}, bf16[2,64,3584]{2,1,0:T(8,128)(2,1)}, u32[]{:S(2)}, u32[]{:S(2)}) collective-permute-start(bf16[2,64,3584]{2,1,0:T(8,128)(2,1)S(1)} %copy-done.67), channel_id=1, source_target_pairs={{0,4},{2,6},{4,0},{6,2},{8,12},{10,14},{12,8},{14,10},{16,20},{18,... | collective-permute-start | bytes 2752520 | tf_op jit(solution)/shard_map/ppermute | solution.py:33
  630.9 85.5 %collective-permute-start.68 = (bf16[256,3584]{1,0:T(8,128)(2,1)S(1)}, bf16[256,3584]{1,0:T(8,128)(2,1)}, u32[]{:S(2)}, u32[]{:S(2)}) collective-permute-start(bf16[256,3584]{1,0:T(8,128)(2,1)S(1)} %collective-permute-done.67), channel_id=1, source_target_pairs={{8,0},{10,2},{12,4},{14,6},{16,24},{18,26},{20,28},{22,30},{9,1},{... | collective-permute-start | bytes 5505032 | tf_op jit(solution)/shard_map/ppermute | solution.py:25
  638.8 98.2 %collective-permute-start.13 = (bf16[2,64,3584]{2,1,0:T(8,128)(2,1)S(1)}, bf16[2,64,3584]{2,1,0:T(8,128)(2,1)}, u32[]{:S(2)}, u32[]{:S(2)}) collective-permute-start(bf16[2,64,3584]{2,1,0:T(8,128)(2,1)S(1)} %copy-done.66), channel_id=1, source_target_pairs={{0,2},{2,4},{4,6},{6,0},{8,10},{10,12},{12,14},{14,8},{16,18},{18,... | collective-permute-start | bytes 2752520 | tf_op jit(solution)/shard_map/ppermute | solution.py:33
  678.0 74.4 %collective-permute-start.29 = (bf16[256,3584]{1,0:T(8,128)(2,1)}, bf16[256,3584]{1,0:T(8,128)(2,1)S(1)}, u32[]{:S(2)}, u32[]{:S(2)}) collective-permute-start(bf16[256,3584]{1,0:T(8,128)(2,1)} %collective-permute-done.21), channel_id=1, source_target_pairs={{8,16},{10,18},{12,20},{14,22},{16,8},{18,10},{20,12},{22,14},{9,1... | collective-permute-start | bytes 5505032 | tf_op jit(solution)/shard_map/ppermute | solution.py:25
  731.5 82.3 %collective-permute-start.60 = (bf16[256,3584]{1,0:T(8,128)(2,1)}, bf16[256,3584]{1,0:T(8,128)(2,1)S(1)}, u32[]{:S(2)}, u32[]{:S(2)}) collective-permute-start(bf16[256,3584]{1,0:T(8,128)(2,1)} %collective-permute-done.58), channel_id=1, source_target_pairs={{8,16},{10,18},{12,20},{14,22},{16,8},{18,10},{20,12},{22,14},{9,1... | collective-permute-start | bytes 5505032 | tf_op jit(solution)/shard_map/ppermute | solution.py:25
  750.4 100.1 %collective-permute-start.74 = (bf16[256,3584]{1,0:T(8,128)(2,1)}, bf16[256,3584]{1,0:T(8,128)(2,1)}, u32[]{:S(2)}, u32[]{:S(2)}) collective-permute-start(bf16[256,3584]{1,0:T(8,128)(2,1)} %collective-permute-done.72), channel_id=1, source_target_pairs={{8,16},{10,18},{12,20},{14,22},{16,8},{18,10},{20,12},{22,14},{9,1... | collective-permute-start | bytes 5505032 | tf_op jit(solution)/shard_map/ppermute | solution.py:25
  761.6 88.9 %collective-permute-start.30 = (bf16[256,3584]{1,0:T(8,128)(2,1)S(1)}, bf16[256,3584]{1,0:T(8,128)(2,1)}, u32[]{:S(2)}, u32[]{:S(2)}) collective-permute-start(bf16[256,3584]{1,0:T(8,128)(2,1)S(1)} %collective-permute-done.29), channel_id=1, source_target_pairs={{8,0},{10,2},{12,4},{14,6},{16,24},{18,26},{20,28},{22,30},{9,1},{... | collective-permute-start | bytes 5505032 | tf_op jit(solution)/shard_map/ppermute | solution.py:25
  774.5 186.3 %collective-permute-start.32 = (bf16[2,64,3584]{2,1,0:T(8,128)(2,1)S(1)}, bf16[2,64,3584]{2,1,0:T(8,128)(2,1)}, u32[]{:S(2)}, u32[]{:S(2)}) collective-permute-start(bf16[2,64,3584]{2,1,0:T(8,128)(2,1)S(1)} %copy-done.65), channel_id=1, source_target_pairs={{0,2},{2,4},{4,6},{6,0},{8,10},{10,12},{12,14},{14,8},{16,18},{18,... | collective-permute-start | bytes 2752520 | tf_op jit(solution)/shard_map/ppermute | solution.py:33
  816.3 78.6 %collective-permute-start.61 = (bf16[256,3584]{1,0:T(8,128)(2,1)S(1)}, bf16[256,3584]{1,0:T(8,128)(2,1)}, u32[]{:S(2)}, u32[]{:S(2)}) collective-permute-start(bf16[256,3584]{1,0:T(8,128)(2,1)S(1)} %collective-permute-done.60), channel_id=1, source_target_pairs={{8,0},{10,2},{12,4},{14,6},{16,24},{18,26},{20,28},{22,30},{9,1},{... | collective-permute-start | bytes 5505032 | tf_op jit(solution)/shard_map/ppermute | solution.py:25
  850.5 110.3 %collective-permute-start.33 = (bf16[2,64,3584]{2,1,0:T(8,128)(2,1)S(1)}, bf16[2,64,3584]{2,1,0:T(8,128)(2,1)}, u32[]{:S(2)}, u32[]{:S(2)}) collective-permute-start(bf16[2,64,3584]{2,1,0:T(8,128)(2,1)S(1)} %copy-done.64), channel_id=1, source_target_pairs={{0,4},{2,6},{4,0},{6,2},{8,12},{10,14},{12,8},{14,10},{16,20},{18,... | collective-permute-start | bytes 2752520 | tf_op jit(solution)/shard_map/ppermute | solution.py:33
  850.5 77.6 %collective-permute-start.75 = (bf16[256,3584]{1,0:T(8,128)(2,1)}, bf16[256,3584]{1,0:T(8,128)(2,1)}, u32[]{:S(2)}, u32[]{:S(2)}) collective-permute-start(bf16[256,3584]{1,0:T(8,128)(2,1)} %collective-permute-done.74), channel_id=1, source_target_pairs={{8,0},{10,2},{12,4},{14,6},{16,24},{18,26},{20,28},{22,30},{9,1},{... | collective-permute-start | bytes 5505032 | tf_op jit(solution)/shard_map/ppermute | solution.py:25
  855.6 105.3 %collective-permute-start.34 = (bf16[2,64,3584]{2,1,0:T(8,128)(2,1)S(1)}, bf16[2,64,3584]{2,1,0:T(8,128)(2,1)}, u32[]{:S(2)}, u32[]{:S(2)}) collective-permute-start(bf16[2,64,3584]{2,1,0:T(8,128)(2,1)S(1)} %copy-done.63), channel_id=1, source_target_pairs={{0,6},{2,0},{4,2},{6,4},{8,14},{10,8},{12,10},{14,12},{16,22},{18,... | collective-permute-start | bytes 2752520 | tf_op jit(solution)/shard_map/ppermute | solution.py:33
  952.8 249.1 %collective-permute-start.23 = (bf16[2,64,3584]{2,1,0:T(8,128)(2,1)}, bf16[2,64,3584]{2,1,0:T(8,128)(2,1)}, u32[]{:S(2)}, u32[]{:S(2)}) collective-permute-start(bf16[2,64,3584]{2,1,0:T(8,128)(2,1)} %pad_maximum_fusion.27), channel_id=1, source_target_pairs={{0,2},{2,4},{4,6},{6,0},{8,10},{10,12},{12,14},{14,8},{16,18},{18,... | collective-permute-start | bytes 2752520 | tf_op jit(solution)/shard_map/ppermute | solution.py:33
  960.8 282.1 %collective-permute-start.24 = (bf16[2,64,3584]{2,1,0:T(8,128)(2,1)}, bf16[2,64,3584]{2,1,0:T(8,128)(2,1)}, u32[]{:S(2)}, u32[]{:S(2)}) collective-permute-start(bf16[2,64,3584]{2,1,0:T(8,128)(2,1)} %pad_maximum_fusion.28), channel_id=1, source_target_pairs={{0,4},{2,6},{4,0},{6,2},{8,12},{10,14},{12,8},{14,10},{16,20},{18,... | collective-permute-start | bytes 2752520 | tf_op jit(solution)/shard_map/ppermute | solution.py:33
  960.8 282.8 %collective-permute-start.25 = (bf16[2,64,3584]{2,1,0:T(8,128)(2,1)}, bf16[2,64,3584]{2,1,0:T(8,128)(2,1)}, u32[]{:S(2)}, u32[]{:S(2)}) collective-permute-start(bf16[2,64,3584]{2,1,0:T(8,128)(2,1)} %pad_maximum_fusion.29), channel_id=1, source_target_pairs={{0,6},{2,0},{4,2},{6,4},{8,14},{10,8},{12,10},{14,12},{16,22},{18,... | collective-permute-start | bytes 2752520 | tf_op jit(solution)/shard_map/ppermute | solution.py:33
  960.9 81.9 %collective-permute-start.42 = (bf16[256,3584]{1,0:T(8,128)(2,1)}, bf16[256,3584]{1,0:T(8,128)(2,1)S(1)}, u32[]{:S(2)}, u32[]{:S(2)}) collective-permute-start(bf16[256,3584]{1,0:T(8,128)(2,1)} %get-tuple-element.151), channel_id=1, source_target_pairs={{0,8},{2,10},{4,12},{6,14},{24,16},{26,18},{28,20},{30,22},{1,9},{... | collective-permute-start | bytes 5505032 | tf_op jit(solution)/shard_map/ppermute | solution.py:25
  1003.4 78.6 %collective-permute-start.56 = (bf16[256,3584]{1,0:T(8,128)(2,1)}, bf16[256,3584]{1,0:T(8,128)(2,1)S(1)}, u32[]{:S(2)}, u32[]{:S(2)}) collective-permute-start(bf16[256,3584]{1,0:T(8,128)(2,1)} %get-tuple-element.147), channel_id=1, source_target_pairs={{0,8},{2,10},{4,12},{6,14},{24,16},{26,18},{28,20},{30,22},{1,9},{... | collective-permute-start | bytes 5505032 | tf_op jit(solution)/shard_map/ppermute | solution.py:25
  1042.7 78.6 %collective-permute-start.70 = (bf16[256,3584]{1,0:T(8,128)(2,1)}, bf16[256,3584]{1,0:T(8,128)(2,1)S(1)}, u32[]{:S(2)}, u32[]{:S(2)}) collective-permute-start(bf16[256,3584]{1,0:T(8,128)(2,1)} %get-tuple-element.143), channel_id=1, source_target_pairs={{0,8},{2,10},{4,12},{6,14},{24,16},{26,18},{28,20},{30,22},{1,9},{... | collective-permute-start | bytes 5505032 | tf_op jit(solution)/shard_map/ppermute | solution.py:25
  1082.1 78.6 %collective-permute-start.35 = (bf16[256,3584]{1,0:T(8,128)(2,1)}, bf16[256,3584]{1,0:T(8,128)(2,1)S(1)}, u32[]{:S(2)}, u32[]{:S(2)}) collective-permute-start(bf16[256,3584]{1,0:T(8,128)(2,1)} %get-tuple-element.153), channel_id=1, source_target_pairs={{0,8},{2,10},{4,12},{6,14},{24,16},{26,18},{28,20},{30,22},{1,9},{... | collective-permute-start | bytes 5505032 | tf_op jit(solution)/shard_map/ppermute | solution.py:25
  1121.4 78.6 %collective-permute-start.49 = (bf16[256,3584]{1,0:T(8,128)(2,1)}, bf16[256,3584]{1,0:T(8,128)(2,1)S(1)}, u32[]{:S(2)}, u32[]{:S(2)}) collective-permute-start(bf16[256,3584]{1,0:T(8,128)(2,1)} %get-tuple-element.149), channel_id=1, source_target_pairs={{0,8},{2,10},{4,12},{6,14},{24,16},{26,18},{28,20},{30,22},{1,9},{... | collective-permute-start | bytes 5505032 | tf_op jit(solution)/shard_map/ppermute | solution.py:25
  1160.7 78.6 %collective-permute-start.63 = (bf16[256,3584]{1,0:T(8,128)(2,1)}, bf16[256,3584]{1,0:T(8,128)(2,1)S(1)}, u32[]{:S(2)}, u32[]{:S(2)}) collective-permute-start(bf16[256,3584]{1,0:T(8,128)(2,1)} %get-tuple-element.145), channel_id=1, source_target_pairs={{0,8},{2,10},{4,12},{6,14},{24,16},{26,18},{28,20},{30,22},{1,9},{... | collective-permute-start | bytes 5505032 | tf_op jit(solution)/shard_map/ppermute | solution.py:25
  1243.9 79.8 %collective-permute-start.50 = (bf16[256,3584]{1,0:T(8,128)(2,1)S(1)}, bf16[256,3584]{1,0:T(8,128)(2,1)}, u32[]{:S(2)}, u32[]{:S(2)}) collective-permute-start(bf16[256,3584]{1,0:T(8,128)(2,1)S(1)} %add_convert_fusion.4), channel_id=1, source_target_pairs={{8,16},{10,18},{12,20},{14,22},{16,8},{18,10},{20,12},{22,14},{9,1... | collective-permute-start | bytes 5505032 | tf_op jit(solution)/shard_map/ppermute | solution.py:25
  1270.8 92.2 %collective-permute-start.64 = (bf16[256,3584]{1,0:T(8,128)(2,1)S(1)}, bf16[256,3584]{1,0:T(8,128)(2,1)}, u32[]{:S(2)}, u32[]{:S(2)}) collective-permute-start(bf16[256,3584]{1,0:T(8,128)(2,1)S(1)} %add_convert_fusion.2), channel_id=1, source_target_pairs={{8,16},{10,18},{12,20},{14,22},{16,8},{18,10},{20,12},{22,14},{9,1... | collective-permute-start | bytes 5505032 | tf_op jit(solution)/shard_map/ppermute | solution.py:25
  1275.0 127.2 %collective-permute-start.17 = (bf16[256,3584]{1,0:T(8,128)(2,1)S(1)}, bf16[256,3584]{1,0:T(8,128)(2,1)S(1)}, u32[]{:S(2)}, u32[]{:S(2)}) collective-permute-start(bf16[256,3584]{1,0:T(8,128)(2,1)S(1)} %add_convert_fusion.7), channel_id=1, source_target_pairs={{8,16},{10,18},{12,20},{14,22},{16,8},{18,10},{20,12},{22,14},{9,1... | collective-permute-start | bytes 5505032 | tf_op jit(solution)/shard_map/ppermute | solution.py:25
  1284.2 157.4 %collective-permute-start.78 = (bf16[256,3584]{1,0:T(8,128)(2,1)S(1)}, bf16[256,3584]{1,0:T(8,128)(2,1)}, u32[]{:S(2)}, u32[]{:S(2)}) collective-permute-start(bf16[256,3584]{1,0:T(8,128)(2,1)S(1)} %add_convert_fusion), channel_id=1, source_target_pairs={{8,16},{10,18},{12,20},{14,22},{16,8},{18,10},{20,12},{22,14},{9,1... | collective-permute-start | bytes 5505032 | tf_op jit(solution)/shard_map/ppermute | solution.py:25
  1290.4 190.4 %collective-permute-start.43 = (bf16[256,3584]{1,0:T(8,128)(2,1)S(1)}, bf16[256,3584]{1,0:T(8,128)(2,1)S(1)}, u32[]{:S(2)}, u32[]{:S(2)}) collective-permute-start(bf16[256,3584]{1,0:T(8,128)(2,1)S(1)} %add_convert_fusion.5), channel_id=1, source_target_pairs={{8,16},{10,18},{12,20},{14,22},{16,8},{18,10},{20,12},{22,14},{9,1... | collective-permute-start | bytes 5505032 | tf_op jit(solution)/shard_map/ppermute | solution.py:25
  1323.6 160.5 %collective-permute-start.37 = (bf16[256,3584]{1,0:T(8,128)(2,1)S(1)}, bf16[256,3584]{1,0:T(8,128)(2,1)S(1)}, u32[]{:S(2)}, u32[]{:S(2)}) collective-permute-start(bf16[256,3584]{1,0:T(8,128)(2,1)S(1)} %fusion.21), channel_id=1, source_target_pairs={{0,8},{2,10},{4,12},{6,14},{8,0},{10,2},{12,4},{14,6},{16,24},{18,... | collective-permute-start | bytes 5505032 | tf_op jit(solution)/shard_map/ppermute | solution.py:25
  1362.9 124.4 %collective-permute-start.51 = (bf16[256,3584]{1,0:T(8,128)(2,1)S(1)}, bf16[256,3584]{1,0:T(8,128)(2,1)}, u32[]{:S(2)}, u32[]{:S(2)}) collective-permute-start(bf16[256,3584]{1,0:T(8,128)(2,1)S(1)} %fusion.20), channel_id=1, source_target_pairs={{0,8},{2,10},{4,12},{6,14},{8,0},{10,2},{12,4},{14,6},{16,24},{18,... | collective-permute-start | bytes 5505032 | tf_op jit(solution)/shard_map/ppermute | solution.py:25
  1402.2 118.0 %collective-permute-start.57 = (bf16[256,3584]{1,0:T(8,128)(2,1)S(1)}, bf16[256,3584]{1,0:T(8,128)(2,1)S(1)}, u32[]{:S(2)}, u32[]{:S(2)}) collective-permute-start(bf16[256,3584]{1,0:T(8,128)(2,1)S(1)} %add_convert_fusion.3), channel_id=1, source_target_pairs={{8,16},{10,18},{12,20},{14,22},{16,8},{18,10},{20,12},{22,14},{9,1... | collective-permute-start | bytes 5505032 | tf_op jit(solution)/shard_map/ppermute | solution.py:25
  1441.6 78.5 %collective-permute-start.65 = (bf16[256,3584]{1,0:T(8,128)(2,1)S(1)}, bf16[256,3584]{1,0:T(8,128)(2,1)S(1)}, u32[]{:S(2)}, u32[]{:S(2)}) collective-permute-start(bf16[256,3584]{1,0:T(8,128)(2,1)S(1)} %fusion.19), channel_id=1, source_target_pairs={{0,8},{2,10},{4,12},{6,14},{8,0},{10,2},{12,4},{14,6},{16,24},{18,... | collective-permute-start | bytes 5505032 | tf_op jit(solution)/shard_map/ppermute | solution.py:25
  (142 other events, 3245.0 us)

commit v2 on v0

v2 whole, which is shorter than its diff:
```python
import jax
import jax.numpy as jnp
from jax import lax
from jax.experimental import pallas as pl
from jax.experimental.pallas import tpu as pltpu
from jax.sharding import PartitionSpec as P

SLABS = 4


def gather_kernel(chosen, source, *rest):
    count = chosen.shape[0]
    paired = len(source.shape) == 4
    if paired:
        outs, held, flat, sems = rest[:-3], rest[-3], rest[-2], rest[-1]
    else:
        outs, held, sems = rest[:-2], rest[-2], rest[-1]
        flat = held
    slots = count // len(outs)
    units = flat.shape[1]
    moves = []
    for n in range(count):
        k, l = divmod(n, slots)
        moves.append(
            (
                pltpu.make_async_copy(source.at[chosen[n]], held.at[n], sems.at[0, n]),
                pltpu.make_async_copy(
                    flat.at[n], outs[k].at[pl.ds(l * units, units)], sems.at[1, n]
                ),
            )
        )
    for into, _ in moves:
        into.start()
    for n, (into, out) in enumerate(moves):
        into.wait()
        if paired:

            @pl.loop(0, units // 16)
            def _(block):
                pairs = held[n, pl.ds(block * 8, 8)]
                flat[n, pl.ds(pl.multiple_of(block * 16, 16), 16)] = pairs.reshape(16, flat.shape[2])

        out.start()
    for _, out in moves:
        out.wait()


def gather_experts(chosen, source, parts):
    count = chosen.shape[0]
    width = source.shape[-1]
    units = source.size // (source.shape[0] * width)
    scratch = [pltpu.VMEM((count,) + source.shape[1:], source.dtype)]
    if source.ndim == 4:
        scratch.append(pltpu.VMEM((count, units, width), source.dtype))
    return pl.pallas_call(
        gather_kernel,
        out_shape=[jax.ShapeDtypeStruct((count // parts * units, width), source.dtype)] * parts,
        grid_spec=pltpu.PrefetchScalarGridSpec(
            num_scalar_prefetch=1,
            grid=(),
            in_specs=[pl.BlockSpec(memory_space=pl.ANY)],
            out_specs=[pl.BlockSpec(memory_space=pl.ANY)] * parts,
            scratch_shapes=scratch + [pltpu.SemaphoreType.DMA((2, count))],
        ),
        compiler_params=pltpu.CompilerParams(vmem_limit_bytes=40 << 20),
    )(chosen, source)


def hold_kernel(*refs):
    del refs


def hold_until(values, landed):
    count = len(values)
    anywhere = pl.BlockSpec(memory_space=pl.ANY)
    return pl.pallas_call(
        hold_kernel,
        out_shape=[jax.ShapeDtypeStruct(v.shape, v.dtype) for v in values],
        in_specs=[anywhere] * (count + len(landed)),
        out_specs=[anywhere] * count,
        input_output_aliases={n: n for n in range(count)},
        compiler_params=pltpu.CompilerParams(vmem_limit_bytes=1 << 20),
    )(*values, *landed)


def on_device(tokens, proj_in, proj_out, expert_list, block_pattern, route_weight):
    dp_size = lax.axis_size("dp")
    group_size = lax.axis_size("group")
    peers = dp_size // SLABS
    dp_index = lax.axis_index("dp")
    slab = dp_index // peers
    column = dp_index % peers
    rows, width = tokens.shape
    slots = expert_list.shape[1]
    units = proj_in.shape[1]
    block_rows = rows // block_pattern.shape[2]

    def over_z(value, hops, offset=0):
        pairs = [(a * peers + j, b * peers + (j ^ offset)) for a, b in hops for j in range(peers)]
        return lax.ppermute(value, "dp", pairs)

    rightward = [(0, 1), (1, 2), (2, 3)]
    leftward = [(3, 2), (2, 1), (1, 0)]
    middle = [(1, 2), (2, 1)]
    low_half = slab < 2
    outer = (slab == 0) | (slab == 3)
    far, mid, near, own = 0, 1, 2, 3
    slab_of = [jnp.where(low_half, 3, 0), jnp.where(low_half, 2, 1), slab ^ 1, slab]

    def gather(source, slabs):
        chosen = jnp.concatenate(
            [
                lax.dynamic_index_in_dim(expert_list, s * peers + (column ^ o), 0, keepdims=False)
                for o in range(peers)
                for s in slabs
            ]
        )
        return gather_experts(chosen, source, peers)

    def over_peers(parts, name):
        same = [(a, a) for a in range(SLABS)]
        with jax.named_scope("hop_" + name):
            return [parts[0]] + [over_z(parts[o], same, o) for o in range(1, peers)]

    def joined(parts, place, places):
        size = parts[0].shape[0] // places
        return jnp.concatenate([part[place * size : (place + 1) * size] for part in parts], axis=0)

    def held(parts, landed):
        return [parts[0]] + list(hold_until(parts[1:], landed))

    first = gather(proj_in, [slab_of[far], slab_of[near]])
    with jax.named_scope("hop_right1"):
        right1 = over_z(tokens, rightward)
    with jax.named_scope("hop_left1"):
        left1 = over_z(tokens, leftward)
    first = over_peers(first, "in_far_near")
    far_in, near_in = joined(first, 0, 2), joined(first, 1, 2)

    with jax.named_scope("hop_right2"):
        right2 = over_z(right1, [(1, 2), (2, 3)])
    with jax.named_scope("hop_left2"):
        left2 = over_z(left1, [(2, 1), (1, 0)])
    with jax.named_scope("hop_edge"):
        edge_in = over_z(far_in, [(0, 1), (3, 2)])
    second = over_peers(
        held(gather(proj_out, [slab ^ 2, slab ^ 3]), first[1:] + [right1, left1]), "out23"
    )
    out2, out3 = joined(second, 0, 2), joined(second, 1, 2)

    def terms_of(token_rows, weight_in):
        return lax.dot_general(
            weight_in, token_rows, (((1,), (1,)), ((), ())), preferred_element_type=jnp.float32
        ).astype(jnp.bfloat16)

    def hidden_of(name, part):
        total = part.astype(jnp.float32)
        for offset in range(1, group_size):
            pairs = [(g, (g + offset) % group_size) for g in range(group_size)]
            with jax.named_scope("terms_" + name):
                total = total + lax.ppermute(part, "group", pairs).astype(jnp.float32)
        total = total.reshape(-1, 2, rows)
        return (jax.nn.silu(total[:, 0]) * total[:, 1]).astype(jnp.bfloat16)

    toward1 = jnp.where(low_half, left1, right1)
    away1 = jnp.where(low_half, right1, left1)
    near_hidden = hidden_of("near", terms_of(jnp.where(outer, toward1, away1), near_in))
    with jax.named_scope("hop_hidden1"):
        hidden1 = over_z(near_hidden, [(a, a ^ 1) for a in range(SLABS)])

    out2, out3 = hold_until([out2, out3], [right2, left2, hidden1])
    with jax.named_scope("hop_out2"):
        out2 = over_z(out2, [(a, a ^ 2) for a in range(SLABS)])
    with jax.named_scope("hop_out3"):
        out3 = over_z(out3, [(a, a ^ 3) for a in range(SLABS)])
    third = over_peers(
        held(gather(proj_in, [slab_of[mid]]), second[1:] + [right2, left2, hidden1]), "in_mid"
    )
    mid_in = joined(third, 0, 1)

    toward2 = jnp.where(low_half, left2, right2)
    far_hidden = hidden_of("far", terms_of(toward2, far_in))
    edge_hidden = hidden_of("edge", terms_of(toward2, edge_in))
    mid_hidden = hidden_of("mid", terms_of(jnp.where(outer, toward2, toward1), mid_in))

    fourth = over_peers(held(gather(proj_out, [slab, slab ^ 1]), third[1:]), "out01")
    out0, out1 = joined(fourth, 0, 2), joined(fourth, 1, 2)
    with jax.named_scope("hop_out1"):
        out1 = over_z(out1, [(a, a ^ 1) for a in range(SLABS)])
    fifth = over_peers(held(gather(proj_in, [slab]), fourth[1:]), "in_own")
    own_hidden = hidden_of("own", terms_of(tokens, joined(fifth, 0, 1)))

    cross_hidden = jnp.where(outer, mid_hidden, far_hidden)
    cross_hidden, edge_hidden, mid_hidden = hold_until(
        [cross_hidden, edge_hidden, mid_hidden], [out2, out3]
    )
    with jax.named_scope("hop_hidden2"):
        hidden2 = over_z(cross_hidden, [(a, a ^ 2) for a in range(SLABS)])
    with jax.named_scope("hop_hidden3"):
        hidden3 = jnp.where(
            outer, over_z(edge_hidden, [(1, 3), (2, 0)]), over_z(mid_hidden, middle)
        )

    own_pattern = lax.dynamic_index_in_dim(block_pattern, dp_index, 0, keepdims=False)
    scale = route_weight.T * jnp.repeat(own_pattern, block_rows, axis=1).astype(jnp.float32)

    def weighted(hidden):
        split = hidden.astype(jnp.float32).reshape(peers, slots, units, rows)
        return (split * scale[None, :, None, :]).astype(jnp.bfloat16).reshape(-1, rows)

    total = 0.0
    for hidden, weight_out in ((own_hidden, out0), (hidden1, out1), (hidden2, out2), (hidden3, out3)):
        total = total + lax.dot_general(
            weighted(hidden),
            weight_out,
            (((0,), (0,)), ((), ())),
            preferred_element_type=jnp.float32,
        )
    return total.astype(jnp.bfloat16)


def solution(mesh):
    return jax.shard_map(
        on_device,
        mesh=mesh,
        in_specs=(
            P("dp", "group"),
            P(None, "dp", None, "group"),
            P(None, "dp", "group"),
            P(),
            P(),
            P("dp", None),
        ),
        out_specs=P("dp", "group"),
        check_vma=False,
    )
```

time: 1150 us -> 870 us (0.76)
  waiting for transfers between devices: 800 us -> 504 us
  local copies, waits for them, and re-layouts: 227 us -> 113 us
  matrix products: 61.7 us -> 119 us
  starting transfers between devices: 13.1 us -> 47.9 us
  Pallas kernels: 0 us -> 32.2 us
  other arithmetic: 33.7 us -> 49.1 us
  between operations: 13.5 us -> 1.02 us
    all_to_all x2 -> x0, waiting for transfers between devices: 700 us -> none  [the longest x1 530 us: on_device(): lax.all_to_all(send_in, 'dp', split_axis=1, concat_axis=1, tiled=True)]
    ppermute x0 -> x32, waiting for transfers between devices: none -> 504 us  [the longest x27 469 us: over_z(): return lax.ppermute(value, 'dp', pairs)]
    select_n x2 -> x0, local copies, waits for them, and re-layouts: 134 us -> none  [the longest x1 80.7 us: on_device(): jnp.take(proj_out, requested, axis=0).reshape(slots, -1, width_here)]
    reduce_scatter x1 -> x0, waiting for transfers between devices: 100 us -> none  [on_device(): lax.psum_scatter(partial_here.astype(jnp.bfloat16), 'group', scatter_dime...]
    gather x3 -> x0, local copies, waits for them, and re-layouts: 92.4 us -> none  [the longest x2 79.6 us: on_device(): jnp.take(proj_in, requested, axis=0).reshape(slots, -1, 2, width_here)]
    slice x0 -> x17, local copies, waits for them, and re-layouts: none -> 63.5 us  [the longest x5 33.7 us: hidden_of(): return (jax.nn.silu(total[:, 0]) * total[:, 1]).astype(jnp.bfloat16)]
    dot_general x2 -> x9, matrix products: 61.7 us -> 119 us  [the longest x5 72.5 us: terms_of(): lax.dot_general(weight_in, token_rows, (((1,), (1,)), ((), ())), preferre...]
    ppermute x0 -> x32, starting transfers between devices: none -> 47.9 us  [the longest x27 41.4 us: over_z(): return lax.ppermute(value, 'dp', pairs)]
  transfers between devices with their start and end apart: 4 -> 32, of which waited for: 3 -> 15; matrix products, arithmetic and copies ran while one was open for 13% -> 27% of each run, Pallas kernels for 0% -> 3%
where the time goes in v2:
time: 870 us; the launch traced here: 865 us
  waiting for transfers between devices  504 us (58%)
  matrix products  119 us (14%)
  local copies, waits for them, and re-layouts  113 us (13%)
  other arithmetic  49.1 us (6%)
  starting transfers between devices  47.9 us (6%)
  Pallas kernels  32.2 us (4%)
    ppermute x27, waiting for transfers between devices, over_z(): return lax.ppermute(value, 'dp', pairs)  469 us
    dot_general x5, matrix products, terms_of(): lax.dot_general(weight_in, token_rows, (((1,), (1,)), ((), ())), preferre...  72.5 us
    dot_general x4, matrix products, on_device(): lax.dot_general(weighted(hidden), weight_out, (((0,), (0,)), ((), ())), p...  46.1 us
    ppermute x27, starting transfers between devices, over_z(): return lax.ppermute(value, 'dp', pairs)  41.4 us
    ppermute x5, waiting for transfers between devices, hidden_of(): total = total + lax.ppermute(part, 'group', pairs).astype(jnp.float32)  34.6 us
    slice x5, local copies, waits for them, and re-layouts, hidden_of(): return (jax.nn.silu(total[:, 0]) * total[:, 1]).astype(jnp.bfloat16)  33.7 us
    pallas_call x5, Pallas kernels, gather_experts(): pl.pallas_call(gather_kernel, out_shape=[jax.ShapeDtypeStruct((count // p...  32.2 us
    slice x12, local copies, waits for them, and re-layouts, joined(): part[place * size:(place + 1) * size]  29.9 us
  transfers between devices with their start and end apart: 32, of which 15 were waited for; matrix products, arithmetic and copies ran while one was open for 27% of the time, Pallas kernels for 3%

profile of v2, /device:TPU:8, one launch (start us, length us, event | category | flops | bytes accessed | tf_op | source)
XLA Modules:
  0.0 865.1 jit_solution(13013831000965174529)
XLA Ops:
  3.2 10.2 %shard_map.68 = (bf16[512,3584]{1,0:T(8,128)(2,1)S(1)}, bf16[512,3584]{1,0:T(8,128)(2,1)}, bf16[512,3584]{1,0:T(8,128)(2,1)}, bf16[512,3584]{1,0:T(8,128)(2,1)}) custom-call(s32[16]{0:T(128)S(1)} %concatenate.43.chosen, bf16[32,64,2,3584]{3,2,1,0:T(2,128)(2,1)} %source.9), custom_call_target="tpu_custom_call" | custom-call | tf_op jit(solution)/shard_map/pallas_call | solution.py:55
  18.4 5.5 collective-permute-start.4
  25.4 5.3 shard_map.65
  33.1 5.9 shard_map.67
  40.5 6.1 shard_map.66
  47.8 4.8 shard_map.64
  61.4 4.2 fusion.101
  65.6 41.0 %collective-permute-done.1.refs_4_ = bf16[512,3584]{1,0:T(8,128)(2,1)} collective-permute-done((bf16[512,3584]{1,0:T(8,128)(2,1)}, bf16[512,3584]{1,0:T(8,128)(2,1)}, u32[]{:S(2)}, u32[]{:S(2)}) %collective-permute-start.1) | collective-permute-done | bytes 3670048 | tf_op jit(solution)/shard_map/hop_in_far_near/ppermute | solution.py:100
  110.1 73.0 %collective-permute-done.2.refs_5_ = bf16[512,3584]{1,0:T(8,128)(2,1)} collective-permute-done((bf16[512,3584]{1,0:T(8,128)(2,1)}, bf16[512,3584]{1,0:T(8,128)(2,1)}, u32[]{:S(2)}, u32[]{:S(2)}) %collective-permute-start.2) | collective-permute-done | bytes 3670048 | tf_op jit(solution)/shard_map/hop_in_far_near/ppermute | solution.py:100
  195.1 4.2 collective-permute-start.8
  199.3 6.8 collective-permute-start.9
  206.1 16.4 %fusion.60 = bf16[1024,1024]{1,0:T(8,128)(2,1)} fusion(bf16[1024,3584]{1,0:T(8,128)(2,1)} %collective-permute-done.3.refs_6_, bf16[1024,3584]{1,0:T(8,128)(2,1)} %collective-permute-done.4.refs_7_, pred[]{:T(512)S(6)} %lt.101, pred[]{:T(512)S(6)} %or.3, bf16[256,3584]{1,0:T(8,128)(2,1)} %get-tuple-element.121, bf16[256,3584]{1,0:T(8,128)(2,1)} %get-tuple-element.119, ...), kind=kOutput, calls=%fused_computation.80 | convolution fusion | flops 7557611520 | bytes 24117250 | tf_op jit(solution)/shard_map/dot_general | solution.py:152
  226.0 10.1 %collective-permute-done.6.refs_4_ = bf16[256,3584]{1,0:T(8,128)(2,1)} collective-permute-done((bf16[256,3584]{1,0:T(8,128)(2,1)}, bf16[256,3584]{1,0:T(8,128)(2,1)}, u32[]{:S(2)}, u32[]{:S(2)}) %collective-permute-start.6) | collective-permute-done | bytes 1835040 | tf_op jit(solution)/shard_map/hop_out23/ppermute | solution.py:100
  238.9 30.8 %collective-permute-done.10 = bf16[1024,1024]{1,0:T(8,128)(2,1)S(1)} collective-permute-done((bf16[1024,1024]{1,0:T(8,128)(2,1)}, bf16[1024,1024]{1,0:T(8,128)(2,1)S(1)}, u32[]{:S(2)}, u32[]{:S(2)}) %collective-permute-start.10) | collective-permute-done | bytes 2097184 | tf_op jit(solution)/shard_map/terms_near/ppermute | solution.py:161
  272.6 6.0 reshape.35
  278.7 7.2 fusion.98
  292.4 93.3 %collective-permute-done.11.refs_8_.refs_4_ = bf16[512,1024]{1,0:T(8,128)(2,1)S(1)} collective-permute-done((bf16[512,1024]{1,0:T(8,128)(2,1)S(1)}, bf16[512,1024]{1,0:T(8,128)(2,1)S(1)}, u32[]{:S(2)}, u32[]{:S(2)}) %collective-permute-start.11) | collective-permute-done | bytes 1048608 | tf_op jit(solution)/shard_map/hop_hidden1/ppermute | solution.py:100
  387.5 6.9 broadcast_select_fusion
  394.4 13.3 %convolution_convert_fusion = bf16[1024,1024]{1,0:T(8,128)(2,1)} fusion(bf16[1024,3584]{1,0:T(8,128)(2,1)} %collective-permute-done.25, bf16[1024,3584]{1,0:T(8,128)(2,1)} %broadcast_select_fusion), kind=kOutput, calls=%fused_computation.81 | convolution fusion | flops 7517241344 | bytes 16777216 | tf_op jit(solution)/shard_map/dot_general | solution.py:152
  409.2 15.3 %convolution_convert_fusion.1 = bf16[1024,1024]{1,0:T(8,128)(2,1)} fusion(bf16[1024,3584]{1,0:T(8,128)(2,1)} %broadcast_select_fusion, bf16[256,3584]{1,0:T(8,128)(2,1)} %copy-done.24, bf16[256,3584]{1,0:T(8,128)(2,1)} %copy-done.23, bf16[256,3584]{1,0:T(8,128)(2,1)} %copy-done.22, bf16[256,3584]{1,0:T(8,128)(2,1)} %copy-done.21), kind=kOutput, calls=%fused_computation.82 | convolution fusion | flops 7546601472 | bytes 16777216 | tf_op jit(solution)/shard_map/dot_general | solution.py:152
  425.0 3.9 collective-permute-done.13.refs_4_
  428.9 38.4 %collective-permute-done.14.refs_5_ = bf16[256,3584]{1,0:T(8,128)(2,1)} collective-permute-done((bf16[256,3584]{1,0:T(8,128)(2,1)}, bf16[256,3584]{1,0:T(8,128)(2,1)}, u32[]{:S(2)}, u32[]{:S(2)}) %collective-permute-start.14) | collective-permute-done | bytes 1835040 | tf_op jit(solution)/shard_map/hop_in_mid/ppermute | solution.py:100
  472.7 12.9 %fusion.52 = bf16[1024,1024]{1,0:T(8,128)(2,1)} fusion(bf16[1024,3584]{1,0:T(8,128)(2,1)} %broadcast_select_fusion, bf16[1024,3584]{1,0:T(8,128)(2,1)} %collective-permute-done.4.refs_7_, bf16[1024,3584]{1,0:T(8,128)(2,1)} %collective-permute-done.3.refs_6_, pred[]{:T(512)S(6)} %lt.101, pred[]{:T(512)S(6)} %or.3, ...), kind=kOutput, calls=%fused_computation.78 | convolution fusion | flops 7553941504 | bytes 31457282 | tf_op jit(solution)/shard_map/dot_general | solution.py:152
  486.1 5.1 convert_add_fusion
  491.3 5.8 reshape.39
  502.4 5.1 convert_add_fusion.1
  507.5 6.1 reshape.38
  513.6 7.1 fusion.96
  523.2 5.2 fusion.99
  528.4 24.1 %collective-permute-done.17.refs_5_ = bf16[256,3584]{1,0:T(8,128)(2,1)} collective-permute-done((bf16[256,3584]{1,0:T(8,128)(2,1)}, bf16[256,3584]{1,0:T(8,128)(2,1)}, u32[]{:S(2)}, u32[]{:S(2)}) %collective-permute-start.17) | collective-permute-done | bytes 1835040 | tf_op jit(solution)/shard_map/hop_out01/ppermute | solution.py:100
  562.8 33.4 %collective-permute-done.19 = bf16[256,3584]{1,0:T(8,128)(2,1)S(1)} collective-permute-done((bf16[256,3584]{1,0:T(8,128)(2,1)S(1)}, bf16[256,3584]{1,0:T(8,128)(2,1)S(1)}, u32[]{:S(2)}, u32[]{:S(2)}) %collective-permute-start.19) | collective-permute-done | bytes 1835040 | tf_op jit(solution)/shard_map/hop_in_own/ppermute | solution.py:100
  598.8 35.0 %collective-permute-done.20 = bf16[256,3584]{1,0:T(8,128)(2,1)S(1)} collective-permute-done((bf16[256,3584]{1,0:T(8,128)(2,1)S(1)}, bf16[256,3584]{1,0:T(8,128)(2,1)S(1)}, u32[]{:S(2)}, u32[]{:S(2)}) %collective-permute-start.20) | collective-permute-done | bytes 1835040 | tf_op jit(solution)/shard_map/hop_in_own/ppermute | solution.py:100
  635.0 14.7 %fusion.57 = bf16[1024,1024]{1,0:T(8,128)(2,1)} fusion(bf16[1024,3584]{1,0:T(8,128)(2,1)} %param.6, bf16[256,3584]{1,0:T(8,128)(2,1)} %copy-done.43, bf16[256,3584]{1,0:T(8,128)(2,1)} %copy-done.42, bf16[256,3584]{1,0:T(8,128)(2,1)} %copy-done.41, bf16[256,3584]{1,0:T(8,128)(2,1)S(1)} %copy-done.16), kind=kOutput, calls=%fused_computation.79 | convolution fusion | flops 7546601472 | bytes 16777216 | tf_op jit(solution)/shard_map/dot_general | solution.py:152
  651.2 5.1 convert_add_fusion.2
  656.4 5.8 reshape.37
  662.2 7.2 fusion.97
  672.5 51.2 %collective-permute-done.28.refs_4_ = bf16[512,3584]{1,0:T(8,128)(2,1)} collective-permute-done((bf16[512,3584]{1,0:T(8,128)(2,1)}, bf16[512,3584]{1,0:T(8,128)(2,1)}, u32[]{:S(2)}, u32[]{:S(2)}) %collective-permute-start.28) | collective-permute-done | bytes 3670048 | tf_op jit(solution)/shard_map/hop_out3/ppermute | solution.py:100
  723.8 5.8 collective-permute-start.30
  732.0 4.5 convert_add_fusion.3
  736.5 5.8 reshape.36
  742.3 7.1 fusion.95
  749.4 20.4 %collective-permute-done.29 = bf16[512,1024]{1,0:T(8,128)(2,1)} collective-permute-done((bf16[512,1024]{1,0:T(8,128)(2,1)S(1)}, bf16[512,1024]{1,0:T(8,128)(2,1)}, u32[]{:S(2)}, u32[]{:S(2)}) %collective-permute-start.29) | collective-permute-done | bytes 1048608 | tf_op jit(solution)/shard_map/hop_hidden2/ppermute | solution.py:100
  769.8 22.5 %collective-permute-done.30 = bf16[512,1024]{1,0:T(8,128)(2,1)} collective-permute-done((bf16[512,1024]{1,0:T(8,128)(2,1)S(1)}, bf16[512,1024]{1,0:T(8,128)(2,1)}, u32[]{:S(2)}, u32[]{:S(2)}) %collective-permute-start.30) | collective-permute-done | bytes 1048608 | tf_op jit(solution)/shard_map/hop_hidden3/ppermute | solution.py:100
  792.2 22.8 %collective-permute-done.31 = bf16[512,1024]{1,0:T(8,128)(2,1)} collective-permute-done((bf16[512,1024]{1,0:T(8,128)(2,1)}, bf16[512,1024]{1,0:T(8,128)(2,1)}, u32[]{:S(2)}, u32[]{:S(2)}) %collective-permute-start.31) | collective-permute-done | bytes 1048608 | tf_op jit(solution)/shard_map/hop_hidden3/ppermute | solution.py:100
  818.5 9.5 %fusion.113 = f32[1024,3584]{1,0:T(8,128)} fusion(bf16[512,1024]{1,0:T(8,128)(2,1)S(1)} %get-tuple-element.141, bf16[512,3584]{1,0:T(8,128)(2,1)} %collective-permute-done.27.refs_3_), kind=kOutput, calls=%fused_computation.159 | convolution fusion | flops 3758096384 | bytes 19398656 | tf_op jit(solution)/shard_map/dot_general | solution.py:213
  828.0 7.3 fusion.30
  835.4 9.6 %fusion.112 = f32[1024,3584]{1,0:T(8,128)} fusion(bf16[512,1024]{1,0:T(8,128)(2,1)S(1)} %get-tuple-element.139, bf16[512,3584]{1,0:T(8,128)(2,1)} %collective-permute-done.22), kind=kOutput, calls=%fused_computation.158 | convolution fusion | flops 3758096384 | bytes 19398656 | tf_op jit(solution)/shard_map/dot_general | solution.py:213
  845.0 19.6 %add_convert_fusion = bf16[1024,3584]{1,0:T(8,128)(2,1)} fusion(f32[1024,3584]{1,0:T(8,128)} %fusion.113, f32[1024,3584]{1,0:T(8,128)} %fusion.30, f32[1024,3584]{1,0:T(8,128)} %fusion.112, bf16[512,1024]{1,0:T(8,128)(2,1)S(1)} %get-tuple-element.140, bf16[512,3584]{1,0:T(8,128)(2,1)} %collective-permute-done.28.refs_4_), kind=kOutput, calls=%fused_computation | convolution fusion | flops 3772776448 | bytes 56098816 | tf_op jit(solution)/shard_map/dot_general | solution.py:213
  (168 shorter events, 97.0 us)
Async XLA Ops:
  15.2 46.2 %collective-permute-start = (bf16[512,3584]{1,0:T(8,128)(2,1)}, bf16[512,3584]{1,0:T(8,128)(2,1)}, u32[]{:S(2)}, u32[]{:S(2)}) collective-permute-start(bf16[512,3584]{1,0:T(8,128)(2,1)} %get-tuple-element.55), channel_id=1, source_target_pairs={{0,2},{2,0},{4,6},{6,4},{8,10},{10,8},{12,14},{14,12},{16,18},{18,... | collective-permute-start | bytes 11010056 | tf_op jit(solution)/shard_map/hop_in_far_near/ppermute | solution.py:100
  15.2 176.5 %collective-permute-start.3 = (bf16[1024,3584]{1,0:T(8,128)(2,1)}, bf16[1024,3584]{1,0:T(8,128)(2,1)}, u32[]{:S(2)}, u32[]{:S(2)}) collective-permute-start(bf16[1024,3584]{1,0:T(8,128)(2,1)} %param.6), channel_id=1, source_target_pairs={{0,8},{2,10},{4,12},{6,14},{8,16},{10,18},{12,20},{14,22},{16,24},... | collective-permute-start | bytes 22020104 | tf_op jit(solution)/shard_map/hop_right1/ppermute | solution.py:100
  18.4 173.3 %collective-permute-start.4 = (bf16[1024,3584]{1,0:T(8,128)(2,1)}, bf16[1024,3584]{1,0:T(8,128)(2,1)}, u32[]{:S(2)}, u32[]{:S(2)}) collective-permute-start(bf16[1024,3584]{1,0:T(8,128)(2,1)} %param.6), channel_id=1, source_target_pairs={{24,16},{26,18},{28,20},{30,22},{16,8},{18,10},{20,12},{22,14},{8,... | collective-permute-start | bytes 22020104 | tf_op jit(solution)/shard_map/hop_left1/ppermute | solution.py:100
  24.0 82.6 %collective-permute-start.1 = (bf16[512,3584]{1,0:T(8,128)(2,1)}, bf16[512,3584]{1,0:T(8,128)(2,1)}, u32[]{:S(2)}, u32[]{:S(2)}) collective-permute-start(bf16[512,3584]{1,0:T(8,128)(2,1)} %get-tuple-element.56), channel_id=1, source_target_pairs={{0,4},{2,6},{4,0},{6,2},{8,12},{10,14},{12,8},{14,10},{16,20},{18,... | collective-permute-start | bytes 11010056 | tf_op jit(solution)/shard_map/hop_in_far_near/ppermute | solution.py:100
  25.2 157.9 %collective-permute-start.2 = (bf16[512,3584]{1,0:T(8,128)(2,1)}, bf16[512,3584]{1,0:T(8,128)(2,1)}, u32[]{:S(2)}, u32[]{:S(2)}) collective-permute-start(bf16[512,3584]{1,0:T(8,128)(2,1)} %get-tuple-element.57), channel_id=1, source_target_pairs={{0,6},{2,4},{4,2},{6,0},{8,14},{10,12},{12,10},{14,8},{16,22},{18,... | collective-permute-start | bytes 11010056 | tf_op jit(solution)/shard_map/hop_in_far_near/ppermute | solution.py:100
  47.8 9.8 %copy-start.40 = (s32[16,2,8]{0,2,1:T(8,128)S(1)}, s32[16,2,8]{0,2,1:T(8,128)}, u32[]{:S(2)}) copy-start(s32[16,2,8]{0,2,1:T(8,128)} %param.10) | copy-start | bytes 3076
  61.4 125.3 %copy-start.21 = (bf16[256,3584]{1,0:T(8,128)(2,1)}, bf16[256,3584]{1,0:T(8,128)(2,1)S(1)}, u32[]{:S(2)}) copy-start(bf16[256,3584]{1,0:T(8,128)(2,1)S(1)} %get-tuple-element.116) | copy-start | bytes 5505028
  65.6 121.1 %copy-start.22 = (bf16[256,3584]{1,0:T(8,128)(2,1)}, bf16[256,3584]{1,0:T(8,128)(2,1)S(1)}, u32[]{:S(2)}) copy-start(bf16[256,3584]{1,0:T(8,128)(2,1)S(1)} %get-tuple-element.118) | copy-start | bytes 5505028
  110.1 76.6 %copy-start.23 = (bf16[256,3584]{1,0:T(8,128)(2,1)}, bf16[256,3584]{1,0:T(8,128)(2,1)S(1)}, u32[]{:S(2)}) copy-start(bf16[256,3584]{1,0:T(8,128)(2,1)S(1)} %get-tuple-element.120) | copy-start | bytes 5505028
  190.4 204.0 %collective-permute-start.25 = (bf16[1024,3584]{1,0:T(8,128)(2,1)}, bf16[1024,3584]{1,0:T(8,128)(2,1)}, u32[]{:S(2)}, u32[]{:S(2)}) collective-permute-start(bf16[1024,3584]{1,0:T(8,128)(2,1)} %pad_maximum_fusion), channel_id=1, source_target_pairs={{0,8},{2,10},{4,12},{6,14},{24,16},{26,18},{28,20},{30,22},{1,9},{... | collective-permute-start | bytes 22020104 | tf_op jit(solution)/shard_map/hop_edge/ppermute | solution.py:100
  193.0 29.5 %collective-permute-start.5 = (bf16[256,3584]{1,0:T(8,128)(2,1)}, bf16[256,3584]{1,0:T(8,128)(2,1)S(1)}, u32[]{:S(2)}, u32[]{:S(2)}) collective-permute-start(bf16[256,3584]{1,0:T(8,128)(2,1)} %copy-done.14), channel_id=1, source_target_pairs={{0,2},{2,0},{4,6},{6,4},{8,10},{10,8},{12,14},{14,12},{16,18},{18,... | collective-permute-start | bytes 5505032 | tf_op jit(solution)/shard_map/hop_out23/ppermute | solution.py:100
  193.8 42.2 %collective-permute-start.6 = (bf16[256,3584]{1,0:T(8,128)(2,1)}, bf16[256,3584]{1,0:T(8,128)(2,1)}, u32[]{:S(2)}, u32[]{:S(2)}) collective-permute-start(bf16[256,3584]{1,0:T(8,128)(2,1)} %get-tuple-element.59), channel_id=1, source_target_pairs={{0,4},{2,6},{4,0},{6,2},{8,12},{10,14},{12,8},{14,10},{16,20},{18,... | collective-permute-start | bytes 5505032 | tf_op jit(solution)/shard_map/hop_out23/ppermute | solution.py:100
  195.1 190.6 %collective-permute-start.8 = (bf16[1024,3584]{1,0:T(8,128)(2,1)}, bf16[1024,3584]{1,0:T(8,128)(2,1)}, u32[]{:S(2)}, u32[]{:S(2)}) collective-permute-start(bf16[1024,3584]{1,0:T(8,128)(2,1)} %collective-permute-done.3.refs_6_), channel_id=1, source_target_pairs={{8,16},{10,18},{12,20},{14,22},{16,24},{18,26},{20,28},{22,30},{9,... | collective-permute-start | bytes 22020104 | tf_op jit(solution)/shard_map/hop_right2/ppermute | solution.py:100
  199.3 186.4 %collective-permute-start.9 = (bf16[1024,3584]{1,0:T(8,128)(2,1)}, bf16[1024,3584]{1,0:T(8,128)(2,1)}, u32[]{:S(2)}, u32[]{:S(2)}) collective-permute-start(bf16[1024,3584]{1,0:T(8,128)(2,1)} %collective-permute-done.4.refs_7_), channel_id=1, source_target_pairs={{16,8},{18,10},{20,12},{22,14},{8,0},{10,2},{12,4},{14,6},{17,9},{... | collective-permute-start | bytes 22020104 | tf_op jit(solution)/shard_map/hop_left2/ppermute | solution.py:100
  206.1 18.0 %copy-start.39 = (f32[1024,2]{0,1:T(2,128)S(1)}, f32[1024,2]{0,1:T(2,128)}, u32[]{:S(2)}) copy-start(f32[1024,2]{0,1:T(2,128)} %param.11) | copy-start | bytes 24580
  222.5 47.2 %collective-permute-start.10 = (bf16[1024,1024]{1,0:T(8,128)(2,1)}, bf16[1024,1024]{1,0:T(8,128)(2,1)S(1)}, u32[]{:S(2)}, u32[]{:S(2)}) collective-permute-start(bf16[1024,1024]{1,0:T(8,128)(2,1)} %fusion.60), channel_id=1, source_target_pairs={{0,1},{1,0},{2,3},{3,2},{4,5},{5,4},{6,7},{7,6},{8,9},{9,8},{10,11... | collective-permute-start | bytes 6291464 | tf_op jit(solution)/shard_map/terms_near/ppermute | solution.py:161
  224.6 45.1 %copy-start.37 = (bf16[1024,1024]{1,0:T(8,128)(2,1)S(1)}, bf16[1024,1024]{1,0:T(8,128)(2,1)}, u32[]{:S(2)}) copy-start(bf16[1024,1024]{1,0:T(8,128)(2,1)} %fusion.60) | copy-start | bytes 6291460
  236.1 51.0 %collective-permute-start.7 = (bf16[256,3584]{1,0:T(8,128)(2,1)}, bf16[256,3584]{1,0:T(8,128)(2,1)}, u32[]{:S(2)}, u32[]{:S(2)}) collective-permute-start(bf16[256,3584]{1,0:T(8,128)(2,1)} %get-tuple-element.60), channel_id=1, source_target_pairs={{0,6},{2,4},{4,2},{6,0},{8,14},{10,12},{12,10},{14,8},{16,22},{18,... | collective-permute-start | bytes 5505032 | tf_op jit(solution)/shard_map/hop_out23/ppermute | solution.py:100
  287.0 98.7 %collective-permute-start.11 = (bf16[512,1024]{1,0:T(8,128)(2,1)S(1)}, bf16[512,1024]{1,0:T(8,128)(2,1)S(1)}, u32[]{:S(2)}, u32[]{:S(2)}) collective-permute-start(bf16[512,1024]{1,0:T(8,128)(2,1)S(1)} %fusion.51), channel_id=1, source_target_pairs={{0,8},{2,10},{4,12},{6,14},{8,0},{10,2},{12,4},{14,6},{16,24},{18,... | collective-permute-start | bytes 3145736 | tf_op jit(solution)/shard_map/hop_hidden1/ppermute | solution.py:100
  385.7 38.8 %collective-permute-start.12 = (bf16[256,3584]{1,0:T(8,128)(2,1)}, bf16[256,3584]{1,0:T(8,128)(2,1)}, u32[]{:S(2)}, u32[]{:S(2)}) collective-permute-start(bf16[256,3584]{1,0:T(8,128)(2,1)} %get-tuple-element.62), channel_id=1, source_target_pairs={{0,2},{2,0},{4,6},{6,4},{8,10},{10,8},{12,14},{14,12},{16,18},{18,... | collective-permute-start | bytes 5505032 | tf_op jit(solution)/shard_map/hop_in_mid/ppermute | solution.py:100
  385.7 43.2 %collective-permute-start.13 = (bf16[256,3584]{1,0:T(8,128)(2,1)}, bf16[256,3584]{1,0:T(8,128)(2,1)}, u32[]{:S(2)}, u32[]{:S(2)}) collective-permute-start(bf16[256,3584]{1,0:T(8,128)(2,1)} %get-tuple-element.63), channel_id=1, source_target_pairs={{0,4},{2,6},{4,0},{6,2},{8,12},{10,14},{12,8},{14,10},{16,20},{18,... | collective-permute-start | bytes 5505032 | tf_op jit(solution)/shard_map/hop_in_mid/ppermute | solution.py:100
  386.5 80.7 %collective-permute-start.14 = (bf16[256,3584]{1,0:T(8,128)(2,1)}, bf16[256,3584]{1,0:T(8,128)(2,1)}, u32[]{:S(2)}, u32[]{:S(2)}) collective-permute-start(bf16[256,3584]{1,0:T(8,128)(2,1)} %get-tuple-element.64), channel_id=1, source_target_pairs={{0,6},{2,4},{4,2},{6,0},{8,14},{10,12},{12,10},{14,8},{16,22},{18,... | collective-permute-start | bytes 5505032 | tf_op jit(solution)/shard_map/hop_in_mid/ppermute | solution.py:100
  387.5 285.0 %collective-permute-start.27 = (bf16[512,3584]{1,0:T(8,128)(2,1)}, bf16[512,3584]{1,0:T(8,128)(2,1)}, u32[]{:S(2)}, u32[]{:S(2)}) collective-permute-start(bf16[512,3584]{1,0:T(8,128)(2,1)} %get-tuple-element.74), channel_id=1, source_target_pairs={{0,16},{2,18},{4,20},{6,22},{8,24},{10,26},{12,28},{14,30},{16,0},... | collective-permute-start | bytes 11010056 | tf_op jit(solution)/shard_map/hop_out2/ppermute | solution.py:100
  407.7 59.6 %copy-start.9 = (bf16[256,3584]{1,0:T(8,128)(2,1)S(1)}, bf16[256,3584]{1,0:T(8,128)(2,1)}, u32[]{:S(2)}) copy-start(bf16[256,3584]{1,0:T(8,128)(2,1)} %copy-done.8) | copy-start | bytes 5505028
  407.7 77.9 %collective-permute-start.26 = (bf16[1024,1024]{1,0:T(8,128)(2,1)}, bf16[1024,1024]{1,0:T(8,128)(2,1)}, u32[]{:S(2)}, u32[]{:S(2)}) collective-permute-start(bf16[1024,1024]{1,0:T(8,128)(2,1)} %convolution_convert_fusion), channel_id=1, source_target_pairs={{0,1},{1,0},{2,3},{3,2},{4,5},{5,4},{6,7},{7,6},{8,9},{9,8},{10,11... | collective-permute-start | bytes 6291464 | tf_op jit(solution)/shard_map/terms_edge/ppermute | solution.py:161
  424.5 76.4 %collective-permute-start.24 = (bf16[1024,1024]{1,0:T(8,128)(2,1)}, bf16[1024,1024]{1,0:T(8,128)(2,1)}, u32[]{:S(2)}, u32[]{:S(2)}) collective-permute-start(bf16[1024,1024]{1,0:T(8,128)(2,1)} %convolution_convert_fusion.1), channel_id=1, source_target_pairs={{0,1},{1,0},{2,3},{3,2},{4,5},{5,4},{6,7},{7,6},{8,9},{9,8},{10,11... | collective-permute-start | bytes 6291464 | tf_op jit(solution)/shard_map/terms_far/ppermute | solution.py:161
  471.3 57.1 %collective-permute-start.15 = (bf16[256,3584]{1,0:T(8,128)(2,1)}, bf16[256,3584]{1,0:T(8,128)(2,1)S(1)}, u32[]{:S(2)}, u32[]{:S(2)}) collective-permute-start(bf16[256,3584]{1,0:T(8,128)(2,1)} %copy-done.10), channel_id=1, source_target_pairs={{0,2},{2,0},{4,6},{6,4},{8,10},{10,8},{12,14},{14,12},{16,18},{18,... | collective-permute-start | bytes 5505032 | tf_op jit(solution)/shard_map/hop_out01/ppermute | solution.py:100
  471.9 56.5 %collective-permute-start.16 = (bf16[256,3584]{1,0:T(8,128)(2,1)}, bf16[256,3584]{1,0:T(8,128)(2,1)}, u32[]{:S(2)}, u32[]{:S(2)}) collective-permute-start(bf16[256,3584]{1,0:T(8,128)(2,1)} %get-tuple-element.66), channel_id=1, source_target_pairs={{0,4},{2,6},{4,0},{6,2},{8,12},{10,14},{12,8},{14,10},{16,20},{18,... | collective-permute-start | bytes 5505032 | tf_op jit(solution)/shard_map/hop_out01/ppermute | solution.py:100
  485.6 66.9 %collective-permute-start.17 = (bf16[256,3584]{1,0:T(8,128)(2,1)}, bf16[256,3584]{1,0:T(8,128)(2,1)}, u32[]{:S(2)}, u32[]{:S(2)}) collective-permute-start(bf16[256,3584]{1,0:T(8,128)(2,1)} %copy-done.13), channel_id=1, source_target_pairs={{0,6},{2,4},{4,2},{6,0},{8,14},{10,12},{12,10},{14,8},{16,22},{18,... | collective-permute-start | bytes 5505032 | tf_op jit(solution)/shard_map/hop_out01/ppermute | solution.py:100
  500.8 150.4 %collective-permute-start.23 = (bf16[1024,1024]{1,0:T(8,128)(2,1)}, bf16[1024,1024]{1,0:T(8,128)(2,1)}, u32[]{:S(2)}, u32[]{:S(2)}) collective-permute-start(bf16[1024,1024]{1,0:T(8,128)(2,1)} %fusion.52), channel_id=1, source_target_pairs={{0,1},{1,0},{2,3},{3,2},{4,5},{5,4},{6,7},{7,6},{8,9},{9,8},{10,11... | collective-permute-start | bytes 6291464 | tf_op jit(solution)/shard_map/terms_mid/ppermute | solution.py:161
  523.2 29.3 %copy-start.3 = (bf16[256,3584]{1,0:T(8,128)(2,1)S(1)}, bf16[256,3584]{1,0:T(8,128)(2,1)}, u32[]{:S(2)}) copy-start(bf16[256,3584]{1,0:T(8,128)(2,1)} %copy-done.2) | copy-start | bytes 5505028
  523.2 29.3 %copy-start.5 = (bf16[256,3584]{1,0:T(8,128)(2,1)S(1)}, bf16[256,3584]{1,0:T(8,128)(2,1)}, u32[]{:S(2)}) copy-start(bf16[256,3584]{1,0:T(8,128)(2,1)} %copy-done.4) | copy-start | bytes 5505028
  523.2 29.3 %copy-start.7 = (bf16[256,3584]{1,0:T(8,128)(2,1)S(1)}, bf16[256,3584]{1,0:T(8,128)(2,1)}, u32[]{:S(2)}) copy-start(bf16[256,3584]{1,0:T(8,128)(2,1)} %copy-done.6) | copy-start | bytes 5505028
  552.5 10.3 %collective-permute-start.18 = (bf16[256,3584]{1,0:T(8,128)(2,1)S(1)}, bf16[256,3584]{1,0:T(8,128)(2,1)S(1)}, u32[]{:S(2)}, u32[]{:S(2)}) collective-permute-start(bf16[256,3584]{1,0:T(8,128)(2,1)S(1)} %get-tuple-element.68), channel_id=1, source_target_pairs={{0,2},{2,0},{4,6},{6,4},{8,10},{10,8},{12,14},{14,12},{16,18},{18,... | collective-permute-start | bytes 5505032 | tf_op jit(solution)/shard_map/hop_in_own/ppermute | solution.py:100
  553.3 42.9 %collective-permute-start.19 = (bf16[256,3584]{1,0:T(8,128)(2,1)S(1)}, bf16[256,3584]{1,0:T(8,128)(2,1)S(1)}, u32[]{:S(2)}, u32[]{:S(2)}) collective-permute-start(bf16[256,3584]{1,0:T(8,128)(2,1)S(1)} %get-tuple-element.69), channel_id=1, source_target_pairs={{0,4},{2,6},{4,0},{6,2},{8,12},{10,14},{12,8},{14,10},{16,20},{18,... | collective-permute-start | bytes 5505032 | tf_op jit(solution)/shard_map/hop_in_own/ppermute | solution.py:100
  554.1 79.6 %collective-permute-start.20 = (bf16[256,3584]{1,0:T(8,128)(2,1)S(1)}, bf16[256,3584]{1,0:T(8,128)(2,1)S(1)}, u32[]{:S(2)}, u32[]{:S(2)}) collective-permute-start(bf16[256,3584]{1,0:T(8,128)(2,1)S(1)} %get-tuple-element.70), channel_id=1, source_target_pairs={{0,6},{2,4},{4,2},{6,0},{8,14},{10,12},{12,10},{14,8},{16,22},{18,... | collective-permute-start | bytes 5505032 | tf_op jit(solution)/shard_map/hop_in_own/ppermute | solution.py:100
  560.9 74.1 %copy-start.16 = (bf16[256,3584]{1,0:T(8,128)(2,1)S(1)}, bf16[256,3584]{1,0:T(8,128)(2,1)}, u32[]{:S(2)}) copy-start(bf16[256,3584]{1,0:T(8,128)(2,1)} %copy-done.15) | copy-start | bytes 5505028
  562.8 70.9 %copy-start.41 = (bf16[256,3584]{1,0:T(8,128)(2,1)}, bf16[256,3584]{1,0:T(8,128)(2,1)S(1)}, u32[]{:S(2)}) copy-start(bf16[256,3584]{1,0:T(8,128)(2,1)S(1)} %collective-permute-done.18) | copy-start | bytes 5505028
  562.8 160.9 %collective-permute-start.28 = (bf16[512,3584]{1,0:T(8,128)(2,1)}, bf16[512,3584]{1,0:T(8,128)(2,1)}, u32[]{:S(2)}, u32[]{:S(2)}) collective-permute-start(bf16[512,3584]{1,0:T(8,128)(2,1)} %get-tuple-element.75), channel_id=1, source_target_pairs={{0,24},{2,26},{4,28},{6,30},{8,16},{10,18},{12,20},{14,22},{16,8},... | collective-permute-start | bytes 11010056 | tf_op jit(solution)/shard_map/hop_out3/ppermute | solution.py:100
  596.2 37.6 %copy-start.42 = (bf16[256,3584]{1,0:T(8,128)(2,1)}, bf16[256,3584]{1,0:T(8,128)(2,1)S(1)}, u32[]{:S(2)}) copy-start(bf16[256,3584]{1,0:T(8,128)(2,1)S(1)} %collective-permute-done.19) | copy-start | bytes 5505028
  596.2 239.2 %collective-permute-start.22 = (bf16[512,3584]{1,0:T(8,128)(2,1)}, bf16[512,3584]{1,0:T(8,128)(2,1)}, u32[]{:S(2)}, u32[]{:S(2)}) collective-permute-start(bf16[512,3584]{1,0:T(8,128)(2,1)} %pad_maximum_fusion.1), channel_id=1, source_target_pairs={{0,8},{2,10},{4,12},{6,14},{8,0},{10,2},{12,4},{14,6},{16,24},{18,... | collective-permute-start | bytes 11010056 | tf_op jit(solution)/shard_map/hop_out1/ppermute | solution.py:100
  649.7 82.3 %collective-permute-start.21 = (bf16[1024,1024]{1,0:T(8,128)(2,1)}, bf16[1024,1024]{1,0:T(8,128)(2,1)}, u32[]{:S(2)}, u32[]{:S(2)}) collective-permute-start(bf16[1024,1024]{1,0:T(8,128)(2,1)} %fusion.57), channel_id=1, source_target_pairs={{0,1},{1,0},{2,3},{3,2},{4,5},{5,4},{6,7},{7,6},{8,9},{9,8},{10,11... | collective-permute-start | bytes 6291464 | tf_op jit(solution)/shard_map/terms_own/ppermute | solution.py:161
  669.4 54.4 %copy-start = (bf16[512,1024]{1,0:T(8,128)(2,1)S(1)}, bf16[512,1024]{1,0:T(8,128)(2,1)}, u32[]{:S(2)}) copy-start(bf16[512,1024]{1,0:T(8,128)(2,1)} %fusion.43.refs_1_) | copy-start | bytes 3145732
  723.8 46.0 %collective-permute-start.29 = (bf16[512,1024]{1,0:T(8,128)(2,1)S(1)}, bf16[512,1024]{1,0:T(8,128)(2,1)}, u32[]{:S(2)}, u32[]{:S(2)}) collective-permute-start(bf16[512,1024]{1,0:T(8,128)(2,1)S(1)} %get-tuple-element.76), channel_id=1, source_target_pairs={{0,16},{2,18},{4,20},{6,22},{8,24},{10,26},{12,28},{14,30},{16,0},... | collective-permute-start | bytes 3145736 | tf_op jit(solution)/shard_map/hop_hidden2/ppermute | solution.py:100
  723.8 68.5 %collective-permute-start.30 = (bf16[512,1024]{1,0:T(8,128)(2,1)S(1)}, bf16[512,1024]{1,0:T(8,128)(2,1)}, u32[]{:S(2)}, u32[]{:S(2)}) collective-permute-start(bf16[512,1024]{1,0:T(8,128)(2,1)S(1)} %get-tuple-element.77), channel_id=1, source_target_pairs={{8,24},{10,26},{12,28},{14,30},{16,0},{18,2},{20,4},{22,6},{9,25},... | collective-permute-start | bytes 3145736 | tf_op jit(solution)/shard_map/hop_hidden3/ppermute | solution.py:100
  729.6 85.5 %collective-permute-start.31 = (bf16[512,1024]{1,0:T(8,128)(2,1)}, bf16[512,1024]{1,0:T(8,128)(2,1)}, u32[]{:S(2)}, u32[]{:S(2)}) collective-permute-start(bf16[512,1024]{1,0:T(8,128)(2,1)} %get-tuple-element.78), channel_id=1, source_target_pairs={{8,16},{10,18},{12,20},{14,22},{16,8},{18,10},{20,12},{22,14},{9,1... | collective-permute-start | bytes 3145736 | tf_op jit(solution)/shard_map/hop_hidden3/ppermute | solution.py:100
  742.3 72.7 %copy-start.38 = (f32[2,1024]{1,0:T(2,128)S(1)}, f32[2,1024]{1,0:T(2,128)}, u32[]{:S(2)}) copy-start(f32[2,1024]{1,0:T(2,128)} %bitcast_multiply_fusion.4) | copy-start | bytes 24580
  818.4 9.6 %copy-start.32 = (bf16[128,3584]{1,0:T(8,128)(2,1)S(1)}, bf16[128,3584]{1,0:T(8,128)(2,1)}, u32[]{:S(2)}) copy-start(bf16[128,3584]{1,0:T(8,128)(2,1)} %get-tuple-element.124) | copy-start | bytes 2752516
  (28 other events, 100.8 us)

commit v3 on v0

v3 whole, which is shorter than its diff:
```python
import functools

import jax
import jax.numpy as jnp
from jax import lax
from jax.experimental import pallas as pl
from jax.experimental.pallas import tpu as pltpu
from jax.sharding import PartitionSpec as P

SLABS = 4
CORES = 2


def gather_kernel(counts, chosen, proj_in, proj_out, *rest):
    outs, (held_in, flat_in, held_out, sems) = rest[:-4], rest[-4:]
    count_in, count_out = counts
    high_in, high_out = flat_in.shape[1], held_out.shape[1]
    size = count_in * high_in + count_out * high_out
    moves = []
    for core in range(CORES):
        out, base = (outs[0], core * size) if len(outs) == 1 else (outs[core], 0)
        for n in range(count_in + count_out):
            item = core * (count_in + count_out) + n
            if n < count_in:
                slot, row = core * count_in + n, base + n * high_in
                into = pltpu.make_async_copy(
                    proj_in.at[chosen[item]], held_in.at[slot], sems.at[0, item]
                )
                move = pltpu.make_async_copy(
                    flat_in.at[slot], out.at[pl.ds(row, high_in)], sems.at[1, item]
                )
            else:
                slot = core * count_out + n - count_in
                row = base + count_in * high_in + (n - count_in) * high_out
                into = pltpu.make_async_copy(
                    proj_out.at[chosen[item]], held_out.at[slot], sems.at[0, item]
                )
                move = pltpu.make_async_copy(
                    held_out.at[slot], out.at[pl.ds(row, high_out)], sems.at[1, item]
                )
            moves.append((into, move, slot if n < count_in else None))
    for into, _, _ in moves:
        into.start()
    for into, move, slot in moves:
        into.wait()
        if slot is not None:

            @pl.loop(0, high_in // 16)
            def _(block):
                pairs = held_in[slot, pl.ds(block * 8, 8)]
                flat_in[slot, pl.ds(pl.multiple_of(block * 16, 16), 16)] = pairs.reshape(
                    16, flat_in.shape[2]
                )

        move.start()
    for _, move, _ in moves:
        move.wait()


def gather_experts(chosen, proj_in, proj_out, counts, parts):
    width = proj_in.shape[-1]
    high_in, high_out = 2 * proj_in.shape[1], proj_out.shape[1]
    rows = CORES * (counts[0] * high_in + counts[1] * high_out)
    anywhere = pl.BlockSpec(memory_space=pl.ANY)
    got = pl.pallas_call(
        functools.partial(gather_kernel, counts),
        out_shape=[jax.ShapeDtypeStruct((rows // parts, width), proj_in.dtype)] * parts,
        grid_spec=pltpu.PrefetchScalarGridSpec(
            num_scalar_prefetch=1,
            grid=(),
            in_specs=[anywhere] * 2,
            out_specs=[anywhere] * parts,
            scratch_shapes=[
                pltpu.VMEM((max(CORES * counts[0], 1),) + proj_in.shape[1:], proj_in.dtype),
                pltpu.VMEM((max(CORES * counts[0], 1), high_in, width), proj_in.dtype),
                pltpu.VMEM((max(CORES * counts[1], 1), high_out, width), proj_out.dtype),
                pltpu.SemaphoreType.DMA((2, CORES * sum(counts))),
            ],
        ),
        compiler_params=pltpu.CompilerParams(vmem_limit_bytes=40 << 20),
    )(chosen, proj_in, proj_out)
    return list(got)


def hold_kernel(*refs):
    del refs


def hold_until(values, landed):
    count = len(values)
    anywhere = pl.BlockSpec(memory_space=pl.ANY)
    return pl.pallas_call(
        hold_kernel,
        out_shape=[jax.ShapeDtypeStruct(v.shape, v.dtype) for v in values],
        in_specs=[anywhere] * (count + len(landed)),
        out_specs=[anywhere] * count,
        input_output_aliases={n: n for n in range(count)},
        compiler_params=pltpu.CompilerParams(vmem_limit_bytes=1 << 20),
    )(*values, *landed)


def add_product_kernel(left, right, total, result):
    product = jnp.dot(left[...], right[...], preferred_element_type=jnp.float32)
    result[...] = (total[...] + product).astype(result.dtype)


def add_product(left, right, total):
    rows, depth = left.shape
    width = right.shape[1]
    block = next(n for n in (512, 384, 256, 128) if width % n == 0)
    return pl.pallas_call(
        add_product_kernel,
        grid=(width // block,),
        in_specs=[
            pl.BlockSpec((rows, depth), lambda n: (0, 0)),
            pl.BlockSpec((depth, block), lambda n: (0, n)),
            pl.BlockSpec((rows, block), lambda n: (0, n)),
        ],
        out_specs=pl.BlockSpec((rows, block), lambda n: (0, n)),
        out_shape=jax.ShapeDtypeStruct((rows, width), left.dtype),
        compiler_params=pltpu.CompilerParams(vmem_limit_bytes=24 << 20),
    )(left, right, total)


def on_device(tokens, proj_in, proj_out, expert_list, block_pattern, route_weight):
    dp_size = lax.axis_size("dp")
    group_size = lax.axis_size("group")
    peers = dp_size // SLABS
    dp_index = lax.axis_index("dp")
    group_index = lax.axis_index("group")
    slab = dp_index // peers
    column = dp_index % peers
    rows = tokens.shape[0]
    slots = expert_list.shape[1]
    units = proj_in.shape[1]
    block_rows = rows // block_pattern.shape[2]
    share = rows // group_size

    def over_z(value, hops, offset=0):
        pairs = [(a * peers + j, b * peers + (j ^ offset)) for a, b in hops for j in range(peers)]
        return lax.ppermute(value, "dp", pairs)

    def over_group(value, offset):
        pairs = [(g, (g + offset) % group_size) for g in range(group_size)]
        return lax.ppermute(value, "group", pairs)

    same = [(a, a) for a in range(SLABS)]
    middle = [(1, 2), (2, 1)]
    low_half = slab < 2
    outer = (slab == 0) | (slab == 3)
    far, mid, near, own = jnp.where(low_half, 3, 0), jnp.where(low_half, 2, 1), slab ^ 1, slab

    def gathered(in_slabs, out_slabs):
        counts = (slots * len(in_slabs), slots * len(out_slabs))

        def slices(chip, parts):
            chosen = jnp.concatenate(
                [
                    lax.dynamic_index_in_dim(
                        expert_list, s * peers + (column ^ (CORES * chip + core)), 0, keepdims=False
                    )
                    for core in range(CORES)
                    for s in in_slabs + out_slabs
                ]
            )
            return gather_experts(chosen, proj_in, proj_out, counts, parts)

        kept, sibling = slices(0, CORES)
        return [slices(chip, 1)[0] for chip in range(1, peers // CORES)] + [kept, sibling]

    def over_chips(name, gather, start_after):
        sends = gather[:-2]
        if start_after:
            sends = hold_until(sends, start_after)
        with jax.named_scope("hop_chips_" + name):
            return [over_z(v, same, CORES * (n + 1)) for n, v in enumerate(sends)]

    def over_cores(name, gather, across, merged=True):
        kept, sibling = gather[-2:]
        size = kept.shape[0]
        parts = [sibling] + [v[size:] for v in across]
        if merged:
            parts = [jnp.concatenate(parts, axis=0)]
        else:
            parts[:1] = hold_until(parts[:1], across)
        with jax.named_scope("hop_cores_" + name):
            swapped = [over_z(v, same, 1) for v in parts]
        if merged:
            swapped = [swapped[0][n * size : (n + 1) * size] for n in range(1 + len(across))]
        return [kept] + [v[:size] for v in across] + swapped

    def joined(pieces, low, high):
        return jnp.concatenate([v[low:high] for v in pieces], axis=0)

    rows_in, rows_out = slots * units * 2, slots * units

    def terms_of(token_rows, weight_in):
        return lax.dot_general(
            weight_in, token_rows, (((1,), (1,)), ((), ())), preferred_element_type=jnp.float32
        ).astype(jnp.bfloat16)

    def gated(total):
        total = total.reshape(-1, 2, total.shape[1])
        return (jax.nn.silu(total[:, 0]) * total[:, 1]).astype(jnp.bfloat16)

    def hidden_of(name, part):
        total = part.astype(jnp.float32)
        for offset in range(1, group_size):
            with jax.named_scope("terms_" + name):
                total = total + over_group(part, offset).astype(jnp.float32)
        return gated(total)

    def hidden_share_of(name, part):
        def share_of(member):
            return lax.dynamic_slice_in_dim(part, member * share, share, 1)

        total = share_of(group_index).astype(jnp.float32)
        for offset in range(1, group_size):
            with jax.named_scope("terms_" + name):
                moved = over_group(share_of((group_index + offset) % group_size), offset)
                total = total + moved.astype(jnp.float32)
        return gated(total)

    def all_rows(name, piece):
        result = jnp.zeros((piece.shape[0], rows), piece.dtype)
        for offset in range(group_size):
            with jax.named_scope("terms_" + name):
                moved = over_group(piece, offset) if offset else piece
            member = (group_index - offset) % group_size
            result = lax.dynamic_update_slice_in_dim(result, moved, member * share, 1)
        return result

    first = gathered([far], [slab ^ 2, slab ^ 3])
    second = gathered([mid, near], [])
    third = gathered([own], [own, near])

    with jax.named_scope("hop_right1"):
        right1 = over_z(tokens, [(0, 1), (1, 2), (2, 3)])
    with jax.named_scope("hop_left1"):
        left1 = over_z(tokens, [(3, 2), (2, 1), (1, 0)])
    across1 = over_chips("one", first, [])
    across1 = list(hold_until(across1, [right1, left1] + second + third))

    with jax.named_scope("hop_right2"):
        right2 = over_z(right1, [(1, 2), (2, 3)])
    with jax.named_scope("hop_left2"):
        left2 = over_z(left1, [(2, 1), (1, 0)])
    across2 = over_chips("two", second, across1)
    pieces = over_cores("one", first, across1, merged=False)
    far_in = joined(pieces, 0, rows_in)
    out2 = joined(pieces, rows_in, rows_in + rows_out)
    out3 = joined(pieces, rows_in + rows_out, rows_in + 2 * rows_out)
    with jax.named_scope("hop_edge"):
        edge_in = over_z(far_in, [(0, 1), (3, 2)])

    (out2,) = hold_until([out2], [right2, left2] + across2)
    with jax.named_scope("hop_out2"):
        out2 = over_z(out2, [(a, a ^ 2) for a in range(SLABS)])
    across3 = over_chips("three", third, across2 + [right2, left2])
    pieces = over_cores("two", second, across2)
    mid_in, near_in = joined(pieces, 0, rows_in), joined(pieces, rows_in, 2 * rows_in)
    toward1 = jnp.where(low_half, left1, right1)
    away1 = jnp.where(low_half, right1, left1)
    toward2 = jnp.where(low_half, left2, right2)
    far_hidden = hidden_share_of("far", terms_of(toward2, far_in))
    mid_hidden = hidden_share_of("mid", terms_of(jnp.where(outer, toward2, toward1), mid_in))
    edge_hidden = hidden_share_of("edge", terms_of(toward2, edge_in))
    near_hidden = hidden_of("near", terms_of(jnp.where(outer, toward1, away1), near_in))
    cross_hidden = jnp.where(outer, mid_hidden, far_hidden)
    with jax.named_scope("hop_hidden3"):
        edge_hidden = over_z(edge_hidden, [(1, 3), (2, 0)])

    out3, cross_hidden, mid_hidden = hold_until(
        [out3, cross_hidden, mid_hidden], [out2, near_hidden, edge_hidden]
    )
    across3 = list(hold_until(across3, [out3, cross_hidden, mid_hidden]))
    with jax.named_scope("hop_out3"):
        out3 = over_z(out3, [(a, a ^ 3) for a in range(SLABS)])
    with jax.named_scope("hop_hidden2"):
        hidden2 = over_z(cross_hidden, [(a, a ^ 2) for a in range(SLABS)])
    with jax.named_scope("hop_hidden3"):
        hidden3 = jnp.where(outer, edge_hidden, over_z(mid_hidden, middle))
    pieces = over_cores("three", third, across3)
    own_in = joined(pieces, 0, rows_in)
    out0 = joined(pieces, rows_in, rows_in + rows_out)
    out1 = joined(pieces, rows_in + rows_out, rows_in + 2 * rows_out)
    both1 = jnp.concatenate([out1, near_hidden], axis=1)
    with jax.named_scope("hop_out1"):
        both1 = over_z(both1, [(a, a ^ 1) for a in range(SLABS)])
    out1, hidden1 = both1[:, : out1.shape[1]], both1[:, out1.shape[1] :]
    own_hidden = hidden_of("own", terms_of(tokens, own_in))

    own_pattern = lax.dynamic_index_in_dim(block_pattern, dp_index, 0, keepdims=False)
    scale = route_weight.T * jnp.repeat(own_pattern, block_rows, axis=1).astype(jnp.float32)

    def weighted(hiddens):
        hidden = jnp.concatenate(hiddens, axis=0).astype(jnp.float32)
        hidden = hidden.reshape(-1, slots, units, rows) * scale[None, :, None, :]
        return hidden.astype(jnp.bfloat16).reshape(-1, rows)

    total = lax.dot_general(
        weighted([own_hidden, hidden1]),
        jnp.concatenate([out0, out1], axis=0),
        (((0,), (0,)), ((), ())),
        preferred_element_type=jnp.float32,
    )

    crossed = jnp.concatenate([hidden2, hidden3], axis=0)
    (crossed,) = hold_until([crossed], [out3, own_hidden])
    crossed = weighted([all_rows("rows", crossed)]).T
    return add_product(crossed, jnp.concatenate([out2, out3], axis=0), total)


def solution(mesh):
    return jax.shard_map(
        on_device,
        mesh=mesh,
        in_specs=(
            P("dp", "group"),
            P(None, "dp", None, "group"),
            P(None, "dp", "group"),
            P(),
            P(),
            P("dp", None),
        ),
        out_specs=P("dp", "group"),
        check_vma=False,
    )
```

time: 1150 us -> 838 us (0.73)
  waiting for transfers between devices: 800 us -> 464 us
  local copies, waits for them, and re-layouts: 227 us -> 135 us
  Pallas kernels: 0 us -> 47.8 us
  starting transfers between devices: 13.1 us -> 42.2 us
  other arithmetic: 33.7 us -> 61.5 us
  matrix products: 61.7 us -> 81 us
  between operations: 13.5 us -> 1.02 us
    all_to_all x2 -> x0, waiting for transfers between devices: 700 us -> none  [the longest x1 530 us: on_device(): lax.all_to_all(send_in, 'dp', split_axis=1, concat_axis=1, tiled=True)]
    ppermute x0 -> x24, waiting for transfers between devices: none -> 464 us  [the longest x18 410 us: over_z(): return lax.ppermute(value, 'dp', pairs)]
    select_n x2 -> x0, local copies, waits for them, and re-layouts: 134 us -> none  [the longest x1 80.7 us: on_device(): jnp.take(proj_out, requested, axis=0).reshape(slots, -1, width_here)]
    reduce_scatter x1 -> x0, waiting for transfers between devices: 100 us -> none  [on_device(): lax.psum_scatter(partial_here.astype(jnp.bfloat16), 'group', scatter_dime...]
    gather x3 -> x0, local copies, waits for them, and re-layouts: 92.4 us -> none  [the longest x2 79.6 us: on_device(): jnp.take(proj_in, requested, axis=0).reshape(slots, -1, 2, width_here)]
    slice x0 -> x25, local copies, waits for them, and re-layouts: none -> 80.9 us  [the longest x17 43.9 us: joined(): return jnp.concatenate([v[low:high] for v in pieces], axis=0)]
    pallas_call x0 -> x15, Pallas kernels: none -> 47.8 us  [the longest x6 36.5 us: gather_experts(): pl.pallas_call(functools.partial(gather_kernel, counts), out_shape=[jax.S...]
    ppermute x0 -> x24, starting transfers between devices: none -> 42.2 us  [the longest x18 35.9 us: over_z(): return lax.ppermute(value, 'dp', pairs)]
  transfers between devices with their start and end apart: 4 -> 24, of which waited for: 3 -> 13; matrix products, arithmetic and copies ran while one was open for 13% -> 28% of each run, Pallas kernels for 0% -> 4%
where the time goes in v3:
time: 838 us; the launch traced here: 832 us
  waiting for transfers between devices  464 us (55%)
  local copies, waits for them, and re-layouts  135 us (16%)
  matrix products  81 us (10%)
  other arithmetic  61.5 us (7%)
  Pallas kernels  47.8 us (6%)
  starting transfers between devices  42.2 us (5%)
    ppermute x18, waiting for transfers between devices, over_z(): return lax.ppermute(value, 'dp', pairs)  410 us
    dot_general x5, matrix products, terms_of(): lax.dot_general(weight_in, token_rows, (((1,), (1,)), ((), ())), preferre...  68.8 us
    ppermute x6, waiting for transfers between devices, over_group(): return lax.ppermute(value, 'group', pairs)  54.8 us
    slice x17, local copies, waits for them, and re-layouts, joined(): return jnp.concatenate([v[low:high] for v in pieces], axis=0)  43.9 us
    pallas_call x6, Pallas kernels, gather_experts(): pl.pallas_call(functools.partial(gather_kernel, counts), out_shape=[jax.S...  36.5 us
    ppermute x18, starting transfers between devices, over_z(): return lax.ppermute(value, 'dp', pairs)  35.9 us
    slice x4, local copies, waits for them, and re-layouts, gated(): return (jax.nn.silu(total[:, 0]) * total[:, 1]).astype(jnp.bfloat16)  23.4 us
    reshape x5, local copies, waits for them, and re-layouts, gated(): total = total.reshape(-1, 2, total.shape[1])  18.9 us
  transfers between devices with their start and end apart: 24, of which 13 were waited for; matrix products, arithmetic and copies ran while one was open for 28% of the time, Pallas kernels for 4%

profile of v3, /device:TPU:8, one launch (start us, length us, event | category | flops | bytes accessed | tf_op | source)
XLA Modules:
  0.0 832.5 jit_solution(15454720097330845067)
XLA Ops:
  1.9 6.7 shard_map.65
  13.6 5.3 collective-permute-start.2
  19.1 4.8 shard_map.67
  27.5 6.8 shard_map.66.refs_3_.refs_0_
  34.4 6.7 shard_map.68.refs_6_.refs_0_
  41.6 5.9 shard_map.69
  47.4 121.3 %collective-permute-done.refs_0_ = bf16[1024,3584]{1,0:T(8,128)(2,1)} collective-permute-done((bf16[1024,3584]{1,0:T(8,128)(2,1)}, bf16[1024,3584]{1,0:T(8,128)(2,1)}, u32[]{:S(2)}, u32[]{:S(2)}) %collective-permute-start) | collective-permute-done | bytes 7340064 | tf_op jit(solution)/shard_map/hop_chips_one/ppermute | solution.py:141
  171.6 4.1 collective-permute-done.2.refs_2_
  176.6 5.7 shard_map.64
  184.2 4.1 slice.215
  190.4 4.7 collective-permute-start.7
  195.1 7.4 collective-permute-start.8
  208.9 3.5 fusion.95
  216.3 3.6 pad_maximum_fusion.1
  227.0 107.1 %collective-permute-done.5.refs_3_.refs_1_ = bf16[1024,3584]{1,0:T(8,128)(2,1)} collective-permute-done((bf16[1024,3584]{1,0:T(8,128)(2,1)}, bf16[1024,3584]{1,0:T(8,128)(2,1)}, u32[]{:S(2)}, u32[]{:S(2)}) %collective-permute-start.5) | collective-permute-done | bytes 7340064 | tf_op jit(solution)/shard_map/hop_chips_two/ppermute | solution.py:141
  334.1 4.2 slice.218
  338.3 5.5 pad_maximum_fusion
  343.8 3.5 pad_maximum_fusion.6.refs_0_
  352.8 4.1 collective-permute-done.8.refs_1_.refs_2_
  359.2 6.8 broadcast_select_fusion.1
  366.0 14.4 %convolution_convert_fusion.1 = bf16[1024,1024]{1,0:T(8,128)(2,1)} fusion(bf16[1024,3584]{1,0:T(8,128)(2,1)} %broadcast_select_fusion.1, bf16[256,3584]{1,0:T(8,128)(2,1)} %copy-done.22, bf16[256,3584]{1,0:T(8,128)(2,1)} %copy-done.21, bf16[256,3584]{1,0:T(8,128)(2,1)} %copy-done.20, bf16[256,3584]{1,0:T(8,128)(2,1)S(1)} %copy-done.19), kind=kOutput, calls=%fused_computation.64 | convolution fusion | flops 7546601472 | bytes 16777216 | tf_op jit(solution)/shard_map/dot_general | solution.py:198
  384.6 4.1 fusion.93
  388.7 17.0 %collective-permute-done.10 = bf16[1024,512]{1,0:T(8,128)(2,1)S(1)} collective-permute-done((bf16[1024,512]{1,0:T(8,128)(2,1)S(1)}, bf16[1024,512]{1,0:T(8,128)(2,1)S(1)}, u32[]{:S(2)}, u32[]{:S(2)}) %collective-permute-start.10) | collective-permute-done | bytes 1048608 | tf_op jit(solution)/shard_map/terms_far/ppermute | solution.py:145
  408.3 12.2 %convolution_convert_fusion = bf16[1024,1024]{1,0:T(8,128)(2,1)S(1)} fusion(bf16[1024,3584]{1,0:T(8,128)(2,1)} %collective-permute-done.13, bf16[1024,3584]{1,0:T(8,128)(2,1)} %broadcast_select_fusion.1), kind=kOutput, calls=%fused_computation.63 | convolution fusion | flops 7517241344 | bytes 16777216 | tf_op jit(solution)/shard_map/dot_general | solution.py:198
  424.5 6.3 fusion.94
  430.8 12.0 %fusion.47 = bf16[1024,1024]{1,0:T(8,128)(2,1)S(1)} fusion(bf16[1024,3584]{1,0:T(8,128)(2,1)} %broadcast_select_fusion.1, bf16[1024,3584]{1,0:T(8,128)(2,1)} %collective-permute-done.2.refs_2_, bf16[1024,3584]{1,0:T(8,128)(2,1)} %collective-permute-done.1.refs_1_, pred[]{:T(512)S(6)} %lt.124, pred[]{:T(512)S(6)} %or.3, ...), kind=kOutput, calls=%fused_computation.62 | convolution fusion | flops 7553941504 | bytes 31457282 | tf_op jit(solution)/shard_map/dot_general | solution.py:198
  444.5 16.4 %fusion.42 = bf16[1024,1024]{1,0:T(8,128)(2,1)} fusion(bf16[1024,3584]{1,0:T(8,128)(2,1)} %collective-permute-done.1.refs_1_, bf16[1024,3584]{1,0:T(8,128)(2,1)} %collective-permute-done.2.refs_2_, pred[]{:T(512)S(6)} %lt.124, pred[]{:T(512)S(6)} %or.3, bf16[256,3584]{1,0:T(8,128)(2,1)} %get-tuple-element.59, bf16[256,3584]{1,0:T(8,128)(2,1)} %get-tuple-element.58, ...), kind=kOutput, calls=%fused_computation.61 | convolution fusion | flops 7557611520 | bytes 24117250 | tf_op jit(solution)/shard_map/dot_general | solution.py:198
  477.1 7.6 fusion.103
  485.3 28.5 %collective-permute-done.12 = bf16[1024,1024]{1,0:T(8,128)(2,1)} collective-permute-done((bf16[1024,1024]{1,0:T(8,128)(2,1)}, bf16[1024,1024]{1,0:T(8,128)(2,1)}, u32[]{:S(2)}, u32[]{:S(2)}) %collective-permute-start.12) | collective-permute-done | bytes 2097184 | tf_op jit(solution)/shard_map/terms_near/ppermute | solution.py:145
  513.8 4.5 convert_add_fusion.1
  518.3 6.0 reshape.28
  524.4 7.1 fusion.97
  533.3 8.8 %collective-permute-done.19.refs_0_ = bf16[1024,3584]{1,0:T(8,128)(2,1)} collective-permute-done((bf16[1024,3584]{1,0:T(8,128)(2,1)}, bf16[1024,3584]{1,0:T(8,128)(2,1)}, u32[]{:S(2)}, u32[]{:S(2)}) %collective-permute-start.19) | collective-permute-done | bytes 7340064 | tf_op jit(solution)/shard_map/hop_chips_three/ppermute | solution.py:141
  542.1 4.1 slice.239
  546.2 6.8 pad_maximum_fusion.2
  569.4 13.8 %fusion.39 = bf16[1024,1024]{1,0:T(8,128)(2,1)} fusion(bf16[1024,3584]{1,0:T(8,128)(2,1)} %param.6, bf16[256,3584]{1,0:T(8,128)(2,1)} %get-tuple-element.55, bf16[256,3584]{1,0:T(8,128)(2,1)S(1)} %get-tuple-element.54, bf16[256,3584]{1,0:T(8,128)(2,1)} %slice.238, bf16[256,3584]{1,0:T(8,128)(2,1)} %slice.196), kind=kOutput, calls=%fused_computation.60 | convolution fusion | flops 7546601472 | bytes 16777216 | tf_op jit(solution)/shard_map/dot_general | solution.py:198
  588.8 7.8 pad_maximum_fusion.4
  600.2 130.6 %collective-permute-done.17 = bf16[512,512]{1,0:T(8,128)(2,1)S(1)} collective-permute-done((bf16[512,512]{1,0:T(8,128)(2,1)S(1)}, bf16[512,512]{1,0:T(8,128)(2,1)S(1)}, u32[]{:S(2)}, u32[]{:S(2)}) %collective-permute-start.17) | collective-permute-done | bytes 524320 | tf_op jit(solution)/shard_map/hop_hidden3/ppermute | solution.py:141
  730.9 23.9 %collective-permute-done.16 = bf16[512,512]{1,0:T(8,128)(2,1)S(1)} collective-permute-done((bf16[512,512]{1,0:T(8,128)(2,1)S(1)}, bf16[512,512]{1,0:T(8,128)(2,1)S(1)}, u32[]{:S(2)}, u32[]{:S(2)}) %collective-permute-start.16) | collective-permute-done | bytes 524320 | tf_op jit(solution)/shard_map/hop_hidden2/ppermute | solution.py:141
  754.8 5.1 convert_add_fusion
  760.0 5.8 reshape.30
  765.8 7.1 fusion.96
  777.6 5.4 copy.42
  783.0 6.7 pad_maximum_fusion.3.right
  790.0 9.3 %collective-permute-done.22 = bf16[1024,512]{0,1:T(8,128)(2,1)S(1)} collective-permute-done((bf16[1024,512]{0,1:T(8,128)(2,1)S(1)}, bf16[1024,512]{0,1:T(8,128)(2,1)S(1)}, u32[]{:S(2)}, u32[]{:S(2)}) %collective-permute-start.22) | collective-permute-done | bytes 1048608 | tf_op jit(solution)/shard_map/terms_rows/ppermute | solution.py:145
  801.6 4.1 slice_dynamic-update-slice_fusion
  805.7 12.1 %fusion.31.total = f32[1024,3584]{1,0:T(8,128)S(1)} fusion(bf16[1024,3584]{1,0:T(8,128)(2,1)} %slice_dynamic-update-slice_fusion, f32[1024,1024]{1,0:T(8,128)} %bitcast.71, bf16[512,1024]{1,0:T(8,128)(2,1)S(1)} %slice.247, bf16[512,1024]{1,0:T(8,128)(2,1)S(1)} %fusion.36.refs_2_), kind=kOutput, calls=%fused_computation.45 | convolution fusion | flops 7522484224 | bytes 28311552 | tf_op jit(solution)/shard_map/dot_general | solution.py:301
  821.0 11.2 %shard_map.78 = bf16[1024,3584]{1,0:T(8,128)(2,1)} custom-call(bf16[1024,1024]{1,0:T(8,128)(2,1)S(1)} %fusion.30.left, bf16[1024,3584]{1,0:T(8,128)(2,1)S(1)} %copy-done, f32[1024,3584]{1,0:T(8,128)S(1)} %fusion.31.total), custom_call_target="tpu_custom_call" | custom-call | tf_op jit(solution)/shard_map/pallas_call | solution.py:111
  (165 shorter events, 111.0 us)
Async XLA Ops:
  8.6 160.1 %collective-permute-start = (bf16[1024,3584]{1,0:T(8,128)(2,1)}, bf16[1024,3584]{1,0:T(8,128)(2,1)}, u32[]{:S(2)}, u32[]{:S(2)}) collective-permute-start(bf16[1024,3584]{1,0:T(8,128)(2,1)} %shard_map.65), channel_id=1, source_target_pairs={{0,4},{2,6},{4,0},{6,2},{8,12},{10,14},{12,8},{14,10},{16,20},{18,... | collective-permute-start | bytes 22020104 | tf_op jit(solution)/shard_map/hop_chips_one/ppermute | solution.py:141
  10.2 161.4 %collective-permute-start.1 = (bf16[1024,3584]{1,0:T(8,128)(2,1)}, bf16[1024,3584]{1,0:T(8,128)(2,1)}, u32[]{:S(2)}, u32[]{:S(2)}) collective-permute-start(bf16[1024,3584]{1,0:T(8,128)(2,1)} %param.6), channel_id=1, source_target_pairs={{0,8},{2,10},{4,12},{6,14},{8,16},{10,18},{12,20},{14,22},{16,24},... | collective-permute-start | bytes 22020104 | tf_op jit(solution)/shard_map/hop_right1/ppermute | solution.py:141
  13.6 162.1 %collective-permute-start.2 = (bf16[1024,3584]{1,0:T(8,128)(2,1)}, bf16[1024,3584]{1,0:T(8,128)(2,1)}, u32[]{:S(2)}, u32[]{:S(2)}) collective-permute-start(bf16[1024,3584]{1,0:T(8,128)(2,1)} %param.6), channel_id=1, source_target_pairs={{24,16},{26,18},{28,20},{30,22},{16,8},{18,10},{20,12},{22,14},{8,... | collective-permute-start | bytes 22020104 | tf_op jit(solution)/shard_map/hop_left1/ppermute | solution.py:141
  34.4 6.7 copy-start.33
  41.6 134.1 %copy-start.5 = (bf16[512,3584]{1,0:T(8,128)(2,1)S(1)}, bf16[512,3584]{1,0:T(8,128)(2,1)}, u32[]{:S(2)}) copy-start(bf16[512,3584]{1,0:T(8,128)(2,1)} %copy-done.4) | copy-start | bytes 11010052
  41.6 134.1 %copy-start.8 = (bf16[512,3584]{1,0:T(8,128)(2,1)S(1)}, bf16[512,3584]{1,0:T(8,128)(2,1)}, u32[]{:S(2)}) copy-start(bf16[512,3584]{1,0:T(8,128)(2,1)} %copy-done.7) | copy-start | bytes 11010052
  47.4 128.3 %copy-start.1 = (bf16[512,3584]{1,0:T(8,128)(2,1)}, bf16[512,3584]{1,0:T(8,128)(2,1)S(1)}, u32[]{:S(2)}) copy-start(bf16[512,3584]{1,0:T(8,128)(2,1)S(1)} %get-tuple-element.17.refs_7_) | copy-start | bytes 11010052
  47.4 128.3 %copy-start.3 = (bf16[512,3584]{1,0:T(8,128)(2,1)}, bf16[512,3584]{1,0:T(8,128)(2,1)S(1)}, u32[]{:S(2)}) copy-start(bf16[512,3584]{1,0:T(8,128)(2,1)S(1)} %get-tuple-element.18.refs_8_) | copy-start | bytes 11010052
  175.7 158.4 %collective-permute-start.5 = (bf16[1024,3584]{1,0:T(8,128)(2,1)}, bf16[1024,3584]{1,0:T(8,128)(2,1)}, u32[]{:S(2)}, u32[]{:S(2)}) collective-permute-start(bf16[1024,3584]{1,0:T(8,128)(2,1)} %shard_map.72), channel_id=1, source_target_pairs={{0,4},{2,6},{4,0},{6,2},{8,12},{10,14},{12,8},{14,10},{16,20},{18,... | collective-permute-start | bytes 22020104 | tf_op jit(solution)/shard_map/hop_chips_two/ppermute | solution.py:141
  184.2 28.2 %collective-permute-start.3 = (bf16[512,3584]{1,0:T(8,128)(2,1)}, bf16[512,3584]{1,0:T(8,128)(2,1)}, u32[]{:S(2)}, u32[]{:S(2)}) collective-permute-start(bf16[512,3584]{1,0:T(8,128)(2,1)} %shard_map.71), channel_id=1, source_target_pairs={{0,2},{2,0},{4,6},{6,4},{8,10},{10,8},{12,14},{14,12},{16,18},{18,... | collective-permute-start | bytes 11010056 | tf_op jit(solution)/shard_map/hop_cores_one/ppermute | solution.py:141
  188.3 25.7 %collective-permute-start.4 = (bf16[512,3584]{1,0:T(8,128)(2,1)}, bf16[512,3584]{1,0:T(8,128)(2,1)}, u32[]{:S(2)}, u32[]{:S(2)}) collective-permute-start(bf16[512,3584]{1,0:T(8,128)(2,1)} %slice.215), channel_id=1, source_target_pairs={{0,2},{2,0},{4,6},{6,4},{8,10},{10,8},{12,14},{14,12},{16,18},{18,... | collective-permute-start | bytes 11010056 | tf_op jit(solution)/shard_map/hop_cores_one/ppermute | solution.py:141
  190.4 25.9 %copy-start.18 = (bf16[256,3584]{1,0:T(8,128)(2,1)}, bf16[256,3584]{1,0:T(8,128)(2,1)S(1)}, u32[]{:S(2)}) copy-start(bf16[256,3584]{1,0:T(8,128)(2,1)S(1)} %slice.178) | copy-start | bytes 5505028
  190.4 14.6 %copy-start.9 = (bf16[512,3584]{1,0:T(8,128)(2,1)S(1)}, bf16[512,3584]{1,0:T(8,128)(2,1)}, u32[]{:S(2)}) copy-start(bf16[512,3584]{1,0:T(8,128)(2,1)} %copy-done.7) | copy-start | bytes 11010052
  190.4 162.4 %collective-permute-start.7 = (bf16[1024,3584]{1,0:T(8,128)(2,1)}, bf16[1024,3584]{1,0:T(8,128)(2,1)}, u32[]{:S(2)}, u32[]{:S(2)}) collective-permute-start(bf16[1024,3584]{1,0:T(8,128)(2,1)} %collective-permute-done.2.refs_2_), channel_id=1, source_target_pairs={{16,8},{18,10},{20,12},{22,14},{8,0},{10,2},{12,4},{14,6},{17,9},{... | collective-permute-start | bytes 22020104 | tf_op jit(solution)/shard_map/hop_left2/ppermute | solution.py:141
  195.1 161.8 %collective-permute-start.8 = (bf16[1024,3584]{1,0:T(8,128)(2,1)}, bf16[1024,3584]{1,0:T(8,128)(2,1)}, u32[]{:S(2)}, u32[]{:S(2)}) collective-permute-start(bf16[1024,3584]{1,0:T(8,128)(2,1)} %collective-permute-done.1.refs_1_), channel_id=1, source_target_pairs={{8,16},{10,18},{12,20},{14,22},{16,24},{18,26},{20,28},{22,30},{9,... | collective-permute-start | bytes 22020104 | tf_op jit(solution)/shard_map/hop_right2/ppermute | solution.py:141
  208.9 7.4 copy-start.20
  214.0 13.0 %copy-start.21 = (bf16[256,3584]{1,0:T(8,128)(2,1)}, bf16[256,3584]{1,0:T(8,128)(2,1)S(1)}, u32[]{:S(2)}) copy-start(bf16[256,3584]{1,0:T(8,128)(2,1)S(1)} %slice.224) | copy-start | bytes 5505028
  216.3 7.9 copy-start.22
  219.9 188.4 %collective-permute-start.13 = (bf16[1024,3584]{1,0:T(8,128)(2,1)}, bf16[1024,3584]{1,0:T(8,128)(2,1)}, u32[]{:S(2)}, u32[]{:S(2)}) collective-permute-start(bf16[1024,3584]{1,0:T(8,128)(2,1)} %pad_maximum_fusion.1), channel_id=1, source_target_pairs={{0,8},{2,10},{4,12},{6,14},{24,16},{26,18},{28,20},{30,22},{1,9},{... | collective-permute-start | bytes 22020104 | tf_op jit(solution)/shard_map/hop_edge/ppermute | solution.py:141
  227.0 111.3 %copy-start.6 = (bf16[512,3584]{1,0:T(8,128)(2,1)S(1)}, bf16[512,3584]{1,0:T(8,128)(2,1)}, u32[]{:S(2)}) copy-start(bf16[512,3584]{1,0:T(8,128)(2,1)} %copy-done.4) | copy-start | bytes 11010052
  343.8 80.7 %collective-permute-start.6 = (bf16[1024,3584]{1,0:T(8,128)(2,1)}, bf16[1024,3584]{1,0:T(8,128)(2,1)}, u32[]{:S(2)}, u32[]{:S(2)}) collective-permute-start(bf16[1024,3584]{1,0:T(8,128)(2,1)} %pad_maximum_fusion), channel_id=1, source_target_pairs={{0,2},{2,0},{4,6},{6,4},{8,10},{10,8},{12,14},{14,12},{16,18},{18,... | collective-permute-start | bytes 22020104 | tf_op jit(solution)/shard_map/hop_cores_two/ppermute | solution.py:141
  357.0 9.1 %copy-start.19 = (bf16[256,3584]{1,0:T(8,128)(2,1)S(1)}, bf16[256,3584]{1,0:T(8,128)(2,1)}, u32[]{:S(2)}) copy-start(bf16[256,3584]{1,0:T(8,128)(2,1)} %copy-done.18) | copy-start | bytes 5505028
  357.0 175.5 %collective-permute-start.11 = (bf16[512,3584]{1,0:T(8,128)(2,1)}, bf16[512,3584]{1,0:T(8,128)(2,1)}, u32[]{:S(2)}, u32[]{:S(2)}) collective-permute-start(bf16[512,3584]{1,0:T(8,128)(2,1)} %shard_map.73), channel_id=1, source_target_pairs={{0,16},{2,18},{4,20},{6,22},{8,24},{10,26},{12,28},{14,30},{16,0},... | collective-permute-start | bytes 11010056 | tf_op jit(solution)/shard_map/hop_out2/ppermute | solution.py:141
  381.7 24.0 %collective-permute-start.10 = (bf16[1024,512]{1,0:T(8,128)(2,1)S(1)}, bf16[1024,512]{1,0:T(8,128)(2,1)S(1)}, u32[]{:S(2)}, u32[]{:S(2)}) collective-permute-start(bf16[1024,512]{1,0:T(8,128)(2,1)S(1)} %constant_dynamic-slice_fusion.2), channel_id=1, source_target_pairs={{0,1},{1,0},{2,3},{3,2},{4,5},{5,4},{6,7},{7,6},{8,9},{9,8},{10,11... | collective-permute-start | bytes 3145736 | tf_op jit(solution)/shard_map/terms_far/ppermute | solution.py:145
  383.3 22.4 %copy-start.31 = (bf16[1024,1024]{1,0:T(8,128)(2,1)S(1)}, bf16[1024,1024]{1,0:T(8,128)(2,1)}, u32[]{:S(2)}) copy-start(bf16[1024,1024]{1,0:T(8,128)(2,1)} %convolution_convert_fusion.1) | copy-start | bytes 6291460
  383.3 158.8 %collective-permute-start.19 = (bf16[1024,3584]{1,0:T(8,128)(2,1)}, bf16[1024,3584]{1,0:T(8,128)(2,1)}, u32[]{:S(2)}, u32[]{:S(2)}) collective-permute-start(bf16[1024,3584]{1,0:T(8,128)(2,1)} %shard_map.75), channel_id=1, source_target_pairs={{0,4},{2,6},{4,0},{6,2},{8,12},{10,14},{12,8},{14,10},{16,20},{18,... | collective-permute-start | bytes 22020104 | tf_op jit(solution)/shard_map/hop_chips_three/ppermute | solution.py:141
  423.0 39.5 %collective-permute-start.14 = (bf16[1024,512]{1,0:T(8,128)(2,1)}, bf16[1024,512]{1,0:T(8,128)(2,1)S(1)}, u32[]{:S(2)}, u32[]{:S(2)}) collective-permute-start(bf16[1024,512]{1,0:T(8,128)(2,1)} %constant_dynamic-slice_fusion.1), channel_id=1, source_target_pairs={{0,1},{1,0},{2,3},{3,2},{4,5},{5,4},{6,7},{7,6},{8,9},{9,8},{10,11... | collective-permute-start | bytes 3145736 | tf_op jit(solution)/shard_map/terms_edge/ppermute | solution.py:145
  442.8 18.2 %copy-start.28 = (bf16[1024,1024]{1,0:T(8,128)(2,1)}, bf16[1024,1024]{1,0:T(8,128)(2,1)S(1)}, u32[]{:S(2)}) copy-start(bf16[1024,1024]{1,0:T(8,128)(2,1)S(1)} %fusion.47) | copy-start | bytes 6291460
  444.0 29.2 %collective-permute-start.9 = (bf16[1024,512]{1,0:T(8,128)(2,1)}, bf16[1024,512]{1,0:T(8,128)(2,1)}, u32[]{:S(2)}, u32[]{:S(2)}) collective-permute-start(bf16[1024,512]{1,0:T(8,128)(2,1)} %constant_dynamic-slice_fusion.3), channel_id=1, source_target_pairs={{0,1},{1,0},{2,3},{3,2},{4,5},{5,4},{6,7},{7,6},{8,9},{9,8},{10,11... | collective-permute-start | bytes 3145736 | tf_op jit(solution)/shard_map/terms_mid/ppermute | solution.py:145
  460.9 52.9 %collective-permute-start.12 = (bf16[1024,1024]{1,0:T(8,128)(2,1)}, bf16[1024,1024]{1,0:T(8,128)(2,1)}, u32[]{:S(2)}, u32[]{:S(2)}) collective-permute-start(bf16[1024,1024]{1,0:T(8,128)(2,1)} %fusion.42), channel_id=1, source_target_pairs={{0,1},{1,0},{2,3},{3,2},{4,5},{5,4},{6,7},{7,6},{8,9},{9,8},{10,11... | collective-permute-start | bytes 6291464 | tf_op jit(solution)/shard_map/terms_near/ppermute | solution.py:145
  469.7 62.8 %collective-permute-start.15 = (bf16[512,512]{1,0:T(8,128)(2,1)S(1)}, bf16[512,512]{1,0:T(8,128)(2,1)S(1)}, u32[]{:S(2)}, u32[]{:S(2)}) collective-permute-start(bf16[512,512]{1,0:T(8,128)(2,1)S(1)} %fusion.53), channel_id=1, source_target_pairs={{8,24},{10,26},{12,28},{14,30},{16,0},{18,2},{20,4},{22,6},{9,25},... | collective-permute-start | bytes 1572872 | tf_op jit(solution)/shard_map/hop_hidden3/ppermute | solution.py:141
  484.7 29.1 %copy-start.32 = (bf16[1024,1024]{1,0:T(8,128)(2,1)S(1)}, bf16[1024,1024]{1,0:T(8,128)(2,1)}, u32[]{:S(2)}) copy-start(bf16[1024,1024]{1,0:T(8,128)(2,1)} %fusion.42) | copy-start | bytes 6291460
  533.3 8.8 %copy-start.10 = (bf16[512,512]{1,0:T(8,128)(2,1)}, bf16[512,512]{1,0:T(8,128)(2,1)S(1)}, u32[]{:S(2)}) copy-start(bf16[512,512]{1,0:T(8,128)(2,1)S(1)} %get-tuple-element.20.refs_2_) | copy-start | bytes 1572868
  533.3 8.8 %copy-start.12 = (bf16[512,512]{1,0:T(8,128)(2,1)}, bf16[512,512]{1,0:T(8,128)(2,1)S(1)}, u32[]{:S(2)}) copy-start(bf16[512,512]{1,0:T(8,128)(2,1)S(1)} %get-tuple-element.21.refs_3_) | copy-start | bytes 1572868
  546.2 6.8 copy-start.2
  553.0 11.9 %collective-permute-start.20 = (bf16[1024,3584]{1,0:T(8,128)(2,1)}, bf16[1024,3584]{1,0:T(8,128)(2,1)S(1)}, u32[]{:S(2)}, u32[]{:S(2)}) collective-permute-start(bf16[1024,3584]{1,0:T(8,128)(2,1)} %pad_maximum_fusion.2), channel_id=1, source_target_pairs={{0,2},{2,0},{4,6},{6,4},{8,10},{10,8},{12,14},{14,12},{16,18},{18,... | collective-permute-start | bytes 22020104 | tf_op jit(solution)/shard_map/hop_cores_three/ppermute | solution.py:141
  558.6 215.3 %collective-permute-start.18 = (bf16[512,3584]{1,0:T(8,128)(2,1)}, bf16[512,3584]{1,0:T(8,128)(2,1)}, u32[]{:S(2)}, u32[]{:S(2)}) collective-permute-start(bf16[512,3584]{1,0:T(8,128)(2,1)} %get-tuple-element.22.refs_1_), channel_id=1, source_target_pairs={{0,24},{2,26},{4,28},{6,30},{8,16},{10,18},{12,20},{14,22},{16,8},... | collective-permute-start | bytes 11010056 | tf_op jit(solution)/shard_map/hop_out3/ppermute | solution.py:141
  583.2 5.6 copy-start.24
  583.2 171.6 %collective-permute-start.21 = (bf16[1024,1024]{1,0:T(8,128)(2,1)}, bf16[1024,1024]{1,0:T(8,128)(2,1)}, u32[]{:S(2)}, u32[]{:S(2)}) collective-permute-start(bf16[1024,1024]{1,0:T(8,128)(2,1)} %fusion.39), channel_id=1, source_target_pairs={{0,1},{1,0},{2,3},{3,2},{4,5},{5,4},{6,7},{7,6},{8,9},{9,8},{10,11... | collective-permute-start | bytes 6291464 | tf_op jit(solution)/shard_map/terms_own/ppermute | solution.py:145
  588.8 9.2 %copy-start.13 = (bf16[512,512]{1,0:T(8,128)(2,1)S(1)}, bf16[512,512]{1,0:T(8,128)(2,1)}, u32[]{:S(2)}) copy-start(bf16[512,512]{1,0:T(8,128)(2,1)} %copy-done.12) | copy-start | bytes 1572868
  588.8 11.2 %copy-start.11 = (bf16[512,512]{1,0:T(8,128)(2,1)S(1)}, bf16[512,512]{1,0:T(8,128)(2,1)}, u32[]{:S(2)}) copy-start(bf16[512,512]{1,0:T(8,128)(2,1)} %copy-done.10) | copy-start | bytes 1572868
  588.8 11.2 %copy-start.35 = (s32[16,2,8]{0,2,1:T(8,128)S(1)}, s32[16,2,8]{0,2,1:T(8,128)}, u32[]{:S(2)}) copy-start(s32[16,2,8]{0,2,1:T(8,128)} %param.10) | copy-start | bytes 3076
  588.8 142.0 %copy-start.16 = (bf16[512,512]{1,0:T(8,128)(2,1)S(1)}, bf16[512,512]{1,0:T(8,128)(2,1)}, u32[]{:S(2)}) copy-start(bf16[512,512]{1,0:T(8,128)(2,1)} %copy-done.15) | copy-start | bytes 1572868
  596.6 203.7 %collective-permute-start.23 = (bf16[512,4608]{1,0:T(8,128)(2,1)}, bf16[512,4608]{1,0:T(8,128)(2,1)}, u32[]{:S(2)}, u32[]{:S(2)}) collective-permute-start(bf16[512,4608]{1,0:T(8,128)(2,1)} %pad_maximum_fusion.4), channel_id=1, source_target_pairs={{0,8},{2,10},{4,12},{6,14},{8,0},{10,2},{12,4},{14,6},{16,24},{18,... | collective-permute-start | bytes 14155784 | tf_op jit(solution)/shard_map/hop_out1/ppermute | solution.py:141
  598.0 132.8 %collective-permute-start.17 = (bf16[512,512]{1,0:T(8,128)(2,1)S(1)}, bf16[512,512]{1,0:T(8,128)(2,1)S(1)}, u32[]{:S(2)}, u32[]{:S(2)}) collective-permute-start(bf16[512,512]{1,0:T(8,128)(2,1)S(1)} %copy-done.13), channel_id=1, source_target_pairs={{8,16},{10,18},{12,20},{14,22},{16,8},{18,10},{20,12},{22,14},{9,1... | collective-permute-start | bytes 1572872 | tf_op jit(solution)/shard_map/hop_hidden3/ppermute | solution.py:141
  600.0 154.8 %collective-permute-start.16 = (bf16[512,512]{1,0:T(8,128)(2,1)S(1)}, bf16[512,512]{1,0:T(8,128)(2,1)S(1)}, u32[]{:S(2)}, u32[]{:S(2)}) collective-permute-start(bf16[512,512]{1,0:T(8,128)(2,1)S(1)} %copy-done.11), channel_id=1, source_target_pairs={{0,16},{2,18},{4,20},{6,22},{8,24},{10,26},{12,28},{14,30},{16,0},... | collective-permute-start | bytes 1572872 | tf_op jit(solution)/shard_map/hop_hidden2/ppermute | solution.py:141
  774.5 24.9 %collective-permute-start.22 = (bf16[1024,512]{0,1:T(8,128)(2,1)S(1)}, bf16[1024,512]{0,1:T(8,128)(2,1)S(1)}, u32[]{:S(2)}, u32[]{:S(2)}) collective-permute-start(bf16[1024,512]{0,1:T(8,128)(2,1)S(1)} %copy.40), channel_id=1, source_target_pairs={{0,1},{1,0},{2,3},{3,2},{4,5},{5,4},{6,7},{7,6},{8,9},{9,8},{10,11... | collective-permute-start | bytes 3145736 | tf_op jit(solution)/shard_map/terms_rows/ppermute | solution.py:145
  789.7 9.8 %copy-start.17 = (f32[1024,1024]{0,1:T(8,128)S(1)}, f32[1024,1024]{0,1:T(8,128)}, u32[]{:S(2)}) copy-start(f32[1024,1024]{0,1:T(8,128)} %copy.42) | copy-start | bytes 12582916
  (12 other events, 31.1 us)

commit v4 on v3

--- a/solution.py
+++ b/solution.py
@@ -99,27 +99,30 @@
     )(*values, *landed)
 
 
-def add_product_kernel(left, right, total, result):
-    product = jnp.dot(left[...], right[...], preferred_element_type=jnp.float32)
+def add_product_kernel(left, right_a, right_b, total, result):
+    depth = right_a.shape[0]
+    product = jnp.dot(left[:, :depth], right_a[...], preferred_element_type=jnp.float32)
+    product += jnp.dot(left[:, depth:], right_b[...], preferred_element_type=jnp.float32)
     result[...] = (total[...] + product).astype(result.dtype)
 
 
-def add_product(left, right, total):
+def add_product(left, right_a, right_b, total):
     rows, depth = left.shape
-    width = right.shape[1]
+    width = right_a.shape[1]
     block = next(n for n in (512, 384, 256, 128) if width % n == 0)
     return pl.pallas_call(
         add_product_kernel,
         grid=(width // block,),
         in_specs=[
             pl.BlockSpec((rows, depth), lambda n: (0, 0)),
-            pl.BlockSpec((depth, block), lambda n: (0, n)),
+            pl.BlockSpec((depth // 2, block), lambda n: (0, n)),
+            pl.BlockSpec((depth // 2, block), lambda n: (0, n)),
             pl.BlockSpec((rows, block), lambda n: (0, n)),
         ],
         out_specs=pl.BlockSpec((rows, block), lambda n: (0, n)),
         out_shape=jax.ShapeDtypeStruct((rows, width), left.dtype),
         compiler_params=pltpu.CompilerParams(vmem_limit_bytes=24 << 20),
-    )(left, right, total)
+    )(left, right_a, right_b, total)
 
 
 def on_device(tokens, proj_in, proj_out, expert_list, block_pattern, route_weight):
@@ -239,7 +242,7 @@
     with jax.named_scope("hop_left1"):
         left1 = over_z(tokens, [(3, 2), (2, 1), (1, 0)])
     across1 = over_chips("one", first, [])
-    across1 = list(hold_until(across1, [right1, left1] + second + third))
+    across1 = list(hold_until(across1, [right1, left1] + first[-2:] + second + third))
 
     with jax.named_scope("hop_right2"):
         right2 = over_z(right1, [(1, 2), (2, 3)])
@@ -308,7 +311,7 @@
     crossed = jnp.concatenate([hidden2, hidden3], axis=0)
     (crossed,) = hold_until([crossed], [out3, own_hidden])
     crossed = weighted([all_rows("rows", crossed)]).T
-    return add_product(crossed, jnp.concatenate([out2, out3], axis=0), total)
+    return add_product(crossed, out2, out3, total)
 
 
 def solution(mesh):

time: 838 us -> 829 us (0.989)
  waiting for transfers between devices: 464 us -> 453 us
    ppermute x18, waiting for transfers between devices: 410 us -> 397 us  [over_z(): return lax.ppermute(value, 'dp', pairs)]
  transfers between devices with their start and end apart: 24 -> 24, of which waited for: 13 -> 11; matrix products, arithmetic and copies ran while one was open for 28% -> 28% of each run, Pallas kernels for 4% -> 4%
where the time goes in v4:
time: 829 us; the launch traced here: 823 us
  waiting for transfers between devices  453 us (55%)
  local copies, waits for them, and re-layouts  135 us (16%)
  matrix products  81.1 us (10%)
  other arithmetic  56.1 us (7%)
  starting transfers between devices  48.5 us (6%)
  Pallas kernels  48 us (6%)
    ppermute x18, waiting for transfers between devices, over_z(): return lax.ppermute(value, 'dp', pairs)  397 us
    dot_general x5, matrix products, terms_of(): lax.dot_general(weight_in, token_rows, (((1,), (1,)), ((), ())), preferre...  68.9 us
    ppermute x6, waiting for transfers between devices, over_group(): return lax.ppermute(value, 'group', pairs)  56.2 us
    slice x17, local copies, waits for them, and re-layouts, joined(): return jnp.concatenate([v[low:high] for v in pieces], axis=0)  43.9 us
    ppermute x18, starting transfers between devices, over_z(): return lax.ppermute(value, 'dp', pairs)  42.3 us
    pallas_call x6, Pallas kernels, gather_experts(): pl.pallas_call(functools.partial(gather_kernel, counts), out_shape=[jax.S...  36 us
    slice x4, local copies, waits for them, and re-layouts, gated(): return (jax.nn.silu(total[:, 0]) * total[:, 1]).astype(jnp.bfloat16)  23.4 us
    reshape x5, local copies, waits for them, and re-layouts, gated(): total = total.reshape(-1, 2, total.shape[1])  20.1 us
  transfers between devices with their start and end apart: 24, of which 11 were waited for; matrix products, arithmetic and copies ran while one was open for 28% of the time, Pallas kernels for 4%

profile of v4, /device:TPU:8, one launch (start us, length us, event | category | flops | bytes accessed | tf_op | source)
XLA Modules:
  0.0 822.9 jit_solution(10011805136295093262)
XLA Ops:
  1.9 6.7 shard_map.65
  10.2 3.5 collective-permute-start.1
  13.6 5.3 collective-permute-start.2
  19.1 4.8 shard_map.67
  27.5 6.2 shard_map.66.refs_5_.refs_0_
  33.8 6.7 shard_map.68.refs_8_.refs_0_
  40.9 5.6 shard_map.69
  50.5 6.0 shard_map.64
  56.5 112.2 %collective-permute-done.refs_0_ = bf16[1024,3584]{1,0:T(8,128)(2,1)} collective-permute-done((bf16[1024,3584]{1,0:T(8,128)(2,1)}, bf16[1024,3584]{1,0:T(8,128)(2,1)}, u32[]{:S(2)}, u32[]{:S(2)}) %collective-permute-start) | collective-permute-done | bytes 7340064 | tf_op jit(solution)/shard_map/hop_chips_one/ppermute | solution.py:144
  171.8 4.1 collective-permute-done.2.refs_2_
  176.6 4.1 slice.215
  182.8 4.7 collective-permute-start.7
  187.5 7.4 collective-permute-start.8
  201.3 3.5 fusion.95
  208.8 3.6 pad_maximum_fusion.1
  219.4 115.1 %collective-permute-done.5.refs_3_.refs_1_ = bf16[1024,3584]{1,0:T(8,128)(2,1)} collective-permute-done((bf16[1024,3584]{1,0:T(8,128)(2,1)}, bf16[1024,3584]{1,0:T(8,128)(2,1)}, u32[]{:S(2)}, u32[]{:S(2)}) %collective-permute-start.5) | collective-permute-done | bytes 7340064 | tf_op jit(solution)/shard_map/hop_chips_two/ppermute | solution.py:144
  334.6 4.2 slice.218
  338.7 5.5 pad_maximum_fusion
  344.2 3.5 pad_maximum_fusion.5.refs_0_
  351.6 6.9 broadcast_select_fusion.1
  358.4 14.4 %convolution_convert_fusion.1 = bf16[1024,1024]{1,0:T(8,128)(2,1)} fusion(bf16[1024,3584]{1,0:T(8,128)(2,1)} %broadcast_select_fusion.1, bf16[256,3584]{1,0:T(8,128)(2,1)} %copy-done.23, bf16[256,3584]{1,0:T(8,128)(2,1)} %copy-done.22, bf16[256,3584]{1,0:T(8,128)(2,1)} %copy-done.21, bf16[256,3584]{1,0:T(8,128)(2,1)S(1)} %copy-done.20), kind=kOutput, calls=%fused_computation.63 | convolution fusion | flops 7546601472 | bytes 16777216 | tf_op jit(solution)/shard_map/dot_general | solution.py:201
  377.2 4.1 fusion.93
  381.3 16.9 %collective-permute-done.10 = bf16[1024,512]{1,0:T(8,128)(2,1)S(1)} collective-permute-done((bf16[1024,512]{1,0:T(8,128)(2,1)S(1)}, bf16[1024,512]{1,0:T(8,128)(2,1)S(1)}, u32[]{:S(2)}, u32[]{:S(2)}) %collective-permute-start.10) | collective-permute-done | bytes 1048608 | tf_op jit(solution)/shard_map/terms_far/ppermute | solution.py:148
  400.9 12.2 %convolution_convert_fusion = bf16[1024,1024]{1,0:T(8,128)(2,1)S(1)} fusion(bf16[1024,3584]{1,0:T(8,128)(2,1)} %collective-permute-done.13, bf16[1024,3584]{1,0:T(8,128)(2,1)} %broadcast_select_fusion.1), kind=kOutput, calls=%fused_computation.62 | convolution fusion | flops 7517241344 | bytes 16777216 | tf_op jit(solution)/shard_map/dot_general | solution.py:201
  417.0 6.3 fusion.94
  423.3 12.0 %fusion.47 = bf16[1024,1024]{1,0:T(8,128)(2,1)S(1)} fusion(bf16[1024,3584]{1,0:T(8,128)(2,1)} %broadcast_select_fusion.1, bf16[1024,3584]{1,0:T(8,128)(2,1)} %collective-permute-done.2.refs_2_, bf16[1024,3584]{1,0:T(8,128)(2,1)} %collective-permute-done.1.refs_1_, pred[]{:T(512)S(6)} %lt.124, pred[]{:T(512)S(6)} %or.3, ...), kind=kOutput, calls=%fused_computation.61 | convolution fusion | flops 7553941504 | bytes 31457282 | tf_op jit(solution)/shard_map/dot_general | solution.py:201
  437.1 16.5 %fusion.42 = bf16[1024,1024]{1,0:T(8,128)(2,1)} fusion(bf16[1024,3584]{1,0:T(8,128)(2,1)} %collective-permute-done.1.refs_1_, bf16[1024,3584]{1,0:T(8,128)(2,1)} %collective-permute-done.2.refs_2_, pred[]{:T(512)S(6)} %lt.124, pred[]{:T(512)S(6)} %or.3, bf16[256,3584]{1,0:T(8,128)(2,1)} %get-tuple-element.59, bf16[256,3584]{1,0:T(8,128)(2,1)} %get-tuple-element.58, ...), kind=kOutput, calls=%fused_computation.60 | convolution fusion | flops 7557611520 | bytes 24117250 | tf_op jit(solution)/shard_map/dot_general | solution.py:201
  463.2 5.3 collective-permute-start.15
  474.8 7.6 fusion.103
  483.1 23.5 %collective-permute-done.12 = bf16[1024,1024]{1,0:T(8,128)(2,1)} collective-permute-done((bf16[1024,1024]{1,0:T(8,128)(2,1)}, bf16[1024,1024]{1,0:T(8,128)(2,1)}, u32[]{:S(2)}, u32[]{:S(2)}) %collective-permute-start.12) | collective-permute-done | bytes 2097184 | tf_op jit(solution)/shard_map/terms_near/ppermute | solution.py:148
  506.5 4.5 convert_add_fusion.1
  511.0 6.0 reshape.28
  517.1 7.1 fusion.97
  526.1 8.6 %collective-permute-done.19.refs_0_ = bf16[1024,3584]{1,0:T(8,128)(2,1)} collective-permute-done((bf16[1024,3584]{1,0:T(8,128)(2,1)}, bf16[1024,3584]{1,0:T(8,128)(2,1)}, u32[]{:S(2)}, u32[]{:S(2)}) %collective-permute-start.19) | collective-permute-done | bytes 7340064 | tf_op jit(solution)/shard_map/hop_chips_three/ppermute | solution.py:144
  534.7 4.1 slice.239
  538.7 6.8 pad_maximum_fusion.2
  562.0 13.8 %fusion.39 = bf16[1024,1024]{1,0:T(8,128)(2,1)} fusion(bf16[1024,3584]{1,0:T(8,128)(2,1)} %param.6, bf16[256,3584]{1,0:T(8,128)(2,1)} %get-tuple-element.55, bf16[256,3584]{1,0:T(8,128)(2,1)S(1)} %get-tuple-element.54, bf16[256,3584]{1,0:T(8,128)(2,1)} %slice.238, bf16[256,3584]{1,0:T(8,128)(2,1)} %slice.196), kind=kOutput, calls=%fused_computation.59 | convolution fusion | flops 7546601472 | bytes 16777216 | tf_op jit(solution)/shard_map/dot_general | solution.py:201
  581.4 7.7 pad_maximum_fusion.3
  594.6 130.1 %collective-permute-done.17 = bf16[512,512]{1,0:T(8,128)(2,1)S(1)} collective-permute-done((bf16[512,512]{1,0:T(8,128)(2,1)S(1)}, bf16[512,512]{1,0:T(8,128)(2,1)S(1)}, u32[]{:S(2)}, u32[]{:S(2)}) %collective-permute-start.17) | collective-permute-done | bytes 524320 | tf_op jit(solution)/shard_map/hop_hidden3/ppermute | solution.py:144
  724.8 23.3 %collective-permute-done.16 = bf16[512,512]{1,0:T(8,128)(2,1)S(1)} collective-permute-done((bf16[512,512]{1,0:T(8,128)(2,1)S(1)}, bf16[512,512]{1,0:T(8,128)(2,1)S(1)}, u32[]{:S(2)}, u32[]{:S(2)}) %collective-permute-start.16) | collective-permute-done | bytes 524320 | tf_op jit(solution)/shard_map/hop_hidden2/ppermute | solution.py:144
  748.2 4.4 convert_add_fusion
  752.7 5.8 reshape.30
  758.5 7.1 fusion.96
  770.5 5.3 copy.42
  776.2 15.8 %collective-permute-done.22 = bf16[1024,512]{0,1:T(8,128)(2,1)S(1)} collective-permute-done((bf16[1024,512]{0,1:T(8,128)(2,1)S(1)}, bf16[1024,512]{0,1:T(8,128)(2,1)S(1)}, u32[]{:S(2)}, u32[]{:S(2)}) %collective-permute-start.22) | collective-permute-done | bytes 1048608 | tf_op jit(solution)/shard_map/terms_rows/ppermute | solution.py:148
  794.3 4.1 slice_dynamic-update-slice_fusion
  798.4 12.1 %fusion.31.total = f32[1024,3584]{1,0:T(8,128)S(1)} fusion(bf16[1024,3584]{1,0:T(8,128)(2,1)} %slice_dynamic-update-slice_fusion, f32[1024,1024]{1,0:T(8,128)} %bitcast.71, bf16[512,1024]{1,0:T(8,128)(2,1)S(1)} %slice.247, bf16[512,1024]{1,0:T(8,128)(2,1)S(1)} %fusion.36.refs_2_), kind=kOutput, calls=%fused_computation.44 | convolution fusion | flops 7522484224 | bytes 28311552 | tf_op jit(solution)/shard_map/dot_general | solution.py:304
  810.6 12.1 %shard_map.78 = bf16[1024,3584]{1,0:T(8,128)(2,1)} custom-call(bf16[1024,1024]{1,0:T(8,128)(2,1)S(1)} %fusion.30.left, bf16[512,3584]{1,0:T(8,128)(2,1)} %collective-permute-done.11.refs_3_.right_a, bf16[512,3584]{1,0:T(8,128)(2,1)} %collective-permute-done.18.refs_1_.right_b, f32[1024,3584]{1,0:T(8,128)S(1)} %fusion.31.total), custom_call_target="tpu_custom_call" | custom-call | tf_op jit(solution)/shard_map/pallas_call | solution.py:113
  (166 shorter events, 104.8 us)
Async XLA Ops:
  8.6 160.1 %collective-permute-start = (bf16[1024,3584]{1,0:T(8,128)(2,1)}, bf16[1024,3584]{1,0:T(8,128)(2,1)}, u32[]{:S(2)}, u32[]{:S(2)}) collective-permute-start(bf16[1024,3584]{1,0:T(8,128)(2,1)} %shard_map.65), channel_id=1, source_target_pairs={{0,4},{2,6},{4,0},{6,2},{8,12},{10,14},{12,8},{14,10},{16,20},{18,... | collective-permute-start | bytes 22020104 | tf_op jit(solution)/shard_map/hop_chips_one/ppermute | solution.py:144
  10.2 161.6 %collective-permute-start.1 = (bf16[1024,3584]{1,0:T(8,128)(2,1)}, bf16[1024,3584]{1,0:T(8,128)(2,1)}, u32[]{:S(2)}, u32[]{:S(2)}) collective-permute-start(bf16[1024,3584]{1,0:T(8,128)(2,1)} %param.6), channel_id=1, source_target_pairs={{0,8},{2,10},{4,12},{6,14},{8,16},{10,18},{12,20},{14,22},{16,24},... | collective-permute-start | bytes 22020104 | tf_op jit(solution)/shard_map/hop_right1/ppermute | solution.py:144
  13.6 162.3 %collective-permute-start.2 = (bf16[1024,3584]{1,0:T(8,128)(2,1)}, bf16[1024,3584]{1,0:T(8,128)(2,1)}, u32[]{:S(2)}, u32[]{:S(2)}) collective-permute-start(bf16[1024,3584]{1,0:T(8,128)(2,1)} %param.6), channel_id=1, source_target_pairs={{24,16},{26,18},{28,20},{30,22},{16,8},{18,10},{20,12},{22,14},{8,... | collective-permute-start | bytes 22020104 | tf_op jit(solution)/shard_map/hop_left1/ppermute | solution.py:144
  33.8 6.7 copy-start.34
  50.4 125.5 %copy-start.1 = (bf16[512,3584]{1,0:T(8,128)(2,1)S(1)}, bf16[512,3584]{1,0:T(8,128)(2,1)}, u32[]{:S(2)}) copy-start(bf16[512,3584]{1,0:T(8,128)(2,1)} %copy-done) | copy-start | bytes 11010052
  50.4 125.5 %copy-start.4 = (bf16[512,3584]{1,0:T(8,128)(2,1)S(1)}, bf16[512,3584]{1,0:T(8,128)(2,1)}, u32[]{:S(2)}) copy-start(bf16[512,3584]{1,0:T(8,128)(2,1)} %copy-done.3) | copy-start | bytes 11010052
  50.4 125.5 %copy-start.6 = (bf16[512,3584]{1,0:T(8,128)(2,1)S(1)}, bf16[512,3584]{1,0:T(8,128)(2,1)}, u32[]{:S(2)}) copy-start(bf16[512,3584]{1,0:T(8,128)(2,1)} %copy-done.5) | copy-start | bytes 11010052
  50.4 125.5 %copy-start.10 = (bf16[512,3584]{1,0:T(8,128)(2,1)S(1)}, bf16[512,3584]{1,0:T(8,128)(2,1)}, u32[]{:S(2)}) copy-start(bf16[512,3584]{1,0:T(8,128)(2,1)} %copy-done.9) | copy-start | bytes 11010052
  56.5 119.5 %copy-start.8 = (bf16[512,3584]{1,0:T(8,128)(2,1)}, bf16[512,3584]{1,0:T(8,128)(2,1)S(1)}, u32[]{:S(2)}) copy-start(bf16[512,3584]{1,0:T(8,128)(2,1)S(1)} %get-tuple-element.14.refs_3_) | copy-start | bytes 11010052
  176.0 158.6 %collective-permute-start.5 = (bf16[1024,3584]{1,0:T(8,128)(2,1)}, bf16[1024,3584]{1,0:T(8,128)(2,1)}, u32[]{:S(2)}, u32[]{:S(2)}) collective-permute-start(bf16[1024,3584]{1,0:T(8,128)(2,1)} %shard_map.72), channel_id=1, source_target_pairs={{0,4},{2,6},{4,0},{6,2},{8,12},{10,14},{12,8},{14,10},{16,20},{18,... | collective-permute-start | bytes 22020104 | tf_op jit(solution)/shard_map/hop_chips_two/ppermute | solution.py:144
  176.6 28.2 %collective-permute-start.3 = (bf16[512,3584]{1,0:T(8,128)(2,1)}, bf16[512,3584]{1,0:T(8,128)(2,1)}, u32[]{:S(2)}, u32[]{:S(2)}) collective-permute-start(bf16[512,3584]{1,0:T(8,128)(2,1)} %shard_map.71), channel_id=1, source_target_pairs={{0,2},{2,0},{4,6},{6,4},{8,10},{10,8},{12,14},{14,12},{16,18},{18,... | collective-permute-start | bytes 11010056 | tf_op jit(solution)/shard_map/hop_cores_one/ppermute | solution.py:144
  180.7 25.8 %collective-permute-start.4 = (bf16[512,3584]{1,0:T(8,128)(2,1)}, bf16[512,3584]{1,0:T(8,128)(2,1)}, u32[]{:S(2)}, u32[]{:S(2)}) collective-permute-start(bf16[512,3584]{1,0:T(8,128)(2,1)} %slice.215), channel_id=1, source_target_pairs={{0,2},{2,0},{4,6},{6,4},{8,10},{10,8},{12,14},{14,12},{16,18},{18,... | collective-permute-start | bytes 11010056 | tf_op jit(solution)/shard_map/hop_cores_one/ppermute | solution.py:144
  182.8 25.9 %copy-start.19 = (bf16[256,3584]{1,0:T(8,128)(2,1)}, bf16[256,3584]{1,0:T(8,128)(2,1)S(1)}, u32[]{:S(2)}) copy-start(bf16[256,3584]{1,0:T(8,128)(2,1)S(1)} %slice.178) | copy-start | bytes 5505028
  182.8 14.6 %copy-start.11 = (bf16[512,3584]{1,0:T(8,128)(2,1)S(1)}, bf16[512,3584]{1,0:T(8,128)(2,1)}, u32[]{:S(2)}) copy-start(bf16[512,3584]{1,0:T(8,128)(2,1)} %copy-done.9) | copy-start | bytes 11010052
  182.8 166.9 %collective-permute-start.7 = (bf16[1024,3584]{1,0:T(8,128)(2,1)}, bf16[1024,3584]{1,0:T(8,128)(2,1)}, u32[]{:S(2)}, u32[]{:S(2)}) collective-permute-start(bf16[1024,3584]{1,0:T(8,128)(2,1)} %collective-permute-done.2.refs_2_), channel_id=1, source_target_pairs={{16,8},{18,10},{20,12},{22,14},{8,0},{10,2},{12,4},{14,6},{17,9},{... | collective-permute-start | bytes 22020104 | tf_op jit(solution)/shard_map/hop_left2/ppermute | solution.py:144
  187.5 162.3 %collective-permute-start.8 = (bf16[1024,3584]{1,0:T(8,128)(2,1)}, bf16[1024,3584]{1,0:T(8,128)(2,1)}, u32[]{:S(2)}, u32[]{:S(2)}) collective-permute-start(bf16[1024,3584]{1,0:T(8,128)(2,1)} %collective-permute-done.1.refs_1_), channel_id=1, source_target_pairs={{8,16},{10,18},{12,20},{14,22},{16,24},{18,26},{20,28},{22,30},{9,... | collective-permute-start | bytes 22020104 | tf_op jit(solution)/shard_map/hop_right2/ppermute | solution.py:144
  201.3 7.4 copy-start.21
  206.4 13.0 %copy-start.22 = (bf16[256,3584]{1,0:T(8,128)(2,1)}, bf16[256,3584]{1,0:T(8,128)(2,1)S(1)}, u32[]{:S(2)}) copy-start(bf16[256,3584]{1,0:T(8,128)(2,1)S(1)} %slice.224) | copy-start | bytes 5505028
  208.7 7.9 copy-start.23
  212.3 188.6 %collective-permute-start.13 = (bf16[1024,3584]{1,0:T(8,128)(2,1)}, bf16[1024,3584]{1,0:T(8,128)(2,1)}, u32[]{:S(2)}, u32[]{:S(2)}) collective-permute-start(bf16[1024,3584]{1,0:T(8,128)(2,1)} %pad_maximum_fusion.1), channel_id=1, source_target_pairs={{0,8},{2,10},{4,12},{6,14},{24,16},{26,18},{28,20},{30,22},{1,9},{... | collective-permute-start | bytes 22020104 | tf_op jit(solution)/shard_map/hop_edge/ppermute | solution.py:144
  219.4 119.3 %copy-start.7 = (bf16[512,3584]{1,0:T(8,128)(2,1)S(1)}, bf16[512,3584]{1,0:T(8,128)(2,1)}, u32[]{:S(2)}) copy-start(bf16[512,3584]{1,0:T(8,128)(2,1)} %copy-done.5) | copy-start | bytes 11010052
  344.2 72.8 %collective-permute-start.6 = (bf16[1024,3584]{1,0:T(8,128)(2,1)}, bf16[1024,3584]{1,0:T(8,128)(2,1)}, u32[]{:S(2)}, u32[]{:S(2)}) collective-permute-start(bf16[1024,3584]{1,0:T(8,128)(2,1)} %pad_maximum_fusion), channel_id=1, source_target_pairs={{0,2},{2,0},{4,6},{6,4},{8,10},{10,8},{12,14},{14,12},{16,18},{18,... | collective-permute-start | bytes 22020104 | tf_op jit(solution)/shard_map/hop_cores_two/ppermute | solution.py:144
  349.8 8.6 %copy-start.20 = (bf16[256,3584]{1,0:T(8,128)(2,1)S(1)}, bf16[256,3584]{1,0:T(8,128)(2,1)}, u32[]{:S(2)}) copy-start(bf16[256,3584]{1,0:T(8,128)(2,1)} %copy-done.19) | copy-start | bytes 5505028
  349.8 175.4 %collective-permute-start.11 = (bf16[512,3584]{1,0:T(8,128)(2,1)}, bf16[512,3584]{1,0:T(8,128)(2,1)}, u32[]{:S(2)}, u32[]{:S(2)}) collective-permute-start(bf16[512,3584]{1,0:T(8,128)(2,1)} %shard_map.73), channel_id=1, source_target_pairs={{0,16},{2,18},{4,20},{6,22},{8,24},{10,26},{12,28},{14,30},{16,0},... | collective-permute-start | bytes 11010056 | tf_op jit(solution)/shard_map/hop_out2/ppermute | solution.py:144
  374.1 24.1 %collective-permute-start.10 = (bf16[1024,512]{1,0:T(8,128)(2,1)S(1)}, bf16[1024,512]{1,0:T(8,128)(2,1)S(1)}, u32[]{:S(2)}, u32[]{:S(2)}) collective-permute-start(bf16[1024,512]{1,0:T(8,128)(2,1)S(1)} %constant_dynamic-slice_fusion.2), channel_id=1, source_target_pairs={{0,1},{1,0},{2,3},{3,2},{4,5},{5,4},{6,7},{7,6},{8,9},{9,8},{10,11... | collective-permute-start | bytes 3145736 | tf_op jit(solution)/shard_map/terms_far/ppermute | solution.py:148
  375.7 22.6 %copy-start.32 = (bf16[1024,1024]{1,0:T(8,128)(2,1)S(1)}, bf16[1024,1024]{1,0:T(8,128)(2,1)}, u32[]{:S(2)}) copy-start(bf16[1024,1024]{1,0:T(8,128)(2,1)} %convolution_convert_fusion.1) | copy-start | bytes 6291460
  375.7 158.9 %collective-permute-start.19 = (bf16[1024,3584]{1,0:T(8,128)(2,1)}, bf16[1024,3584]{1,0:T(8,128)(2,1)}, u32[]{:S(2)}, u32[]{:S(2)}) collective-permute-start(bf16[1024,3584]{1,0:T(8,128)(2,1)} %shard_map.75), channel_id=1, source_target_pairs={{0,4},{2,6},{4,0},{6,2},{8,12},{10,14},{12,8},{14,10},{16,20},{18,... | collective-permute-start | bytes 22020104 | tf_op jit(solution)/shard_map/hop_chips_three/ppermute | solution.py:144
  415.5 39.6 %collective-permute-start.14 = (bf16[1024,512]{1,0:T(8,128)(2,1)}, bf16[1024,512]{1,0:T(8,128)(2,1)S(1)}, u32[]{:S(2)}, u32[]{:S(2)}) collective-permute-start(bf16[1024,512]{1,0:T(8,128)(2,1)} %constant_dynamic-slice_fusion.1), channel_id=1, source_target_pairs={{0,1},{1,0},{2,3},{3,2},{4,5},{5,4},{6,7},{7,6},{8,9},{9,8},{10,11... | collective-permute-start | bytes 3145736 | tf_op jit(solution)/shard_map/terms_edge/ppermute | solution.py:148
  435.3 18.3 %copy-start.29 = (bf16[1024,1024]{1,0:T(8,128)(2,1)}, bf16[1024,1024]{1,0:T(8,128)(2,1)S(1)}, u32[]{:S(2)}) copy-start(bf16[1024,1024]{1,0:T(8,128)(2,1)S(1)} %fusion.47) | copy-start | bytes 6291460
  436.6 31.9 %collective-permute-start.9 = (bf16[1024,512]{1,0:T(8,128)(2,1)}, bf16[1024,512]{1,0:T(8,128)(2,1)}, u32[]{:S(2)}, u32[]{:S(2)}) collective-permute-start(bf16[1024,512]{1,0:T(8,128)(2,1)} %constant_dynamic-slice_fusion.3), channel_id=1, source_target_pairs={{0,1},{1,0},{2,3},{3,2},{4,5},{5,4},{6,7},{7,6},{8,9},{9,8},{10,11... | collective-permute-start | bytes 3145736 | tf_op jit(solution)/shard_map/terms_mid/ppermute | solution.py:148
  453.6 52.9 %collective-permute-start.12 = (bf16[1024,1024]{1,0:T(8,128)(2,1)}, bf16[1024,1024]{1,0:T(8,128)(2,1)}, u32[]{:S(2)}, u32[]{:S(2)}) collective-permute-start(bf16[1024,1024]{1,0:T(8,128)(2,1)} %fusion.42), channel_id=1, source_target_pairs={{0,1},{1,0},{2,3},{3,2},{4,5},{5,4},{6,7},{7,6},{8,9},{9,8},{10,11... | collective-permute-start | bytes 6291464 | tf_op jit(solution)/shard_map/terms_near/ppermute | solution.py:148
  460.4 8.0 copy-start.30
  463.2 62.1 %collective-permute-start.15 = (bf16[512,512]{1,0:T(8,128)(2,1)}, bf16[512,512]{1,0:T(8,128)(2,1)S(1)}, u32[]{:S(2)}, u32[]{:S(2)}) collective-permute-start(bf16[512,512]{1,0:T(8,128)(2,1)} %fusion.53), channel_id=1, source_target_pairs={{8,24},{10,26},{12,28},{14,30},{16,0},{18,2},{20,4},{22,6},{9,25},... | collective-permute-start | bytes 1572872 | tf_op jit(solution)/shard_map/hop_hidden3/ppermute | solution.py:144
  482.5 24.1 %copy-start.33 = (bf16[1024,1024]{1,0:T(8,128)(2,1)S(1)}, bf16[1024,1024]{1,0:T(8,128)(2,1)}, u32[]{:S(2)}) copy-start(bf16[1024,1024]{1,0:T(8,128)(2,1)} %fusion.42) | copy-start | bytes 6291460
  526.1 8.6 %copy-start.12 = (bf16[512,512]{1,0:T(8,128)(2,1)}, bf16[512,512]{1,0:T(8,128)(2,1)S(1)}, u32[]{:S(2)}) copy-start(bf16[512,512]{1,0:T(8,128)(2,1)S(1)} %get-tuple-element.20.refs_2_) | copy-start | bytes 1572868
  526.1 8.6 %copy-start.14 = (bf16[512,512]{1,0:T(8,128)(2,1)}, bf16[512,512]{1,0:T(8,128)(2,1)S(1)}, u32[]{:S(2)}) copy-start(bf16[512,512]{1,0:T(8,128)(2,1)S(1)} %get-tuple-element.21.refs_3_) | copy-start | bytes 1572868
  538.7 6.8 copy-start.2
  545.5 11.9 %collective-permute-start.20 = (bf16[1024,3584]{1,0:T(8,128)(2,1)}, bf16[1024,3584]{1,0:T(8,128)(2,1)S(1)}, u32[]{:S(2)}, u32[]{:S(2)}) collective-permute-start(bf16[1024,3584]{1,0:T(8,128)(2,1)} %pad_maximum_fusion.2), channel_id=1, source_target_pairs={{0,2},{2,0},{4,6},{6,4},{8,10},{10,8},{12,14},{14,12},{16,18},{18,... | collective-permute-start | bytes 22020104 | tf_op jit(solution)/shard_map/hop_cores_three/ppermute | solution.py:144
  551.2 215.5 %collective-permute-start.18 = (bf16[512,3584]{1,0:T(8,128)(2,1)}, bf16[512,3584]{1,0:T(8,128)(2,1)}, u32[]{:S(2)}, u32[]{:S(2)}) collective-permute-start(bf16[512,3584]{1,0:T(8,128)(2,1)} %get-tuple-element.22.refs_1_), channel_id=1, source_target_pairs={{0,24},{2,26},{4,28},{6,30},{8,16},{10,18},{12,20},{14,22},{16,8},... | collective-permute-start | bytes 11010056 | tf_op jit(solution)/shard_map/hop_out3/ppermute | solution.py:144
  575.8 172.4 %collective-permute-start.21 = (bf16[1024,1024]{1,0:T(8,128)(2,1)}, bf16[1024,1024]{1,0:T(8,128)(2,1)S(1)}, u32[]{:S(2)}, u32[]{:S(2)}) collective-permute-start(bf16[1024,1024]{1,0:T(8,128)(2,1)} %fusion.39), channel_id=1, source_target_pairs={{0,1},{1,0},{2,3},{3,2},{4,5},{5,4},{6,7},{7,6},{8,9},{9,8},{10,11... | collective-permute-start | bytes 6291464 | tf_op jit(solution)/shard_map/terms_own/ppermute | solution.py:148
  581.4 10.0 %copy-start.15 = (bf16[512,512]{1,0:T(8,128)(2,1)S(1)}, bf16[512,512]{1,0:T(8,128)(2,1)}, u32[]{:S(2)}) copy-start(bf16[512,512]{1,0:T(8,128)(2,1)} %copy-done.14) | copy-start | bytes 1572868
  581.4 12.9 %copy-start.13 = (bf16[512,512]{1,0:T(8,128)(2,1)S(1)}, bf16[512,512]{1,0:T(8,128)(2,1)}, u32[]{:S(2)}) copy-start(bf16[512,512]{1,0:T(8,128)(2,1)} %copy-done.12) | copy-start | bytes 1572868
  581.4 143.4 %copy-start.17 = (bf16[512,512]{1,0:T(8,128)(2,1)S(1)}, bf16[512,512]{1,0:T(8,128)(2,1)}, u32[]{:S(2)}) copy-start(bf16[512,512]{1,0:T(8,128)(2,1)} %copy-done.16) | copy-start | bytes 1572868
  589.1 203.9 %collective-permute-start.23 = (bf16[512,4608]{1,0:T(8,128)(2,1)}, bf16[512,4608]{1,0:T(8,128)(2,1)}, u32[]{:S(2)}, u32[]{:S(2)}) collective-permute-start(bf16[512,4608]{1,0:T(8,128)(2,1)} %pad_maximum_fusion.3), channel_id=1, source_target_pairs={{0,8},{2,10},{4,12},{6,14},{8,0},{10,2},{12,4},{14,6},{16,24},{18,... | collective-permute-start | bytes 14155784 | tf_op jit(solution)/shard_map/hop_out1/ppermute | solution.py:144
  591.3 133.4 %collective-permute-start.17 = (bf16[512,512]{1,0:T(8,128)(2,1)S(1)}, bf16[512,512]{1,0:T(8,128)(2,1)S(1)}, u32[]{:S(2)}, u32[]{:S(2)}) collective-permute-start(bf16[512,512]{1,0:T(8,128)(2,1)S(1)} %copy-done.15), channel_id=1, source_target_pairs={{8,16},{10,18},{12,20},{14,22},{16,8},{18,10},{20,12},{22,14},{9,1... | collective-permute-start | bytes 1572872 | tf_op jit(solution)/shard_map/hop_hidden3/ppermute | solution.py:144
  594.3 153.8 %collective-permute-start.16 = (bf16[512,512]{1,0:T(8,128)(2,1)S(1)}, bf16[512,512]{1,0:T(8,128)(2,1)S(1)}, u32[]{:S(2)}, u32[]{:S(2)}) collective-permute-start(bf16[512,512]{1,0:T(8,128)(2,1)S(1)} %copy-done.13), channel_id=1, source_target_pairs={{0,16},{2,18},{4,20},{6,22},{8,24},{10,26},{12,28},{14,30},{16,0},... | collective-permute-start | bytes 1572872 | tf_op jit(solution)/shard_map/hop_hidden2/ppermute | solution.py:144
  767.2 24.9 %collective-permute-start.22 = (bf16[1024,512]{0,1:T(8,128)(2,1)S(1)}, bf16[1024,512]{0,1:T(8,128)(2,1)S(1)}, u32[]{:S(2)}, u32[]{:S(2)}) collective-permute-start(bf16[1024,512]{0,1:T(8,128)(2,1)S(1)} %copy.40), channel_id=1, source_target_pairs={{0,1},{1,0},{2,3},{3,2},{4,5},{5,4},{6,7},{7,6},{8,9},{9,8},{10,11... | collective-permute-start | bytes 3145736 | tf_op jit(solution)/shard_map/terms_rows/ppermute | solution.py:148
  775.9 16.3 %copy-start.18 = (f32[1024,1024]{0,1:T(8,128)S(1)}, f32[1024,1024]{0,1:T(8,128)}, u32[]{:S(2)}) copy-start(f32[1024,1024]{0,1:T(8,128)} %copy.42) | copy-start | bytes 12582916
  (13 other events, 31.3 us)

commit v5 on v4

--- a/solution.py
+++ b/solution.py
@@ -256,7 +256,7 @@
     with jax.named_scope("hop_edge"):
         edge_in = over_z(far_in, [(0, 1), (3, 2)])
 
-    (out2,) = hold_until([out2], [right2, left2] + across2)
+    out2, *across2 = hold_until([out2] + across2, [right2, left2])
     with jax.named_scope("hop_out2"):
         out2 = over_z(out2, [(a, a ^ 2) for a in range(SLABS)])
     across3 = over_chips("three", third, across2 + [right2, left2])

time: 829 us -> 868 us (1.047)
  waiting for transfers between devices: 453 us -> 483 us
  local copies, waits for them, and re-layouts: 135 us -> 159 us
  starting transfers between devices: 48.5 us -> 36.9 us
    unnamed x76 -> x108, local copies, waits for them, and re-layouts: 15 us -> 44.1 us
    ppermute x18, waiting for transfers between devices: 397 us -> 420 us  [over_z(): return lax.ppermute(value, 'dp', pairs)]
    ppermute x18, starting transfers between devices: 42.3 us -> 30.8 us  [over_z(): return lax.ppermute(value, 'dp', pairs)]
  transfers between devices with their start and end apart: 24 -> 24, of which waited for: 11 -> 14; matrix products, arithmetic and copies ran while one was open for 28% -> 26% of each run, Pallas kernels for 4% -> 3%
where the time goes in v5:
time: 868 us; the launch traced here: 862 us
  waiting for transfers between devices  483 us (56%)
  local copies, waits for them, and re-layouts  159 us (18%)
  matrix products  79.8 us (9%)
  other arithmetic  55.7 us (6%)
  Pallas kernels  46.5 us (5%)
  starting transfers between devices  36.9 us (4%)
    ppermute x18, waiting for transfers between devices, over_z(): return lax.ppermute(value, 'dp', pairs)  420 us
    dot_general x5, matrix products, terms_of(): lax.dot_general(weight_in, token_rows, (((1,), (1,)), ((), ())), preferre...  68.9 us
    ppermute x6, waiting for transfers between devices, over_group(): return lax.ppermute(value, 'group', pairs)  62.7 us
    unnamed x108, local copies, waits for them, and re-layouts  44.1 us
    slice x17, local copies, waits for them, and re-layouts, joined(): return jnp.concatenate([v[low:high] for v in pieces], axis=0)  38.7 us
    pallas_call x6, Pallas kernels, gather_experts(): pl.pallas_call(functools.partial(gather_kernel, counts), out_shape=[jax.S...  34.5 us
    ppermute x18, starting transfers between devices, over_z(): return lax.ppermute(value, 'dp', pairs)  30.8 us
    slice x4, local copies, waits for them, and re-layouts, gated(): return (jax.nn.silu(total[:, 0]) * total[:, 1]).astype(jnp.bfloat16)  23.3 us
  transfers between devices with their start and end apart: 24, of which 14 were waited for; matrix products, arithmetic and copies ran while one was open for 26% of the time, Pallas kernels for 3%

profile of v5, /device:TPU:8, one launch (start us, length us, event | category | flops | bytes accessed | tf_op | source)
XLA Modules:
  0.0 861.9 jit_solution(10882364940564294303)
XLA Ops:
  1.9 6.7 shard_map.65
  10.2 3.4 collective-permute-start.1
  13.6 5.3 collective-permute-start.2
  19.1 4.8 shard_map.67
  27.5 4.8 shard_map.66.refs_5_.refs_0_
  35.3 6.7 shard_map.68.refs_8_.refs_0_
  42.5 5.6 shard_map.69
  51.8 5.9 shard_map.64
  57.7 111.0 %collective-permute-done.refs_0_ = bf16[1024,3584]{1,0:T(8,128)(2,1)} collective-permute-done((bf16[1024,3584]{1,0:T(8,128)(2,1)}, bf16[1024,3584]{1,0:T(8,128)(2,1)}, u32[]{:S(2)}, u32[]{:S(2)}) %collective-permute-start) | collective-permute-done | bytes 7340064 | tf_op jit(solution)/shard_map/hop_chips_one/ppermute | solution.py:144
  171.8 4.1 collective-permute-done.2.refs_2_
  192.1 4.3 slice.215
  199.6 3.2 fusion.95
  206.4 3.6 pad_maximum_fusion.1
  217.3 123.1 %collective-permute-done.5.refs_1_ = bf16[1024,3584]{1,0:T(8,128)(2,1)S(1)} collective-permute-done((bf16[1024,3584]{1,0:T(8,128)(2,1)S(1)}, bf16[1024,3584]{1,0:T(8,128)(2,1)S(1)}, u32[]{:S(2)}, u32[]{:S(2)}) %collective-permute-start.5) | collective-permute-done | bytes 7340064 | tf_op jit(solution)/shard_map/hop_chips_two/ppermute | solution.py:144
  341.0 4.5 collective-permute-done.7.refs_3_
  353.5 5.5 pad_maximum_fusion
  359.1 4.4 fusion.99
  375.7 6.8 broadcast_select_fusion.1
  382.5 14.4 %convolution_convert_fusion.1 = bf16[1024,1024]{1,0:T(8,128)(2,1)} fusion(bf16[1024,3584]{1,0:T(8,128)(2,1)} %broadcast_select_fusion.1, bf16[256,3584]{1,0:T(8,128)(2,1)} %copy-done.34, bf16[256,3584]{1,0:T(8,128)(2,1)} %copy-done.33, bf16[256,3584]{1,0:T(8,128)(2,1)} %copy-done.32, bf16[256,3584]{1,0:T(8,128)(2,1)S(1)} %copy-done.31), kind=kOutput, calls=%fused_computation.63 | convolution fusion | flops 7546601472 | bytes 16777216 | tf_op jit(solution)/shard_map/dot_general | solution.py:201
  399.8 4.2 fusion.93
  403.9 19.4 %collective-permute-done.10 = bf16[1024,512]{1,0:T(8,128)(2,1)S(1)} collective-permute-done((bf16[1024,512]{1,0:T(8,128)(2,1)S(1)}, bf16[1024,512]{1,0:T(8,128)(2,1)S(1)}, u32[]{:S(2)}, u32[]{:S(2)}) %collective-permute-start.10) | collective-permute-done | bytes 1048608 | tf_op jit(solution)/shard_map/terms_far/ppermute | solution.py:148
  426.0 12.2 %convolution_convert_fusion = bf16[1024,1024]{1,0:T(8,128)(2,1)S(1)} fusion(bf16[1024,3584]{1,0:T(8,128)(2,1)} %collective-permute-done.13, bf16[1024,3584]{1,0:T(8,128)(2,1)} %broadcast_select_fusion.1), kind=kOutput, calls=%fused_computation.62 | convolution fusion | flops 7517241344 | bytes 16777216 | tf_op jit(solution)/shard_map/dot_general | solution.py:201
  442.2 6.2 fusion.94
  448.4 12.0 %fusion.47 = bf16[1024,1024]{1,0:T(8,128)(2,1)S(1)} fusion(bf16[1024,3584]{1,0:T(8,128)(2,1)} %broadcast_select_fusion.1, bf16[1024,3584]{1,0:T(8,128)(2,1)} %collective-permute-done.2.refs_2_, bf16[1024,3584]{1,0:T(8,128)(2,1)} %collective-permute-done.1.refs_1_, pred[]{:T(512)S(6)} %lt.124, pred[]{:T(512)S(6)} %or.3, ...), kind=kOutput, calls=%fused_computation.61 | convolution fusion | flops 7553941504 | bytes 31457282 | tf_op jit(solution)/shard_map/dot_general | solution.py:201
  462.1 16.5 %fusion.42 = bf16[1024,1024]{1,0:T(8,128)(2,1)} fusion(bf16[1024,3584]{1,0:T(8,128)(2,1)} %collective-permute-done.1.refs_1_, bf16[1024,3584]{1,0:T(8,128)(2,1)} %collective-permute-done.2.refs_2_, pred[]{:T(512)S(6)} %lt.124, pred[]{:T(512)S(6)} %or.3, bf16[256,3584]{1,0:T(8,128)(2,1)} %get-tuple-element.63, bf16[256,3584]{1,0:T(8,128)(2,1)} %get-tuple-element.62, ...), kind=kOutput, calls=%fused_computation.60 | convolution fusion | flops 7557611520 | bytes 24117250 | tf_op jit(solution)/shard_map/dot_general | solution.py:201
  493.9 3.5 reshape.26
  497.4 7.5 fusion.103
  505.6 27.3 %collective-permute-done.12 = bf16[1024,1024]{1,0:T(8,128)(2,1)} collective-permute-done((bf16[1024,1024]{1,0:T(8,128)(2,1)}, bf16[1024,1024]{1,0:T(8,128)(2,1)}, u32[]{:S(2)}, u32[]{:S(2)}) %collective-permute-start.12) | collective-permute-done | bytes 2097184 | tf_op jit(solution)/shard_map/terms_near/ppermute | solution.py:148
  532.8 4.5 convert_add_fusion.1
  537.3 5.9 reshape.28
  543.3 7.1 fusion.97
  551.4 7.0 collective-permute-done.11.refs_3_.right_a
  558.4 10.5 %collective-permute-done.15.refs_5_ = bf16[512,512]{1,0:T(8,128)(2,1)S(1)} collective-permute-done((bf16[512,512]{1,0:T(8,128)(2,1)}, bf16[512,512]{1,0:T(8,128)(2,1)S(1)}, u32[]{:S(2)}, u32[]{:S(2)}) %collective-permute-start.15) | collective-permute-done | bytes 524320 | tf_op jit(solution)/shard_map/hop_hidden3/ppermute | solution.py:144
  570.7 4.1 slice.236
  574.8 6.8 pad_maximum_fusion.2
  598.0 13.9 %fusion.39 = bf16[1024,1024]{1,0:T(8,128)(2,1)} fusion(bf16[1024,3584]{1,0:T(8,128)(2,1)} %param.6, bf16[256,3584]{1,0:T(8,128)(2,1)} %get-tuple-element.59, bf16[256,3584]{1,0:T(8,128)(2,1)S(1)} %get-tuple-element.58, bf16[256,3584]{1,0:T(8,128)(2,1)} %slice.235, bf16[256,3584]{1,0:T(8,128)(2,1)} %slice.196), kind=kOutput, calls=%fused_computation.59 | convolution fusion | flops 7546601472 | bytes 16777216 | tf_op jit(solution)/shard_map/dot_general | solution.py:201
  617.4 7.7 pad_maximum_fusion.3
  625.1 4.0 collective-permute-start.23
  631.1 128.6 %collective-permute-done.17 = bf16[512,512]{1,0:T(8,128)(2,1)S(1)} collective-permute-done((bf16[512,512]{1,0:T(8,128)(2,1)S(1)}, bf16[512,512]{1,0:T(8,128)(2,1)S(1)}, u32[]{:S(2)}, u32[]{:S(2)}) %collective-permute-start.17) | collective-permute-done | bytes 524320 | tf_op jit(solution)/shard_map/hop_hidden3/ppermute | solution.py:144
  759.8 26.2 %collective-permute-done.16 = bf16[512,512]{1,0:T(8,128)(2,1)S(1)} collective-permute-done((bf16[512,512]{1,0:T(8,128)(2,1)S(1)}, bf16[512,512]{1,0:T(8,128)(2,1)S(1)}, u32[]{:S(2)}, u32[]{:S(2)}) %collective-permute-start.16) | collective-permute-done | bytes 524320 | tf_op jit(solution)/shard_map/hop_hidden2/ppermute | solution.py:144
  786.1 4.5 convert_add_fusion
  790.5 5.8 reshape.30
  796.4 7.1 fusion.96
  809.1 5.4 copy.43
  814.9 16.0 %collective-permute-done.22 = bf16[1024,512]{0,1:T(8,128)(2,1)} collective-permute-done((bf16[1024,512]{0,1:T(8,128)(2,1)}, bf16[1024,512]{0,1:T(8,128)(2,1)}, u32[]{:S(2)}, u32[]{:S(2)}) %collective-permute-start.22) | collective-permute-done | bytes 1048608 | tf_op jit(solution)/shard_map/terms_rows/ppermute | solution.py:148
  834.4 4.3 slice_dynamic-update-slice_fusion
  838.7 10.9 %fusion.31.total = f32[1024,3584]{1,0:T(8,128)S(1)} fusion(bf16[1024,3584]{1,0:T(8,128)(2,1)} %slice_dynamic-update-slice_fusion, f32[1024,1024]{1,0:T(8,128)S(1)} %bitcast.73, bf16[512,1024]{1,0:T(8,128)(2,1)S(1)} %slice.244, bf16[512,1024]{1,0:T(8,128)(2,1)S(1)} %fusion.36.refs_2_), kind=kOutput, calls=%fused_computation.44 | convolution fusion | flops 7522484224 | bytes 28311552 | tf_op jit(solution)/shard_map/dot_general | solution.py:304
  849.6 12.0 %shard_map.78 = bf16[1024,3584]{1,0:T(8,128)(2,1)} custom-call(bf16[1024,1024]{1,0:T(8,128)(2,1)S(1)} %fusion.30.left, bf16[512,3584]{1,0:T(8,128)(2,1)} %collective-permute-done.11.refs_3_.right_a, bf16[512,3584]{1,0:T(8,128)(2,1)} %collective-permute-done.18.refs_1_.right_b, f32[1024,3584]{1,0:T(8,128)S(1)} %fusion.31.total), custom_call_target="tpu_custom_call" | custom-call | tf_op jit(solution)/shard_map/pallas_call | solution.py:113
  (199 shorter events, 131.9 us)
Async XLA Ops:
  8.6 160.1 %collective-permute-start = (bf16[1024,3584]{1,0:T(8,128)(2,1)}, bf16[1024,3584]{1,0:T(8,128)(2,1)}, u32[]{:S(2)}, u32[]{:S(2)}) collective-permute-start(bf16[1024,3584]{1,0:T(8,128)(2,1)} %shard_map.65), channel_id=1, source_target_pairs={{0,4},{2,6},{4,0},{6,2},{8,12},{10,14},{12,8},{14,10},{16,20},{18,... | collective-permute-start | bytes 22020104 | tf_op jit(solution)/shard_map/hop_chips_one/ppermute | solution.py:144
  10.2 161.6 %collective-permute-start.1 = (bf16[1024,3584]{1,0:T(8,128)(2,1)}, bf16[1024,3584]{1,0:T(8,128)(2,1)}, u32[]{:S(2)}, u32[]{:S(2)}) collective-permute-start(bf16[1024,3584]{1,0:T(8,128)(2,1)} %param.6), channel_id=1, source_target_pairs={{0,8},{2,10},{4,12},{6,14},{8,16},{10,18},{12,20},{14,22},{16,24},... | collective-permute-start | bytes 22020104 | tf_op jit(solution)/shard_map/hop_right1/ppermute | solution.py:144
  13.6 162.3 %collective-permute-start.2 = (bf16[1024,3584]{1,0:T(8,128)(2,1)}, bf16[1024,3584]{1,0:T(8,128)(2,1)}, u32[]{:S(2)}, u32[]{:S(2)}) collective-permute-start(bf16[1024,3584]{1,0:T(8,128)(2,1)} %param.6), channel_id=1, source_target_pairs={{24,16},{26,18},{28,20},{30,22},{16,8},{18,10},{20,12},{22,14},{8,... | collective-permute-start | bytes 22020104 | tf_op jit(solution)/shard_map/hop_left1/ppermute | solution.py:144
  35.3 6.8 copy-start.48
  51.7 124.2 %slice-start = ((s8[7340032]{0:T(1024)(128)(4,1)}), s8[3145728]{0:T(1024)(128)(4,1)S(1)}, s32[]{:S(2)}) async-start(s8[7340032]{0:T(1024)(128)(4,1)} %bitcast.70), calls=%async_computation | async-start | bytes 6291456
  51.8 124.2 %slice-start.1 = ((s8[7340032]{0:T(1024)(128)(4,1)}), s8[4194304]{0:T(1024)(128)(4,1)S(1)}, s32[]{:S(2)}) async-start(s8[7340032]{0:T(1024)(128)(4,1)} %bitcast.70), calls=%async_computation.1 | async-start | bytes 8388608
  51.8 124.2 %copy-start.8 = (bf16[512,3584]{1,0:T(8,128)(2,1)S(1)}, bf16[512,3584]{1,0:T(8,128)(2,1)}, u32[]{:S(2)}) copy-start(bf16[512,3584]{1,0:T(8,128)(2,1)} %copy-done.7) | copy-start | bytes 11010052
  57.7 124.4 %copy-start.15 = (bf16[512,3584]{1,0:T(8,128)(2,1)}, bf16[512,3584]{1,0:T(8,128)(2,1)S(1)}, u32[]{:S(2)}) copy-start(bf16[512,3584]{1,0:T(8,128)(2,1)S(1)} %get-tuple-element.16.refs_3_) | copy-start | bytes 11010052
  57.7 124.4 %copy-start.17 = (bf16[512,3584]{1,0:T(8,128)(2,1)}, bf16[512,3584]{1,0:T(8,128)(2,1)S(1)}, u32[]{:S(2)}) copy-start(bf16[512,3584]{1,0:T(8,128)(2,1)S(1)} %get-tuple-element.17.refs_4_.refs_0_) | copy-start | bytes 11010052
  182.1 158.3 %collective-permute-start.5 = (bf16[1024,3584]{1,0:T(8,128)(2,1)S(1)}, bf16[1024,3584]{1,0:T(8,128)(2,1)S(1)}, u32[]{:S(2)}, u32[]{:S(2)}) collective-permute-start(bf16[1024,3584]{1,0:T(8,128)(2,1)S(1)} %shard_map.72), channel_id=1, source_target_pairs={{0,4},{2,6},{4,0},{6,2},{8,12},{10,14},{12,8},{14,10},{16,20},{18,... | collective-permute-start | bytes 22020104 | tf_op jit(solution)/shard_map/hop_chips_two/ppermute | solution.py:144
  182.7 158.4 %collective-permute-start.6 = (bf16[1024,3584]{1,0:T(8,128)(2,1)}, bf16[1024,3584]{1,0:T(8,128)(2,1)S(1)}, u32[]{:S(2)}, u32[]{:S(2)}) collective-permute-start(bf16[1024,3584]{1,0:T(8,128)(2,1)} %collective-permute-done.1.refs_1_), channel_id=1, source_target_pairs={{8,16},{10,18},{12,20},{14,22},{16,24},{18,26},{20,28},{22,30},{9,... | collective-permute-start | bytes 22020104 | tf_op jit(solution)/shard_map/hop_right2/ppermute | solution.py:144
  185.7 159.8 %collective-permute-start.7 = (bf16[1024,3584]{1,0:T(8,128)(2,1)}, bf16[1024,3584]{1,0:T(8,128)(2,1)S(1)}, u32[]{:S(2)}, u32[]{:S(2)}) collective-permute-start(bf16[1024,3584]{1,0:T(8,128)(2,1)} %collective-permute-done.2.refs_2_), channel_id=1, source_target_pairs={{16,8},{18,10},{20,12},{22,14},{8,0},{10,2},{12,4},{14,6},{17,9},{... | collective-permute-start | bytes 22020104 | tf_op jit(solution)/shard_map/hop_left2/ppermute | solution.py:144
  192.1 4.6 copy-start.16
  192.1 10.7 %collective-permute-start.3 = (bf16[512,3584]{1,0:T(8,128)(2,1)}, bf16[512,3584]{1,0:T(8,128)(2,1)}, u32[]{:S(2)}, u32[]{:S(2)}) collective-permute-start(bf16[512,3584]{1,0:T(8,128)(2,1)} %copy-done.19), channel_id=1, source_target_pairs={{0,2},{2,0},{4,6},{6,4},{8,10},{10,8},{12,14},{14,12},{16,18},{18,... | collective-permute-start | bytes 11010056 | tf_op jit(solution)/shard_map/hop_cores_one/ppermute | solution.py:144
  196.3 8.1 collective-permute-start.4
  196.8 9.6 %copy-start.30 = (bf16[256,3584]{1,0:T(8,128)(2,1)}, bf16[256,3584]{1,0:T(8,128)(2,1)S(1)}, u32[]{:S(2)}) copy-start(bf16[256,3584]{1,0:T(8,128)(2,1)S(1)} %slice.182) | copy-start | bytes 5505028
  199.6 6.8 copy-start.32
  204.4 10.9 %copy-start.33 = (bf16[256,3584]{1,0:T(8,128)(2,1)}, bf16[256,3584]{1,0:T(8,128)(2,1)S(1)}, u32[]{:S(2)}) copy-start(bf16[256,3584]{1,0:T(8,128)(2,1)S(1)} %slice.225) | copy-start | bytes 5505028
  210.0 216.0 %collective-permute-start.13 = (bf16[1024,3584]{1,0:T(8,128)(2,1)}, bf16[1024,3584]{1,0:T(8,128)(2,1)}, u32[]{:S(2)}, u32[]{:S(2)}) collective-permute-start(bf16[1024,3584]{1,0:T(8,128)(2,1)} %pad_maximum_fusion.1), channel_id=1, source_target_pairs={{0,8},{2,10},{4,12},{6,14},{24,16},{26,18},{28,20},{30,22},{1,9},{... | collective-permute-start | bytes 22020104 | tf_op jit(solution)/shard_map/hop_edge/ppermute | solution.py:144
  348.5 5.0 copy-start.14
  359.0 83.2 %collective-permute-start.8 = (bf16[1024,3584]{1,0:T(8,128)(2,1)}, bf16[1024,3584]{1,0:T(8,128)(2,1)}, u32[]{:S(2)}, u32[]{:S(2)}) collective-permute-start(bf16[1024,3584]{1,0:T(8,128)(2,1)} %pad_maximum_fusion), channel_id=1, source_target_pairs={{0,2},{2,0},{4,6},{6,4},{8,10},{10,8},{12,14},{14,12},{16,18},{18,... | collective-permute-start | bytes 22020104 | tf_op jit(solution)/shard_map/hop_cores_two/ppermute | solution.py:144
  363.5 4.7 copy-start.1
  374.3 8.2 copy-start.31
  374.3 195.3 %collective-permute-start.19 = (bf16[1024,3584]{1,0:T(8,128)(2,1)}, bf16[1024,3584]{1,0:T(8,128)(2,1)}, u32[]{:S(2)}, u32[]{:S(2)}) collective-permute-start(bf16[1024,3584]{1,0:T(8,128)(2,1)} %shard_map.75), channel_id=1, source_target_pairs={{0,4},{2,6},{4,0},{6,2},{8,12},{10,14},{12,8},{14,10},{16,20},{18,... | collective-permute-start | bytes 22020104 | tf_op jit(solution)/shard_map/hop_chips_three/ppermute | solution.py:144
  398.2 25.2 %copy-start.46 = (bf16[1024,1024]{1,0:T(8,128)(2,1)S(1)}, bf16[1024,1024]{1,0:T(8,128)(2,1)}, u32[]{:S(2)}) copy-start(bf16[1024,1024]{1,0:T(8,128)(2,1)} %convolution_convert_fusion.1) | copy-start | bytes 6291460
  398.2 25.2 %collective-permute-start.10 = (bf16[1024,512]{1,0:T(8,128)(2,1)S(1)}, bf16[1024,512]{1,0:T(8,128)(2,1)S(1)}, u32[]{:S(2)}, u32[]{:S(2)}) collective-permute-start(bf16[1024,512]{1,0:T(8,128)(2,1)S(1)} %constant_dynamic-slice_fusion.2), channel_id=1, source_target_pairs={{0,1},{1,0},{2,3},{3,2},{4,5},{5,4},{6,7},{7,6},{8,9},{9,8},{10,11... | collective-permute-start | bytes 3145736 | tf_op jit(solution)/shard_map/terms_far/ppermute | solution.py:148
  399.8 158.6 %collective-permute-start.11 = (bf16[512,3584]{1,0:T(8,128)(2,1)}, bf16[512,3584]{1,0:T(8,128)(2,1)}, u32[]{:S(2)}, u32[]{:S(2)}) collective-permute-start(bf16[512,3584]{1,0:T(8,128)(2,1)} %get-tuple-element.23), channel_id=1, source_target_pairs={{0,16},{2,18},{4,20},{6,22},{8,24},{10,26},{12,28},{14,30},{16,0},... | collective-permute-start | bytes 11010056 | tf_op jit(solution)/shard_map/hop_out2/ppermute | solution.py:144
  440.7 39.5 %collective-permute-start.14 = (bf16[1024,512]{1,0:T(8,128)(2,1)}, bf16[1024,512]{1,0:T(8,128)(2,1)S(1)}, u32[]{:S(2)}, u32[]{:S(2)}) collective-permute-start(bf16[1024,512]{1,0:T(8,128)(2,1)} %constant_dynamic-slice_fusion.1), channel_id=1, source_target_pairs={{0,1},{1,0},{2,3},{3,2},{4,5},{5,4},{6,7},{7,6},{8,9},{9,8},{10,11... | collective-permute-start | bytes 3145736 | tf_op jit(solution)/shard_map/terms_edge/ppermute | solution.py:148
  460.4 18.2 %copy-start.43 = (bf16[1024,1024]{1,0:T(8,128)(2,1)}, bf16[1024,1024]{1,0:T(8,128)(2,1)S(1)}, u32[]{:S(2)}) copy-start(bf16[1024,1024]{1,0:T(8,128)(2,1)S(1)} %fusion.47) | copy-start | bytes 6291460
  461.6 29.4 %collective-permute-start.9 = (bf16[1024,512]{1,0:T(8,128)(2,1)}, bf16[1024,512]{1,0:T(8,128)(2,1)}, u32[]{:S(2)}, u32[]{:S(2)}) collective-permute-start(bf16[1024,512]{1,0:T(8,128)(2,1)} %constant_dynamic-slice_fusion.3), channel_id=1, source_target_pairs={{0,1},{1,0},{2,3},{3,2},{4,5},{5,4},{6,7},{7,6},{8,9},{9,8},{10,11... | collective-permute-start | bytes 3145736 | tf_op jit(solution)/shard_map/terms_mid/ppermute | solution.py:148
  478.6 54.2 %collective-permute-start.12 = (bf16[1024,1024]{1,0:T(8,128)(2,1)}, bf16[1024,1024]{1,0:T(8,128)(2,1)}, u32[]{:S(2)}, u32[]{:S(2)}) collective-permute-start(bf16[1024,1024]{1,0:T(8,128)(2,1)} %fusion.42), channel_id=1, source_target_pairs={{0,1},{1,0},{2,3},{3,2},{4,5},{5,4},{6,7},{7,6},{8,9},{9,8},{10,11... | collective-permute-start | bytes 6291464 | tf_op jit(solution)/shard_map/terms_near/ppermute | solution.py:148
  485.5 5.5 copy-start.44
  488.2 80.6 %collective-permute-start.15 = (bf16[512,512]{1,0:T(8,128)(2,1)}, bf16[512,512]{1,0:T(8,128)(2,1)S(1)}, u32[]{:S(2)}, u32[]{:S(2)}) collective-permute-start(bf16[512,512]{1,0:T(8,128)(2,1)} %fusion.53), channel_id=1, source_target_pairs={{8,24},{10,26},{12,28},{14,30},{16,0},{18,2},{20,4},{22,6},{9,25},... | collective-permute-start | bytes 1572872 | tf_op jit(solution)/shard_map/hop_hidden3/ppermute | solution.py:144
  504.9 27.9 %copy-start.47 = (bf16[1024,1024]{1,0:T(8,128)(2,1)S(1)}, bf16[1024,1024]{1,0:T(8,128)(2,1)}, u32[]{:S(2)}) copy-start(bf16[1024,1024]{1,0:T(8,128)(2,1)} %fusion.42) | copy-start | bytes 6291460
  574.8 6.8 copy-start.9
  581.6 11.9 %collective-permute-start.20 = (bf16[1024,3584]{1,0:T(8,128)(2,1)}, bf16[1024,3584]{1,0:T(8,128)(2,1)S(1)}, u32[]{:S(2)}, u32[]{:S(2)}) collective-permute-start(bf16[1024,3584]{1,0:T(8,128)(2,1)} %pad_maximum_fusion.2), channel_id=1, source_target_pairs={{0,2},{2,0},{4,6},{6,4},{8,10},{10,8},{12,14},{14,12},{16,18},{18,... | collective-permute-start | bytes 22020104 | tf_op jit(solution)/shard_map/hop_cores_three/ppermute | solution.py:144
  587.3 217.2 %collective-permute-start.18 = (bf16[512,3584]{1,0:T(8,128)(2,1)}, bf16[512,3584]{1,0:T(8,128)(2,1)}, u32[]{:S(2)}, u32[]{:S(2)}) collective-permute-start(bf16[512,3584]{1,0:T(8,128)(2,1)} %get-tuple-element.26.refs_1_), channel_id=1, source_target_pairs={{0,24},{2,26},{4,28},{6,30},{8,16},{10,18},{12,20},{14,22},{16,8},... | collective-permute-start | bytes 11010056 | tf_op jit(solution)/shard_map/hop_out3/ppermute | solution.py:144
  611.9 5.5 copy-start.37
  611.9 174.2 %collective-permute-start.21 = (bf16[1024,1024]{1,0:T(8,128)(2,1)}, bf16[1024,1024]{1,0:T(8,128)(2,1)S(1)}, u32[]{:S(2)}, u32[]{:S(2)}) collective-permute-start(bf16[1024,1024]{1,0:T(8,128)(2,1)} %fusion.39), channel_id=1, source_target_pairs={{0,1},{1,0},{2,3},{3,2},{4,5},{5,4},{6,7},{7,6},{8,9},{9,8},{10,11... | collective-permute-start | bytes 6291464 | tf_op jit(solution)/shard_map/terms_own/ppermute | solution.py:148
  617.4 11.7 %copy-start.25 = (bf16[512,512]{1,0:T(8,128)(2,1)S(1)}, bf16[512,512]{1,0:T(8,128)(2,1)}, u32[]{:S(2)}) copy-start(bf16[512,512]{1,0:T(8,128)(2,1)} %copy-done.24) | copy-start | bytes 1572868
  617.4 13.6 %copy-start.23 = (bf16[512,512]{1,0:T(8,128)(2,1)S(1)}, bf16[512,512]{1,0:T(8,128)(2,1)}, u32[]{:S(2)}) copy-start(bf16[512,512]{1,0:T(8,128)(2,1)} %copy-done.22) | copy-start | bytes 1572868
  617.4 142.3 %copy-start.27 = (bf16[512,512]{1,0:T(8,128)(2,1)S(1)}, bf16[512,512]{1,0:T(8,128)(2,1)}, u32[]{:S(2)}) copy-start(bf16[512,512]{1,0:T(8,128)(2,1)} %copy-done.26) | copy-start | bytes 1572868
  625.1 208.0 %collective-permute-start.23 = (bf16[512,4608]{1,0:T(8,128)(2,1)}, bf16[512,4608]{1,0:T(8,128)(2,1)}, u32[]{:S(2)}, u32[]{:S(2)}) collective-permute-start(bf16[512,4608]{1,0:T(8,128)(2,1)} %pad_maximum_fusion.3), channel_id=1, source_target_pairs={{0,8},{2,10},{4,12},{6,14},{8,0},{10,2},{12,4},{14,6},{16,24},{18,... | collective-permute-start | bytes 14155784 | tf_op jit(solution)/shard_map/hop_out1/ppermute | solution.py:144
  629.1 130.6 %collective-permute-start.17 = (bf16[512,512]{1,0:T(8,128)(2,1)S(1)}, bf16[512,512]{1,0:T(8,128)(2,1)S(1)}, u32[]{:S(2)}, u32[]{:S(2)}) collective-permute-start(bf16[512,512]{1,0:T(8,128)(2,1)S(1)} %copy-done.25), channel_id=1, source_target_pairs={{8,16},{10,18},{12,20},{14,22},{16,8},{18,10},{20,12},{22,14},{9,1... | collective-permute-start | bytes 1572872 | tf_op jit(solution)/shard_map/hop_hidden3/ppermute | solution.py:144
  631.0 155.0 %collective-permute-start.16 = (bf16[512,512]{1,0:T(8,128)(2,1)S(1)}, bf16[512,512]{1,0:T(8,128)(2,1)S(1)}, u32[]{:S(2)}, u32[]{:S(2)}) collective-permute-start(bf16[512,512]{1,0:T(8,128)(2,1)S(1)} %copy-done.23), channel_id=1, source_target_pairs={{0,16},{2,18},{4,20},{6,22},{8,24},{10,26},{12,28},{14,30},{16,0},... | collective-permute-start | bytes 1572872 | tf_op jit(solution)/shard_map/hop_hidden2/ppermute | solution.py:144
  805.9 25.1 %collective-permute-start.22 = (bf16[1024,512]{0,1:T(8,128)(2,1)}, bf16[1024,512]{0,1:T(8,128)(2,1)}, u32[]{:S(2)}, u32[]{:S(2)}) collective-permute-start(bf16[1024,512]{0,1:T(8,128)(2,1)} %copy.41), channel_id=1, source_target_pairs={{0,1},{1,0},{2,3},{3,2},{4,5},{5,4},{6,7},{7,6},{8,9},{9,8},{10,11... | collective-permute-start | bytes 3145736 | tf_op jit(solution)/shard_map/terms_rows/ppermute | solution.py:148
  809.1 5.7 copy-start.36
  814.5 17.8 %copy-start.29 = (f32[1024,1024]{0,1:T(8,128)S(1)}, f32[1024,1024]{0,1:T(8,128)}, u32[]{:S(2)}) copy-start(f32[1024,1024]{0,1:T(8,128)} %copy.43) | copy-start | bytes 12582916
  (29 other events, 75.0 us)
